TPU v7x, 32 devices: a whole 2x2x4 slice. The times are simulated.
32 devices in a mesh: section: 4 (over y, x), dp: 8 (over z, core).
Axes of the slice: x: 2, y: 2, z: 4, core: 2. Of those that a mesh axis runs over, the one named last changes fastest.
Arguments:
- fresh_q: bfloat16 [4, 896, 2048], P('section', 'dp'), may hold values from -6 to 6
- current_key_value: bfloat16 [4, 896, 512], P('section', 'dp'), may hold values from -6 to 6
- held_q: bfloat16 [4, 896, 2048], P('section', 'dp'), may hold values from -6 to 6
- retained_key_value: bfloat16 [4, 896, 512], P('section', 'dp'), may hold values from -6 to 6
- cotangent: bfloat16 [4, 896, 2048], P('section', 'dp'), may hold values from -6 to 6
- norm_gains: float32 [4, 2, 128], P('section'), may hold values from 0.5 to 1.5
- plan: int32 [4, 2], P('section'), may hold values from 0 to 3, as said below
- segment_ids: int32 [8, 4, 112], P('dp'), may hold values from 0 to 3, never falling along the last dimension, each value on 1 to 56 neighbouring positions
Outputs:
- attention_out: bfloat16 [4, 896, 2048], P('section', 'dp')
- stored_q: bfloat16 [4, 896, 2048], P('section', 'dp')
- stored_kv: bfloat16 [4, 896, 512], P('section', 'dp')
- grad_q: bfloat16 [4, 896, 2048], P('section', 'dp')
- key_value_gradient: bfloat16 [4, 896, 512], P('section', 'dp')
- gain_grads: float32 [4, 2, 128], P('section')
Inputs may be any that keep to these rules, and one draw needn't show every extreme that they name: `plan`: each of the two columns holds every microbatch number 0 to 3 exactly once.
All inputs are finite; a program needn't handle non-finite values.
Results may differ from a plain program's by a relative error of at most 0.0065.
Values may be sent and summed in bfloat16 or wider, within the bound.
No kernel may reach another device: no remote copies, remote signals or barrier semaphores. Data moves between devices by JAX's collectives and lax.ppermute only.
A program may use at most 64 MiB of HBM per device.

v0:
```python
import math

import jax
import jax.numpy as jnp
from jax import lax
from jax.sharding import PartitionSpec as P

HQ = 16
KV_HEAD_COUNT = 2
HEAD_SIZE = 128
QUERY_PER_KV = 8


EPSILON = 1e-06


def partner(value, axis, distance):
    mask = 2**distance
    pairs = [(source, source ^ mask) for source in range(lax.axis_size(axis))]
    return lax.ppermute(value, axis, pairs)


def shifted(block, axis, distance):
    devices = range(lax.axis_size(axis))
    route = [((i - distance) % len(devices), i) for i in devices]
    return lax.ppermute(block, axis, route)


def allowed_pairs(segment_row):
    row_sum_total = segment_row.shape[0]
    rows_at = jnp.arange(row_sum_total)[:, None]
    cols_at = jnp.arange(row_sum_total)[None, :]
    return (cols_at <= rows_at) & (segment_row[:, None] == segment_row[None, :])


def apply_norm(values, gain, heads):
    row_sum_total = values.shape[0]
    widened = values.astype(jnp.float32).reshape(row_sum_total, heads, HEAD_SIZE)
    factor = lax.rsqrt(jnp.mean(widened * widened, axis=-1, keepdims=True) + EPSILON)
    return (widened, factor, widened * factor * gain)


def attention_probs(query_rows, key_value_pair, gain_per_row, segment_row):
    row_sum_total = query_rows.shape[0]
    q_wide, q_factor, normalized_query = apply_norm(query_rows, gain_per_row[0], HQ)
    expanded_key, key_factor, normalized_key = apply_norm(
        key_value_pair[:, : KV_HEAD_COUNT * HEAD_SIZE], gain_per_row[1], KV_HEAD_COUNT
    )
    query_converted = normalized_query.astype(jnp.bfloat16).reshape(
        row_sum_total, KV_HEAD_COUNT, QUERY_PER_KV, HEAD_SIZE
    )
    k_cast = normalized_key.astype(jnp.bfloat16)
    scores = jnp.einsum(
        "qhgd,khd->hgqk", query_converted, k_cast, preferred_element_type=jnp.float32
    ) * (1.0 / math.sqrt(HEAD_SIZE))
    weights = jnp.where(allowed_pairs(segment_row), jnp.exp(scores), 0.0)
    attn_probs = weights / jnp.sum(weights, axis=-1, keepdims=True)
    return (q_wide, q_factor, query_converted, expanded_key, key_factor, k_cast, attn_probs)


def forward(query_rows, key_value_pair, gain_per_row, segment_row):
    row_sum_total = query_rows.shape[0]
    attn_probs = attention_probs(query_rows, key_value_pair, gain_per_row, segment_row)[6]
    value_portion = key_value_pair[:, KV_HEAD_COUNT * HEAD_SIZE :].reshape(
        row_sum_total, KV_HEAD_COUNT, HEAD_SIZE
    )
    output = jnp.einsum(
        "hgqk,khd->qhgd",
        attn_probs.astype(jnp.bfloat16),
        value_portion,
        preferred_element_type=jnp.float32,
    )
    return output.reshape(row_sum_total, HQ * HEAD_SIZE).astype(jnp.bfloat16)


def norm_back(widened, factor, gain, d_normed):
    scaled = gain * d_normed
    inner = jnp.sum(widened * scaled, axis=-1, keepdims=True) / HEAD_SIZE
    d_input = factor * scaled - widened * factor * factor * factor * inner
    d_gain = jnp.sum(d_normed * widened * factor, axis=(0, 1))
    return (d_input, d_gain)


def backward(query_rows, key_value_pair, gain_per_row, segment_row, received_payload):
    row_sum_total = query_rows.shape[0]
    q_wide, q_factor, query_converted, expanded_key, key_factor, k_cast, attn_probs = (
        attention_probs(query_rows, key_value_pair, gain_per_row, segment_row)
    )
    value_portion = key_value_pair[:, KV_HEAD_COUNT * HEAD_SIZE :].reshape(
        row_sum_total, KV_HEAD_COUNT, HEAD_SIZE
    )
    expanded_heads = received_payload.reshape(row_sum_total, KV_HEAD_COUNT, QUERY_PER_KV, HEAD_SIZE)
    prob_cast = attn_probs.astype(jnp.bfloat16)
    d_probs = jnp.einsum(
        "qhgd,khd->hgqk", expanded_heads, value_portion, preferred_element_type=jnp.float32
    )
    value_gradient = jnp.einsum(
        "hgqk,qhgd->khd", prob_cast, expanded_heads, preferred_element_type=jnp.float32
    )
    centre = jnp.sum(attn_probs * d_probs, axis=-1, keepdims=True)
    d_scores = (attn_probs * (d_probs - centre)).astype(jnp.bfloat16)
    score_scale = 1.0 / math.sqrt(HEAD_SIZE)
    d_qn = (
        jnp.einsum("hgqk,khd->qhgd", d_scores, k_cast, preferred_element_type=jnp.float32).reshape(
            row_sum_total, HQ, HEAD_SIZE
        )
        * score_scale
    )
    d_kn = (
        jnp.einsum("hgqk,qhgd->khd", d_scores, query_converted, preferred_element_type=jnp.float32)
        * score_scale
    )
    grad_query, q_gain = norm_back(q_wide, q_factor, gain_per_row[0], d_qn)
    key_gradient, k_gain = norm_back(expanded_key, key_factor, gain_per_row[1], d_kn)
    grad_q = grad_query.reshape(row_sum_total, HQ * HEAD_SIZE).astype(jnp.bfloat16)
    key_value_gradient = jnp.concatenate(
        [
            key_gradient.reshape(row_sum_total, KV_HEAD_COUNT * HEAD_SIZE),
            value_gradient.reshape(row_sum_total, KV_HEAD_COUNT * HEAD_SIZE),
        ],
        axis=1,
    ).astype(jnp.bfloat16)
    return (grad_q, key_value_gradient, jnp.stack([q_gain, k_gain]))


def ascend(first, second, third, fourth, quantize_levels):
    for bit_number in range(quantize_levels):
        first, second, third, fourth = partner(
            (first, second, third, fourth), "section", bit_number
        )
    return (first, second, third, fourth)


def descend(first, second, third, fourth, quantize_levels):
    for bit_number in reversed(range(quantize_levels)):
        first, second, third, fourth = partner(
            (first, second, third, fourth), "section", bit_number
        )
    return (first, second, third, fourth)


def local(
    fresh_q, current_key_value, held_q, retained_key_value, cotangent, norm_gains, plan, segment_ids
):
    quantize_levels = lax.axis_size("section").bit_length() - 1
    gain_per_row = norm_gains[0]
    id_table = segment_ids[0]
    forward_ids = lax.dynamic_index_in_dim(id_table, plan[0, 0], 0, keepdims=False)
    backward_ids = lax.dynamic_index_in_dim(id_table, plan[0, 1], 0, keepdims=False)
    payload = (fresh_q, current_key_value, held_q, retained_key_value)
    middle = fresh_q.shape[1] // 2
    lower_rows = ascend(*[member[:, :middle] for member in payload], quantize_levels)
    upper_rows = descend(*[member[:, middle:] for member in payload], quantize_levels)
    arrived = tuple(
        (
            jnp.concatenate([lower_part, upper_part], axis=1)
            for lower_part, upper_part in zip(lower_rows, upper_rows)
        )
    )
    forward_out = forward(fresh_q[0], current_key_value[0], gain_per_row, forward_ids)
    attention_out = shifted(forward_out[None], "section", 1)
    upstream = shifted(cotangent, "section", -1)
    grad_q, key_value_gradient, gain_terms = backward(
        arrived[2][0], arrived[3][0], gain_per_row, backward_ids, upstream[0]
    )
    gain_total = lax.psum(gain_terms, "dp") / lax.axis_size("dp")
    return (
        attention_out,
        arrived[0],
        arrived[1],
        grad_q[None],
        key_value_gradient[None],
        gain_total[None],
    )


def solution(mesh):
    placed = (
        P("section", "dp", None),
        P("section", "dp", None),
        P("section", "dp", None),
        P("section", "dp", None),
        P("section", "dp", None),
        P("section", None, None),
        P("section", None),
        P("dp", None, None),
    )
    return jax.shard_map(
        local,
        mesh=mesh,
        in_specs=placed,
        out_specs=(
            P("section", "dp", None),
            P("section", "dp", None),
            P("section", "dp", None),
            P("section", "dp", None),
            P("section", "dp", None),
            P("section", None, None),
        ),
        check_vma=False,
    )
```

profile of v0, /device:TPU:0, one launch (start us, length us, event | category | flops | bytes accessed | tf_op | source)
XLA Modules:
  0.0 101.0 jit_solution(14731611003750781998)
XLA Ops:
  0.7 1.8 %fusion.50 = (bf16[1,56,2048]{2,1,0:T(8,128)(2,1)}, bf16[1,56,2048]{2,1,0:T(8,128)(2,1)S(1)}) fusion(bf16[1,112,2048]{2,1,0:T(8,128)(2,1)} %param.10), kind=kLoop, calls=%fused_computation.95 | loop fusion | bytes 917504 | tf_op jit(solution)/shard_map/slice | solution.py:152
  2.5 2.9 %collective-permute-start.9 = (bf16[1,56,2048]{2,1,0:T(8,128)(2,1)}, bf16[1,56,2048]{2,1,0:T(8,128)(2,1)}, u32[]{:S(2)}, u32[]{:S(2)}) collective-permute-start(bf16[1,56,2048]{2,1,0:T(8,128)(2,1)} %get-tuple-element.8), channel_id=1, source_target_pairs={{0,8},{8,0},{16,24},{24,16},{1,9},{9,1},{17,25},{25,17},{2,10},{10... | collective-permute-start | bytes 688136 | tf_op jit(solution)/shard_map/ppermute | solution.py:20
  5.4 0.6 fusion.53
  6.0 2.0 %collective-permute-start.15 = (bf16[1,56,512]{2,1,0:T(8,128)(2,1)}, bf16[1,56,512]{2,1,0:T(8,128)(2,1)}, u32[]{:S(2)}, u32[]{:S(2)}) collective-permute-start(bf16[1,56,512]{2,1,0:T(8,128)(2,1)} %get-tuple-element.16), channel_id=1, source_target_pairs={{0,16},{8,24},{16,0},{24,8},{1,17},{9,25},{17,1},{25,9},{2,18},{10... | collective-permute-start | bytes 172040 | tf_op jit(solution)/shard_map/ppermute | solution.py:20
  8.1 0.6 fusion.54
  8.7 1.5 %collective-permute-start.5 = (bf16[1,56,512]{2,1,0:T(8,128)(2,1)}, bf16[1,56,512]{2,1,0:T(8,128)(2,1)}, u32[]{:S(2)}, u32[]{:S(2)}) collective-permute-start(bf16[1,56,512]{2,1,0:T(8,128)(2,1)} %get-tuple-element.17), channel_id=1, source_target_pairs={{0,8},{8,0},{16,24},{24,16},{1,9},{9,1},{17,25},{25,17},{2,10},{10... | collective-permute-start | bytes 172040 | tf_op jit(solution)/shard_map/ppermute | solution.py:20
  10.2 0.5 collective-permute-start.7
  10.8 0.6 fusion.56
  14.2 0.8 fusion.51
  16.4 0.7 fusion.40
  17.0 0.6 slice_bitcast_fusion.1
  17.6 0.7 fusion.41
  18.7 0.6 add_rsqrt_fusion.2
  20.1 0.6 copy-done.6
  20.7 0.6 fusion.5
  22.0 1.6 %collective-permute-start.14 = (bf16[1,56,512]{2,1,0:T(8,128)(2,1)}, bf16[1,56,512]{2,1,0:T(8,128)(2,1)S(1)}, u32[]{:S(2)}, u32[]{:S(2)}) collective-permute-start(bf16[1,56,512]{2,1,0:T(8,128)(2,1)} %collective-permute-done.13), channel_id=1, source_target_pairs={{0,16},{8,24},{16,0},{24,8},{1,17},{9,25},{17,1},{25,9},{2,18},{10... | collective-permute-start | bytes 172040 | tf_op jit(solution)/shard_map/ppermute | solution.py:20
  23.6 0.5 collective-permute-start.16
  24.1 0.6 broadcast_bitcast_fusion
  24.9 1.0 convert_element_type.114
  25.9 2.8 %collective-permute-start.17 = (bf16[1,112,2048]{2,1,0:T(8,128)(2,1)S(1)}, bf16[1,112,2048]{2,1,0:T(8,128)(2,1)S(1)}, u32[]{:S(2)}, u32[]{:S(2)}) collective-permute-start(bf16[1,112,2048]{2,1,0:T(8,128)(2,1)S(1)} %copy-done.17), channel_id=1, source_target_pairs={{8,0},{16,8},{24,16},{0,24},{9,1},{17,9},{25,17},{1,25},{10,2},{18... | collective-permute-start | bytes 1376264 | tf_op jit(solution)/shard_map/ppermute | solution.py:26
  28.8 0.5 collective-permute-start.6
  29.3 0.6 collective-permute-start.8
  30.2 3.0 %collective-permute-done.6 = bf16[1,56,512]{2,1,0:T(8,128)(2,1)S(1)} collective-permute-done((bf16[1,56,512]{2,1,0:T(8,128)(2,1)}, bf16[1,56,512]{2,1,0:T(8,128)(2,1)S(1)}, u32[]{:S(2)}, u32[]{:S(2)}) %collective-permute-start.6) | collective-permute-done | bytes 57376 | tf_op jit(solution)/shard_map/ppermute | solution.py:20
  33.2 10.6 %collective-permute-start.1 = (bf16[1,56,2048]{2,1,0:T(8,128)(2,1)S(1)}, bf16[1,56,2048]{2,1,0:T(8,128)(2,1)}, u32[]{:S(2)}, u32[]{:S(2)}) collective-permute-start(bf16[1,56,2048]{2,1,0:T(8,128)(2,1)S(1)} %copy-done.3), channel_id=1, source_target_pairs={{0,8},{8,0},{16,24},{24,16},{1,9},{9,1},{17,25},{25,17},{2,10},{10... | collective-permute-start | bytes 688136 | tf_op jit(solution)/shard_map/ppermute | solution.py:20
  43.8 0.7 collective-permute-start.3
  44.5 1.3 %collective-permute-start.10 = (bf16[1,56,2048]{2,1,0:T(8,128)(2,1)}, bf16[1,56,2048]{2,1,0:T(8,128)(2,1)S(1)}, u32[]{:S(2)}, u32[]{:S(2)}) collective-permute-start(bf16[1,56,2048]{2,1,0:T(8,128)(2,1)} %collective-permute-done.9), channel_id=1, source_target_pairs={{0,16},{8,24},{16,0},{24,8},{1,17},{9,25},{17,1},{25,9},{2,18},{10... | collective-permute-start | bytes 688136 | tf_op jit(solution)/shard_map/ppermute | solution.py:20
  45.9 0.7 pad_maximum_fusion.2
  46.6 3.7 %collective-permute-done.1 = bf16[1,56,2048]{2,1,0:T(8,128)(2,1)} collective-permute-done((bf16[1,56,2048]{2,1,0:T(8,128)(2,1)S(1)}, bf16[1,56,2048]{2,1,0:T(8,128)(2,1)}, u32[]{:S(2)}, u32[]{:S(2)}) %collective-permute-start.1) | collective-permute-done | bytes 229408 | tf_op jit(solution)/shard_map/ppermute | solution.py:20
  50.4 2.0 %collective-permute-start = (bf16[1,112,2048]{2,1,0:T(8,128)(2,1)}, bf16[1,112,2048]{2,1,0:T(8,128)(2,1)}, u32[]{:S(2)}, u32[]{:S(2)}) collective-permute-start(bf16[1,112,2048]{2,1,0:T(8,128)(2,1)} %convert_element_type.114), channel_id=1, source_target_pairs={{24,0},{0,8},{8,16},{16,24},{25,1},{1,9},{9,17},{17,25},{26,2},{2,... | collective-permute-start | bytes 1376264 | tf_op jit(solution)/shard_map/ppermute | solution.py:26
  52.4 1.3 %collective-permute-done.3 = bf16[1,56,2048]{2,1,0:T(8,128)(2,1)} collective-permute-done((bf16[1,56,2048]{2,1,0:T(8,128)(2,1)S(1)}, bf16[1,56,2048]{2,1,0:T(8,128)(2,1)}, u32[]{:S(2)}, u32[]{:S(2)}) %collective-permute-start.3) | collective-permute-done | bytes 229408 | tf_op jit(solution)/shard_map/ppermute | solution.py:20
  53.7 13.3 %collective-permute-done.10 = bf16[1,56,2048]{2,1,0:T(8,128)(2,1)S(1)} collective-permute-done((bf16[1,56,2048]{2,1,0:T(8,128)(2,1)}, bf16[1,56,2048]{2,1,0:T(8,128)(2,1)S(1)}, u32[]{:S(2)}, u32[]{:S(2)}) %collective-permute-start.10) | collective-permute-done | bytes 229408 | tf_op jit(solution)/shard_map/ppermute | solution.py:20
  67.7 0.6 add_rsqrt_fusion
  68.4 0.5 convolution_bitcast_fusion
  69.1 1.5 %fusion.2 = f32[2,8,112,112]{2,3,1,0:T(8,128)} fusion(pred[112,112]{0,1:T(8,128)(4,1)S(1)} %copy-done.5, f32[112,2,8,128]{3,2,1,0:T(8,128)S(1)} %bitcast.143, f32[112,2,8]{0,2,1:T(8,128)S(1)} %get-tuple-element.23, f32[128]{0:T(128)S(1)} %copy-done.9, f32[14,2,8,128]{3,2,1,0:T(8,128)S(1)} %get-tuple-element.13, f32[112,2]{0,1:T(2,128)S(1)} %add_rsqrt_fusion.1, ...), kind=kOutput, calls=%fused_computation.5 | convolution fusion | flops 52555776 | bytes 1856640 | tf_op jit(solution)/shard_map/qhgd,khd->hgqk/dot_general | solution.py:53
  70.6 1.9 %fusion.8 = bf16[112,2,128]{2,0,1:T(8,128)(2,1)S(1)} fusion(bf16[112,2,8,128]{3,2,1,0:T(8,128)(2,1)S(1)} %bitcast.152, f32[2,8,112,112]{2,3,1,0:T(8,128)} %fusion.2), kind=kOutput, calls=%fused_computation.18 | convolution fusion | flops 51812208 | bytes 1318912 | tf_op jit(solution)/shard_map/hgqk,qhgd->khd/dot_general | solution.py:97
  72.5 1.7 %multiply_reduce_fusion.1 = (f32[2,8,112]{2,1,0:T(8,128)S(1)}, f32[2,8,112,112]{2,3,1,0:T(8,128)S(1)}) fusion(f32[2,8,112,112]{2,3,1,0:T(8,128)S(1)} %convolution_bitcast_fusion, f32[2,8,112,112]{2,3,1,0:T(8,128)} %fusion.2), kind=kOutput, calls=%fused_computation.31 | output fusion | flops 602223 | bytes 2415616 | tf_op jit(solution)/shard_map/div | solution.py:57
  74.3 0.7 multiply_reduce_fusion
  75.0 0.9 fusion.28
  76.7 0.7 pad_maximum_fusion.3
  77.4 0.6 pad_maximum_fusion.4
  79.0 0.5 copy-done.8
  79.6 1.2 %mul.319 = f32[112,16,128]{2,1,0:T(8,128)} broadcast(f32[112,16]{1,0:T(8,128)S(1)} %copy.140), dimensions={0,1} | broadcast | bytes 924672 | tf_op jit(solution)/shard_map/mul | solution.py:79
  80.8 1.3 %mul.320 = f32[1,112,2048]{2,1,0:T(8,128)S(1)} reshape(f32[112,16,128]{2,1,0:T(8,128)} %mul.319) | data formatting | bytes 1835008 | tf_op jit(solution)/shard_map/mul | solution.py:79
  82.2 13.6 %psum.7 = f32[2,128]{1,0:T(2,128)S(1)} all-reduce(f32[2,128]{1,0:T(2,128)S(1)} %copy-done.14), channel_id=1, replica_groups=mesh['section'=4,'dp'=8] {'dp'}, use_global_device_ids=true, to_apply=%region_11.12 | all-reduce | flops 256 | bytes 2048 | tf_op jit(solution)/shard_map/psum | solution.py:166
  95.8 0.6 multiply_bitcast_fusion
  96.4 1.7 %pad_maximum_fusion = bf16[1,112,2048]{2,1,0:T(8,128)(2,1)} fusion(bf16[1,56,2048]{2,1,0:T(8,128)(2,1)} %collective-permute-done.4, bf16[1,56,2048]{2,1,0:T(8,128)(2,1)S(1)} %collective-permute-done.2), kind=kLoop, calls=%fused_computation.35 | loop fusion | flops 917504 | bytes 917504 | tf_op jit(solution)/shard_map/concatenate | solution.py:156
  98.1 1.1 %fusion.12 = bf16[1,112,2048]{2,1,0:T(8,128)(2,1)} fusion(f32[1,112,2048]{2,1,0:T(8,128)S(1)} %mul.345, f32[1,112,2048]{2,1,0:T(8,128)S(1)} %mul.320, f32[1,112,2048]{2,1,0:T(8,128)S(1)} %reshape.308, f32[2048]{0:T(1024)S(1)} %copy-done.7, bf16[1,56,2048]{2,1,0:T(8,128)(2,1)S(1)} %collective-permute-done.12, bf16[1,56,2048]{2,1,0:T(8,128)(2,1)S(1)} %collective-permute-done.10), kind=kLoop, calls=%fused_computation.22 | loop fusion | flops 2752512 | bytes 3678208 | tf_op jit(solution)/shard_map/convert_element_type | solution.py:115
  99.2 1.8 %copy.216 = bf16[1,112,2048]{2,1,0:T(8,128)(2,1)} copy(bf16[1,112,2048]{2,1,0:T(8,128)(2,1)} %collective-permute-done) | data formatting | bytes 917504
  (97 shorter events, 5.6 us)
Async XLA Ops:
  0.6 4.8 %copy-start.4 = (bf16[1,112,512]{2,1,0:T(8,128)(2,1)S(1)}, bf16[1,112,512]{2,1,0:T(8,128)(2,1)}, u32[]{:S(2)}) copy-start(bf16[1,112,512]{2,1,0:T(8,128)(2,1)} %param.11) | copy-start | bytes 344068
  0.6 7.5 %copy-start.1 = (bf16[1,112,512]{2,1,0:T(8,128)(2,1)S(1)}, bf16[1,112,512]{2,1,0:T(8,128)(2,1)}, u32[]{:S(2)}) copy-start(bf16[1,112,512]{2,1,0:T(8,128)(2,1)} %param.9) | copy-start | bytes 344068
  2.5 11.5 %copy-start = (bf16[1,112,2048]{2,1,0:T(8,128)(2,1)S(1)}, bf16[1,112,2048]{2,1,0:T(8,128)(2,1)}, u32[]{:S(2)}) copy-start(bf16[1,112,2048]{2,1,0:T(8,128)(2,1)} %param.8) | copy-start | bytes 1376260
  2.5 42.0 %collective-permute-start.9 = (bf16[1,56,2048]{2,1,0:T(8,128)(2,1)}, bf16[1,56,2048]{2,1,0:T(8,128)(2,1)}, u32[]{:S(2)}, u32[]{:S(2)}) collective-permute-start(bf16[1,56,2048]{2,1,0:T(8,128)(2,1)} %get-tuple-element.8), channel_id=1, source_target_pairs={{0,8},{8,0},{16,24},{24,16},{1,9},{9,1},{17,25},{25,17},{2,10},{10... | collective-permute-start | bytes 688136 | tf_op jit(solution)/shard_map/ppermute | solution.py:20
  6.0 16.0 %collective-permute-start.13 = (bf16[1,56,512]{2,1,0:T(8,128)(2,1)}, bf16[1,56,512]{2,1,0:T(8,128)(2,1)}, u32[]{:S(2)}, u32[]{:S(2)}) collective-permute-start(bf16[1,56,512]{2,1,0:T(8,128)(2,1)} %get-tuple-element.15), channel_id=1, source_target_pairs={{0,8},{8,0},{16,24},{24,16},{1,9},{9,1},{17,25},{25,17},{2,10},{10... | collective-permute-start | bytes 172040 | tf_op jit(solution)/shard_map/ppermute | solution.py:20
  6.0 17.5 %collective-permute-start.15 = (bf16[1,56,512]{2,1,0:T(8,128)(2,1)}, bf16[1,56,512]{2,1,0:T(8,128)(2,1)}, u32[]{:S(2)}, u32[]{:S(2)}) collective-permute-start(bf16[1,56,512]{2,1,0:T(8,128)(2,1)} %get-tuple-element.16), channel_id=1, source_target_pairs={{0,16},{8,24},{16,0},{24,8},{1,17},{9,25},{17,1},{25,9},{2,18},{10... | collective-permute-start | bytes 172040 | tf_op jit(solution)/shard_map/ppermute | solution.py:20
  8.7 2.0 %copy-start.15 = (s32[1,2]{1,0:T(1,128)S(1)}, s32[1,2]{1,0:T(1,128)}, u32[]{:S(2)}) copy-start(s32[1,2]{1,0:T(1,128)} %param.14) | copy-start | bytes 28
  8.7 17.1 %collective-permute-start.5 = (bf16[1,56,512]{2,1,0:T(8,128)(2,1)}, bf16[1,56,512]{2,1,0:T(8,128)(2,1)}, u32[]{:S(2)}, u32[]{:S(2)}) collective-permute-start(bf16[1,56,512]{2,1,0:T(8,128)(2,1)} %get-tuple-element.17), channel_id=1, source_target_pairs={{0,8},{8,0},{16,24},{24,16},{1,9},{9,1},{17,25},{25,17},{2,10},{10... | collective-permute-start | bytes 172040 | tf_op jit(solution)/shard_map/ppermute | solution.py:20
  10.2 15.7 %collective-permute-start.7 = (bf16[1,56,512]{2,1,0:T(8,128)(2,1)}, bf16[1,56,512]{2,1,0:T(8,128)(2,1)}, u32[]{:S(2)}, u32[]{:S(2)}) collective-permute-start(bf16[1,56,512]{2,1,0:T(8,128)(2,1)} %get-tuple-element.18), channel_id=1, source_target_pairs={{0,16},{8,24},{16,0},{24,8},{1,17},{9,25},{17,1},{25,9},{2,18},{10... | collective-permute-start | bytes 172040 | tf_op jit(solution)/shard_map/ppermute | solution.py:20
  15.0 1.3 %copy-start.16 = (s32[1,4,112]{2,1,0:T(4,128)S(1)}, s32[1,4,112]{2,1,0:T(4,128)}, u32[]{:S(2)}) copy-start(s32[1,4,112]{2,1,0:T(4,128)} %param.15) | copy-start | bytes 5380
  16.3 0.7 copy-start.12
  20.0 0.7 copy-start.6
  20.0 0.7 copy-start.11
  20.0 0.7 copy-start.9
  20.1 0.7 copy-start.10
  21.3 0.7 copy-start.13
  22.0 6.8 %collective-permute-start.14 = (bf16[1,56,512]{2,1,0:T(8,128)(2,1)}, bf16[1,56,512]{2,1,0:T(8,128)(2,1)S(1)}, u32[]{:S(2)}, u32[]{:S(2)}) collective-permute-start(bf16[1,56,512]{2,1,0:T(8,128)(2,1)} %collective-permute-done.13), channel_id=1, source_target_pairs={{0,16},{8,24},{16,0},{24,8},{1,17},{9,25},{17,1},{25,9},{2,18},{10... | collective-permute-start | bytes 172040 | tf_op jit(solution)/shard_map/ppermute | solution.py:20
  23.6 5.7 %collective-permute-start.16 = (bf16[1,56,512]{2,1,0:T(8,128)(2,1)}, bf16[1,56,512]{2,1,0:T(8,128)(2,1)S(1)}, u32[]{:S(2)}, u32[]{:S(2)}) collective-permute-start(bf16[1,56,512]{2,1,0:T(8,128)(2,1)} %collective-permute-done.15), channel_id=1, source_target_pairs={{0,8},{8,0},{16,24},{24,16},{1,9},{9,1},{17,25},{25,17},{2,10},{10... | collective-permute-start | bytes 172040 | tf_op jit(solution)/shard_map/ppermute | solution.py:20
  24.8 1.1 %copy-start.17 = (bf16[1,112,2048]{2,1,0:T(8,128)(2,1)S(1)}, bf16[1,112,2048]{2,1,0:T(8,128)(2,1)}, u32[]{:S(2)}) copy-start(bf16[1,112,2048]{2,1,0:T(8,128)(2,1)} %param.12) | copy-start | bytes 1376260
  25.8 20.0 %collective-permute-start.11 = (bf16[1,56,2048]{2,1,0:T(8,128)(2,1)S(1)}, bf16[1,56,2048]{2,1,0:T(8,128)(2,1)S(1)}, u32[]{:S(2)}, u32[]{:S(2)}) collective-permute-start(bf16[1,56,2048]{2,1,0:T(8,128)(2,1)S(1)} %get-tuple-element.9), channel_id=1, source_target_pairs={{0,16},{8,24},{16,0},{24,8},{1,17},{9,25},{17,1},{25,9},{2,18},{10... | collective-permute-start | bytes 688136 | tf_op jit(solution)/shard_map/ppermute | solution.py:20
  25.9 42.3 %collective-permute-start.17 = (bf16[1,112,2048]{2,1,0:T(8,128)(2,1)S(1)}, bf16[1,112,2048]{2,1,0:T(8,128)(2,1)S(1)}, u32[]{:S(2)}, u32[]{:S(2)}) collective-permute-start(bf16[1,112,2048]{2,1,0:T(8,128)(2,1)S(1)} %copy-done.17), channel_id=1, source_target_pairs={{8,0},{16,8},{24,16},{0,24},{9,1},{17,9},{25,17},{1,25},{10,2},{18... | collective-permute-start | bytes 1376264 | tf_op jit(solution)/shard_map/ppermute | solution.py:26
  28.8 4.4 %collective-permute-start.6 = (bf16[1,56,512]{2,1,0:T(8,128)(2,1)}, bf16[1,56,512]{2,1,0:T(8,128)(2,1)S(1)}, u32[]{:S(2)}, u32[]{:S(2)}) collective-permute-start(bf16[1,56,512]{2,1,0:T(8,128)(2,1)} %collective-permute-done.5), channel_id=1, source_target_pairs={{0,16},{8,24},{16,0},{24,8},{1,17},{9,25},{17,1},{25,9},{2,18},{10... | collective-permute-start | bytes 172040 | tf_op jit(solution)/shard_map/ppermute | solution.py:20
  29.3 14.5 %collective-permute-start.8 = (bf16[1,56,512]{2,1,0:T(8,128)(2,1)}, bf16[1,56,512]{2,1,0:T(8,128)(2,1)S(1)}, u32[]{:S(2)}, u32[]{:S(2)}) collective-permute-start(bf16[1,56,512]{2,1,0:T(8,128)(2,1)} %collective-permute-done.7), channel_id=1, source_target_pairs={{0,8},{8,0},{16,24},{24,16},{1,9},{9,1},{17,25},{25,17},{2,10},{10... | collective-permute-start | bytes 172040 | tf_op jit(solution)/shard_map/ppermute | solution.py:20
  29.9 3.3 %copy-start.3 = (bf16[1,56,2048]{2,1,0:T(8,128)(2,1)S(1)}, bf16[1,56,2048]{2,1,0:T(8,128)(2,1)}, u32[]{:S(2)}) copy-start(bf16[1,56,2048]{2,1,0:T(8,128)(2,1)} %get-tuple-element.10) | copy-start | bytes 688132
  29.9 13.8 %copy-start.2 = (bf16[1,56,2048]{2,1,0:T(8,128)(2,1)S(1)}, bf16[1,56,2048]{2,1,0:T(8,128)(2,1)}, u32[]{:S(2)}) copy-start(bf16[1,56,2048]{2,1,0:T(8,128)(2,1)} %get-tuple-element.11) | copy-start | bytes 688132
  33.2 17.2 %collective-permute-start.1 = (bf16[1,56,2048]{2,1,0:T(8,128)(2,1)S(1)}, bf16[1,56,2048]{2,1,0:T(8,128)(2,1)}, u32[]{:S(2)}, u32[]{:S(2)}) collective-permute-start(bf16[1,56,2048]{2,1,0:T(8,128)(2,1)S(1)} %copy-done.3), channel_id=1, source_target_pairs={{0,8},{8,0},{16,24},{24,16},{1,9},{9,1},{17,25},{25,17},{2,10},{10... | collective-permute-start | bytes 688136 | tf_op jit(solution)/shard_map/ppermute | solution.py:20
  43.8 9.9 %collective-permute-start.3 = (bf16[1,56,2048]{2,1,0:T(8,128)(2,1)S(1)}, bf16[1,56,2048]{2,1,0:T(8,128)(2,1)}, u32[]{:S(2)}, u32[]{:S(2)}) collective-permute-start(bf16[1,56,2048]{2,1,0:T(8,128)(2,1)S(1)} %copy-done.2), channel_id=1, source_target_pairs={{0,16},{8,24},{16,0},{24,8},{1,17},{9,25},{17,1},{25,9},{2,18},{10... | collective-permute-start | bytes 688136 | tf_op jit(solution)/shard_map/ppermute | solution.py:20
  44.5 22.5 %collective-permute-start.10 = (bf16[1,56,2048]{2,1,0:T(8,128)(2,1)}, bf16[1,56,2048]{2,1,0:T(8,128)(2,1)S(1)}, u32[]{:S(2)}, u32[]{:S(2)}) collective-permute-start(bf16[1,56,2048]{2,1,0:T(8,128)(2,1)} %collective-permute-done.9), channel_id=1, source_target_pairs={{0,16},{8,24},{16,0},{24,8},{1,17},{9,25},{17,1},{25,9},{2,18},{10... | collective-permute-start | bytes 688136 | tf_op jit(solution)/shard_map/ppermute | solution.py:20
  45.8 21.2 %collective-permute-start.12 = (bf16[1,56,2048]{2,1,0:T(8,128)(2,1)S(1)}, bf16[1,56,2048]{2,1,0:T(8,128)(2,1)S(1)}, u32[]{:S(2)}, u32[]{:S(2)}) collective-permute-start(bf16[1,56,2048]{2,1,0:T(8,128)(2,1)S(1)} %collective-permute-done.11), channel_id=1, source_target_pairs={{0,8},{8,0},{16,24},{24,16},{1,9},{9,1},{17,25},{25,17},{2,10},{10... | collective-permute-start | bytes 688136 | tf_op jit(solution)/shard_map/ppermute | solution.py:20
  50.4 31.8 %collective-permute-start = (bf16[1,112,2048]{2,1,0:T(8,128)(2,1)}, bf16[1,112,2048]{2,1,0:T(8,128)(2,1)}, u32[]{:S(2)}, u32[]{:S(2)}) collective-permute-start(bf16[1,112,2048]{2,1,0:T(8,128)(2,1)} %convert_element_type.114), channel_id=1, source_target_pairs={{24,0},{0,8},{8,16},{16,24},{25,1},{1,9},{9,17},{17,25},{26,2},{2,... | collective-permute-start | bytes 1376264 | tf_op jit(solution)/shard_map/ppermute | solution.py:26
  53.7 42.6 %collective-permute-start.2 = (bf16[1,56,2048]{2,1,0:T(8,128)(2,1)}, bf16[1,56,2048]{2,1,0:T(8,128)(2,1)S(1)}, u32[]{:S(2)}, u32[]{:S(2)}) collective-permute-start(bf16[1,56,2048]{2,1,0:T(8,128)(2,1)} %collective-permute-done.1), channel_id=1, source_target_pairs={{0,16},{8,24},{16,0},{24,8},{1,17},{9,25},{17,1},{25,9},{2,18},{10... | collective-permute-start | bytes 688136 | tf_op jit(solution)/shard_map/ppermute | solution.py:20
  67.0 29.3 %collective-permute-start.4 = (bf16[1,56,2048]{2,1,0:T(8,128)(2,1)}, bf16[1,56,2048]{2,1,0:T(8,128)(2,1)}, u32[]{:S(2)}, u32[]{:S(2)}) collective-permute-start(bf16[1,56,2048]{2,1,0:T(8,128)(2,1)} %collective-permute-done.3), channel_id=1, source_target_pairs={{0,8},{8,0},{16,24},{24,16},{1,9},{9,1},{17,25},{25,17},{2,10},{10... | collective-permute-start | bytes 688136 | tf_op jit(solution)/shard_map/ppermute | solution.py:20
  68.4 0.7 copy-start.5
  78.8 0.7 copy-start.8
  80.8 1.4 %copy-start.14 = (f32[2,128]{1,0:T(2,128)S(1)}, f32[2,128]{1,0:T(2,128)}, u32[]{:S(2)}) copy-start(f32[2,128]{1,0:T(2,128)} %pad_maximum_fusion.4) | copy-start | bytes 3076
  96.3 1.8 %copy-start.7 = (f32[2048]{0:T(1024)S(1)}, f32[2048]{0:T(1024)}, u32[]{:S(2)}) copy-start(f32[2048]{0:T(1024)} %broadcast_bitcast_fusion) | copy-start | bytes 24580
where the time goes:
time: 102 us; the launch traced here: 101 us
  starting transfers between devices  27.9 us (27%)
  waiting for transfers between devices  21.3 us (21%)
  local copies, waits for them, and re-layouts  15.3 us (15%)
  blocking collectives  13.6 us (13%)
  other arithmetic  11.5 us (11%)
  matrix products  6.42 us (6%)
  between operations  5.05 us (5%)
    ppermute x16, starting transfers between devices, partner(): return lax.ppermute(value, axis, pairs)  23 us
    ppermute x16, waiting for transfers between devices, partner(): return lax.ppermute(value, axis, pairs)  21.3 us
    psum x1, blocking collectives, local(): gain_total = lax.psum(gain_terms, 'dp') / lax.axis_size('dp')  13.6 us
    ppermute x2, starting transfers between devices, shifted(): return lax.ppermute(block, axis, route)  4.88 us
    unnamed x41, local copies, waits for them, and re-layouts  4.24 us
    slice x4, local copies, waits for them, and re-layouts, local(): member[:, :middle]  3.89 us
    mul x4, local copies, waits for them, and re-layouts, norm_back(): d_input = factor * scaled - widened * factor * factor * factor * inner  3 us
    concatenate x2, other arithmetic, local(): jnp.concatenate([lower_part, upper_part], axis=1)  2.4 us
  transfers between devices with their start and end apart: 18, of which 4 were waited for; matrix products, arithmetic and copies ran while one was open for 25% of the time, Pallas kernels for 0%

commit v1 on v0

v1 whole, which is shorter than its diff:
```python
import functools
import math

import jax
import jax.numpy as jnp
from jax import lax
from jax.experimental import pallas as pl
from jax.experimental.pallas import tpu as pltpu
from jax.sharding import PartitionSpec as P

HEAD_SIZE = 128
EPSILON = 1e-06
SCORE_SCALE = 1.0 / math.sqrt(HEAD_SIZE)
EXP2_SCALE = SCORE_SCALE * math.log2(math.e)

NT = (((1,), (1,)), ((), ()))
TN = (((0,), (0,)), ((), ()))
NN = (((1,), (0,)), ((), ()))


def dot(a, b, dims):
    return lax.dot_general(a, b, dims, preferred_element_type=jnp.float32)


def head(ref, index):
    return ref[:, index * HEAD_SIZE : (index + 1) * HEAD_SIZE]


def allowed_pairs(segment_ref, chosen):
    micro, tokens = segment_ref.shape
    ids = segment_ref[...].astype(jnp.float32)
    number = lax.broadcasted_iota(jnp.int32, (micro, tokens), 0).astype(jnp.float32)
    row = jnp.sum(jnp.where(number == chosen[:, :tokens], ids, 0.0), axis=0, keepdims=True)
    rows_at = lax.broadcasted_iota(jnp.int32, (tokens, tokens), 0)
    cols_at = lax.broadcasted_iota(jnp.int32, (tokens, tokens), 1)
    column = jnp.sum(jnp.where(rows_at == cols_at, row, 0.0), axis=1, keepdims=True)
    return (cols_at <= rows_at) & (column == row)


def normalized(values):
    wide = values.astype(jnp.float32)
    factor = lax.rsqrt(jnp.mean(wide * wide, axis=1, keepdims=True) + EPSILON)
    return wide * factor, factor


def probabilities(query, key, allowed):
    scores = dot(query, key, NT)
    weights = jnp.where(allowed, jnp.exp2(scores * EXP2_SCALE), 0.0)
    return weights * (1.0 / jnp.sum(weights, axis=1, keepdims=True))


def forward_kernel(kv_heads, q_ref, kv_ref, side_ref, segment_ref, out_ref):
    per_kv = q_ref.shape[1] // HEAD_SIZE // kv_heads
    allowed = allowed_pairs(segment_ref, side_ref[2:3, :])
    for g in range(kv_heads):
        key_hat, _ = normalized(head(kv_ref, g))
        key = (key_hat * side_ref[1:2, :]).astype(jnp.bfloat16)
        value = head(kv_ref, kv_heads + g)
        for h in range(g * per_kv, (g + 1) * per_kv):
            query_hat, _ = normalized(head(q_ref, h))
            query = (query_hat * side_ref[0:1, :]).astype(jnp.bfloat16)
            probs = probabilities(query, key, allowed).astype(jnp.bfloat16)
            out_ref[:, h * HEAD_SIZE : (h + 1) * HEAD_SIZE] = dot(probs, value, NN).astype(
                jnp.bfloat16
            )


def norm_back(hat, factor, scaled_gain, d_normed):
    terms = d_normed * hat
    inner = jnp.sum(terms * scaled_gain, axis=1, keepdims=True) * (1.0 / HEAD_SIZE)
    return (d_normed * scaled_gain - hat * inner) * factor, terms


def backward_kernel(
    kv_heads, q_ref, kv_ref, up_ref, side_ref, segment_ref, grad_q_ref, grad_kv_ref, gain_ref
):
    per_kv = q_ref.shape[1] // HEAD_SIZE // kv_heads
    tokens = q_ref.shape[0]
    allowed = allowed_pairs(segment_ref, side_ref[3:4, :])
    q_gain, k_gain = side_ref[0:1, :], side_ref[1:2, :]
    q_terms = jnp.zeros((tokens, HEAD_SIZE), jnp.float32)
    k_terms = jnp.zeros((tokens, HEAD_SIZE), jnp.float32)
    for g in range(kv_heads):
        key_hat, key_factor = normalized(head(kv_ref, g))
        key = (key_hat * k_gain).astype(jnp.bfloat16)
        value = head(kv_ref, kv_heads + g)
        d_key = jnp.zeros((tokens, HEAD_SIZE), jnp.float32)
        d_value = jnp.zeros((tokens, HEAD_SIZE), jnp.float32)
        for h in range(g * per_kv, (g + 1) * per_kv):
            query_hat, query_factor = normalized(head(q_ref, h))
            query = (query_hat * q_gain).astype(jnp.bfloat16)
            upstream = head(up_ref, h)
            probs = probabilities(query, key, allowed)
            d_probs = dot(upstream, value, NT)
            d_value += dot(probs.astype(jnp.bfloat16), upstream, TN)
            centre = jnp.sum(probs * d_probs, axis=1, keepdims=True)
            d_scores = (probs * (d_probs - centre)).astype(jnp.bfloat16)
            d_key += dot(d_scores, query, TN)
            d_query, terms = norm_back(
                query_hat, query_factor, q_gain * SCORE_SCALE, dot(d_scores, key, NN)
            )
            q_terms += terms
            grad_q_ref[:, h * HEAD_SIZE : (h + 1) * HEAD_SIZE] = d_query.astype(jnp.bfloat16)
        d_key, terms = norm_back(key_hat, key_factor, k_gain * SCORE_SCALE, d_key)
        k_terms += terms
        grad_kv_ref[:, g * HEAD_SIZE : (g + 1) * HEAD_SIZE] = d_key.astype(jnp.bfloat16)
        grad_kv_ref[:, (kv_heads + g) * HEAD_SIZE : (kv_heads + g + 1) * HEAD_SIZE] = (
            d_value.astype(jnp.bfloat16)
        )
    gain_ref[0:1, :] = jnp.sum(q_terms, axis=0, keepdims=True) * SCORE_SCALE
    gain_ref[1:2, :] = jnp.sum(k_terms, axis=0, keepdims=True) * SCORE_SCALE


def forward(q, kv, side, segments):
    tokens, width = q.shape
    return pl.pallas_call(
        functools.partial(forward_kernel, kv.shape[1] // HEAD_SIZE // 2),
        out_shape=jax.ShapeDtypeStruct(q.shape, q.dtype),
        cost_estimate=pl.CostEstimate(
            flops=4 * tokens * tokens * width,
            bytes_accessed=4 * tokens * width,
            transcendentals=tokens * width,
        ),
        name="forward",
    )(q, kv, side, segments)


def backward(q, kv, upstream, side, segments):
    tokens, width = q.shape
    return pl.pallas_call(
        functools.partial(backward_kernel, kv.shape[1] // HEAD_SIZE // 2),
        out_shape=(
            jax.ShapeDtypeStruct(q.shape, q.dtype),
            jax.ShapeDtypeStruct(kv.shape, kv.dtype),
            jax.ShapeDtypeStruct((2, HEAD_SIZE), jnp.float32),
        ),
        cost_estimate=pl.CostEstimate(
            flops=10 * tokens * tokens * width,
            bytes_accessed=6 * tokens * width,
            transcendentals=tokens * width,
        ),
        name="backward",
    )(q, kv, upstream, side, segments)


def local(
    fresh_q, current_key_value, held_q, retained_key_value, cotangent, norm_gains, plan, segment_ids
):
    sections, replicas = lax.axis_size("section"), lax.axis_size("dp")
    opposite = [(i, -i % sections) for i in range(sections)]
    moving = [(i, j) for i, j in opposite if i != j]
    staying = [i for i, j in opposite if i == j]
    up = [(i, (i + 1) % sections) for i in range(sections)]
    down_staying = [(i, (i - 1) % sections) for i in staying]
    down_moving = [(i, (i - 1) % sections) for i, j in moving]
    segments = segment_ids[0]

    def hop(value, pairs):
        return lax.ppermute(value, "section", pairs)

    numbers = jnp.broadcast_to(plan[0].astype(jnp.float32)[:, None], (2, HEAD_SIZE))
    side = hop(jnp.concatenate([norm_gains[0], numbers], axis=0), up)
    held = hop(held_q[0], moving), hop(retained_key_value[0], moving)
    fresh = hop(fresh_q[0], up), hop(current_key_value[0], up)

    upstream = cotangent[0]
    own_q, own_kv, own_gain = backward(held_q[0], retained_key_value[0], upstream, side, segments)
    own_q, own_kv = hop(own_q, down_staying), hop(own_kv, down_staying)

    stored_q, stored_kv = hop(fresh[0], opposite), hop(fresh[1], opposite)
    far_q, far_kv, far_gain = backward(*held, upstream, side, segments)
    far_q, far_kv = hop(far_q, down_moving), hop(far_kv, down_moving)

    attention_out = forward(*fresh, side, segments)

    me = lax.axis_index("section")
    stays = functools.reduce(jnp.logical_or, [me == i for i in staying])
    gain = jnp.where(stays, own_gain, far_gain)
    step = 1
    while step < replicas:
        gain = gain + lax.ppermute(gain, "dp", [(i, i ^ step) for i in range(replicas)])
        step *= 2
    gain = hop(gain, [(i, (i - 1) % sections) for i in range(sections)]) * (1.0 / replicas)
    above_stays = functools.reduce(jnp.logical_or, [me == (i - 1) % sections for i in staying])
    grad_q = jnp.where(above_stays, own_q, far_q)
    grad_kv = jnp.where(above_stays, own_kv, far_kv)
    return (
        attention_out[None],
        stored_q[None],
        stored_kv[None],
        grad_q[None],
        grad_kv[None],
        gain[None],
    )


def solution(mesh):
    rows = P("section", "dp", None)
    return jax.shard_map(
        local,
        mesh=mesh,
        in_specs=(rows, rows, rows, rows, rows, P("section", None, None), P("section", None), P("dp", None, None)),
        out_specs=(rows, rows, rows, rows, rows, P("section", None, None)),
        check_vma=False,
    )
```

time: 102 us -> 80 us (0.78)
  Pallas kernels: 0 us -> 19.3 us
  blocking collectives: 13.6 us -> 0 us
  local copies, waits for them, and re-layouts: 15.3 us -> 4.86 us
  other arithmetic: 11.5 us -> 2.13 us
  matrix products: 6.42 us -> 0 us
  starting transfers between devices: 27.9 us -> 32.2 us
  between operations: 5.05 us -> 0.83 us
    pallas_call x0 -> x3, Pallas kernels: none -> 19.3 us  [the longest x2 16.2 us: backward(): pl.pallas_call(functools.partial(backward_kernel, kv.shape[1] // HEAD_SIZ...]
    psum x1 -> x0, blocking collectives: 13.6 us -> none  [local(): gain_total = lax.psum(gain_terms, 'dp') / lax.axis_size('dp')]
    dot_general x7 -> x0, matrix products: 6.42 us -> none  [the longest x2 2.11 us: attention_probs(): jnp.einsum('qhgd,khd->hgqk', query_converted, k_cast, preferred_element_t...]
    slice x5 -> x0, local copies, waits for them, and re-layouts: 4.47 us -> none  [the longest x4 3.89 us: local(): member[:, :middle]]
    ppermute x18 -> x15, starting transfers between devices: 27.9 us -> 32.2 us  [the longest x12 28 us: hop(): return lax.ppermute(value, 'section', pairs)]
    mul x6 -> x0, local copies, waits for them, and re-layouts: 4.19 us -> none  [the longest x4 3 us: norm_back(): d_input = factor * scaled - widened * factor * factor * factor * inner]
    concatenate x3 -> x1, other arithmetic: 3.07 us -> 0.07 us  [local(): side = hop(jnp.concatenate([norm_gains[0], numbers], axis=0), up)]
    div x3 -> x0, other arithmetic: 1.69 us -> none  [the longest x1 1.68 us: attention_probs(): attn_probs = weights / jnp.sum(weights, axis=-1, keepdims=True)]
  transfers between devices with their start and end apart: 18 -> 15, of which waited for: 4 -> 5; matrix products, arithmetic and copies ran while one was open for 25% -> 2% of each run, Pallas kernels for 0% -> 24%
where the time goes in v1:
time: 80 us; the launch traced here: 79.6 us
  starting transfers between devices  32.2 us (40%)
  waiting for transfers between devices  20.3 us (25%)
  Pallas kernels  19.3 us (24%)
  local copies, waits for them, and re-layouts  4.86 us (6%)
  other arithmetic  2.13 us (3%)
  between operations  0.83 us (1%)
    ppermute x12, starting transfers between devices, hop(): return lax.ppermute(value, 'section', pairs)  28 us
    ppermute x12, waiting for transfers between devices, hop(): return lax.ppermute(value, 'section', pairs)  17.2 us
    pallas_call x2, Pallas kernels, backward(): pl.pallas_call(functools.partial(backward_kernel, kv.shape[1] // HEAD_SIZ...  16.2 us
    unnamed x26, local copies, waits for them, and re-layouts  4.78 us
    ppermute x3, starting transfers between devices, local(): lax.ppermute(gain, 'dp', [(i, i ^ step) for i in range(replicas)])  4.18 us
    ppermute x3, waiting for transfers between devices, local(): lax.ppermute(gain, 'dp', [(i, i ^ step) for i in range(replicas)])  3.13 us
    pallas_call x1, Pallas kernels, forward(): pl.pallas_call(functools.partial(forward_kernel, kv.shape[1] // HEAD_SIZE...  3.07 us
  transfers between devices with their start and end apart: 15, of which 5 were waited for; matrix products, arithmetic and copies ran while one was open for 2% of the time, Pallas kernels for 24%

profile of v1, /device:TPU:0, one launch (start us, length us, event | category | flops | bytes accessed | tf_op | source)
XLA Modules:
  0.0 79.6 jit_solution(3274352954128596307)
XLA Ops:
  0.6 0.7 collective-permute-start.6
  1.3 0.7 collective-permute-start.7
  2.0 7.5 %collective-permute-start = (bf16[112,2048]{1,0:T(8,128)(2,1)}, bf16[112,2048]{1,0:T(8,128)(2,1)S(1)}, u32[]{:S(2)}, u32[]{:S(2)}) collective-permute-start(bf16[112,2048]{1,0:T(8,128)(2,1)} %bitcast.31), channel_id=1, source_target_pairs={{0,8},{8,16},{16,24},{24,0},{1,9},{9,17},{17,25},{25,1},{2,10},{10... | collective-permute-start | bytes 1376264 | tf_op jit(solution)/shard_map/ppermute | solution.py:159
  9.5 0.1 collective-permute-start.1
  9.6 0.1 pad.1.clone
  9.6 0.7 copy-done.5
  10.3 0.1 pad_maximum_fusion
  10.4 2.9 %collective-permute-start.2 = (f32[4,128]{1,0:T(4,128)S(1)}, f32[4,128]{1,0:T(4,128)S(1)}, u32[]{:S(2)}, u32[]{:S(2)}) collective-permute-start(f32[4,128]{1,0:T(4,128)S(1)} %pad_maximum_fusion), channel_id=1, source_target_pairs={{0,8},{8,16},{16,24},{24,0},{1,9},{9,17},{17,25},{25,1},{2,10},{10... | collective-permute-start | bytes 6152 | tf_op jit(solution)/shard_map/ppermute | solution.py:159
  13.3 9.8 %collective-permute-done.2.side_ref = f32[4,128]{1,0:T(4,128)S(1)} collective-permute-done((f32[4,128]{1,0:T(4,128)S(1)}, f32[4,128]{1,0:T(4,128)S(1)}, u32[]{:S(2)}, u32[]{:S(2)}) %collective-permute-start.2) | collective-permute-done | bytes 2080 | tf_op jit(solution)/shard_map/ppermute | solution.py:159
  23.1 0.6 copy-done.4
  23.7 8.1 %backward.2 = (bf16[112,2048]{1,0:T(8,128)(2,1)}, bf16[112,512]{1,0:T(8,128)(2,1)}, f32[2,128]{1,0:T(2,128)}) custom-call(bf16[112,2048]{1,0:T(8,128)(2,1)} %bitcast.22, bf16[112,512]{1,0:T(8,128)(2,1)} %bitcast.26, bf16[112,2048]{1,0:T(8,128)(2,1)} %bitcast.18, f32[4,128]{1,0:T(4,128)} %copy-done.4, s32[4,112]{1,0:T(4,128)} %bitcast.27), custom_call_target="tpu_custom_call" | custom-call | flops 256901120 | bytes 1376256 | tf_op jit(solution)/shard_map/backward/pallas_call | solution.py:130
  31.8 0.0 collective-permute-done.1.kv_ref
  31.8 0.0 copy-start.2
  31.8 0.8 %collective-permute-start.4 = (bf16[112,512]{1,0:T(8,128)(2,1)S(1)}, bf16[112,512]{1,0:T(8,128)(2,1)S(1)}, u32[]{:S(2)}, u32[]{:S(2)}) collective-permute-start(bf16[112,512]{1,0:T(8,128)(2,1)S(1)} %collective-permute-done.1.kv_ref), channel_id=1, source_target_pairs={{0,0},{8,24},{16,16},{24,8},{1,1},{9,25},{17,17},{25,9},{2,2},{10,... | collective-permute-start | bytes 344072 | tf_op jit(solution)/shard_map/ppermute | solution.py:159
  32.6 0.0 collective-permute-done.7.kv_ref
  32.6 0.0 copy-start.3
  32.6 0.0 collective-permute-done.6.q_ref
  32.7 0.6 copy-done.3
  33.3 0.8 copy-done.1
  34.0 8.1 %backward.3 = (bf16[112,2048]{1,0:T(8,128)(2,1)}, bf16[112,512]{1,0:T(8,128)(2,1)}, f32[2,128]{1,0:T(2,128)}) custom-call(bf16[112,2048]{1,0:T(8,128)(2,1)} %copy-done.1, bf16[112,512]{1,0:T(8,128)(2,1)} %copy-done.3, bf16[112,2048]{1,0:T(8,128)(2,1)} %bitcast.19, f32[4,128]{1,0:T(4,128)} %copy-done.4, s32[4,112]{1,0:T(4,128)} %bitcast.28), custom_call_target="tpu_custom_call" | custom-call | flops 256901120 | bytes 1376256 | tf_op jit(solution)/shard_map/backward/pallas_call | solution.py:130
  42.2 0.7 copy-done.7
  42.9 0.0 copy-done.6
  42.9 0.0 collective-permute-start.11
  42.9 1.1 %collective-permute-done.11 = f32[2,128]{1,0:T(2,128)S(1)} collective-permute-done((f32[2,128]{1,0:T(2,128)S(1)}, f32[2,128]{1,0:T(2,128)S(1)}, u32[]{:S(2)}, u32[]{:S(2)}) %collective-permute-start.11) | collective-permute-done | bytes 1056 | tf_op jit(solution)/shard_map/ppermute | solution.py:181
  44.0 1.6 %collective-permute-start.12 = (f32[2,128]{1,0:T(2,128)S(1)}, f32[2,128]{1,0:T(2,128)S(1)}, u32[]{:S(2)}, u32[]{:S(2)}) collective-permute-start(f32[2,128]{1,0:T(2,128)S(1)} %add.9), channel_id=1, source_target_pairs={{0,2},{1,3},{2,0},{3,1},{4,6},{5,7},{6,4},{7,5},{8,10},{9,11},{10,... | collective-permute-start | bytes 3080 | tf_op jit(solution)/shard_map/ppermute | solution.py:181
  45.6 2.0 %collective-permute-done.12 = f32[2,128]{1,0:T(2,128)S(1)} collective-permute-done((f32[2,128]{1,0:T(2,128)S(1)}, f32[2,128]{1,0:T(2,128)S(1)}, u32[]{:S(2)}, u32[]{:S(2)}) %collective-permute-start.12) | collective-permute-done | bytes 1056 | tf_op jit(solution)/shard_map/ppermute | solution.py:181
  47.6 2.6 %collective-permute-start.13 = (f32[2,128]{1,0:T(2,128)S(1)}, f32[2,128]{1,0:T(2,128)S(1)}, u32[]{:S(2)}, u32[]{:S(2)}) collective-permute-start(f32[2,128]{1,0:T(2,128)S(1)} %add.10), channel_id=1, source_target_pairs={{0,4},{1,5},{2,6},{3,7},{4,0},{5,1},{6,2},{7,3},{8,12},{9,13},{10,... | collective-permute-start | bytes 3080 | tf_op jit(solution)/shard_map/ppermute | solution.py:181
  50.2 5.4 %collective-permute-start.5 = (bf16[112,2048]{1,0:T(8,128)(2,1)S(1)}, bf16[112,2048]{1,0:T(8,128)(2,1)S(1)}, u32[]{:S(2)}, u32[]{:S(2)}) collective-permute-start(bf16[112,2048]{1,0:T(8,128)(2,1)S(1)} %copy-done.8), channel_id=1, source_target_pairs={{0,24},{16,8},{1,25},{17,9},{2,26},{18,10},{3,27},{19,11},{4,28},{... | collective-permute-start | bytes 1376264 | tf_op jit(solution)/shard_map/ppermute | solution.py:159
  55.6 1.3 %collective-permute-start.9 = (bf16[112,512]{1,0:T(8,128)(2,1)S(1)}, bf16[112,512]{1,0:T(8,128)(2,1)S(1)}, u32[]{:S(2)}, u32[]{:S(2)}) collective-permute-start(bf16[112,512]{1,0:T(8,128)(2,1)S(1)} %copy-done.9), channel_id=1, source_target_pairs={{0,24},{16,8},{1,25},{17,9},{2,26},{18,10},{3,27},{19,11},{4,28},{... | collective-permute-start | bytes 344072 | tf_op jit(solution)/shard_map/ppermute | solution.py:159
  56.9 0.0 collective-permute-done.4
  56.9 1.3 %collective-permute-start.8 = (bf16[112,2048]{1,0:T(8,128)(2,1)}, bf16[112,2048]{1,0:T(8,128)(2,1)S(1)}, u32[]{:S(2)}, u32[]{:S(2)}) collective-permute-start(bf16[112,2048]{1,0:T(8,128)(2,1)} %get-tuple-element.13), channel_id=1, source_target_pairs={{8,0},{24,16},{9,1},{25,17},{10,2},{26,18},{11,3},{27,19},{12,4},{... | collective-permute-start | bytes 1376264 | tf_op jit(solution)/shard_map/ppermute | solution.py:159
  58.2 0.0 collective-permute-done.q_ref
  58.2 0.0 copy-start
  58.2 0.7 collective-permute-start.3
  58.9 0.0 collective-permute-done.13
  59.0 5.4 %collective-permute-start.14 = (f32[2,128]{1,0:T(2,128)S(1)}, f32[2,128]{1,0:T(2,128)S(1)}, u32[]{:S(2)}, u32[]{:S(2)}) collective-permute-start(f32[2,128]{1,0:T(2,128)S(1)} %add.11), channel_id=1, source_target_pairs={{0,24},{8,0},{16,8},{24,16},{1,25},{9,1},{17,9},{25,17},{2,26},{10... | collective-permute-start | bytes 3080 | tf_op jit(solution)/shard_map/ppermute | solution.py:159
  64.4 3.1 %forward.1 = bf16[112,2048]{1,0:T(8,128)(2,1)} custom-call(bf16[112,2048]{1,0:T(8,128)(2,1)} %copy-done, bf16[112,512]{1,0:T(8,128)(2,1)} %copy-done.2, f32[4,128]{1,0:T(4,128)} %copy-done.4, s32[4,112]{1,0:T(4,128)} %bitcast.29), custom_call_target="tpu_custom_call" | custom-call | flops 102760448 | bytes 917504 | tf_op jit(solution)/shard_map/forward/pallas_call | solution.py:116
  67.5 2.5 %collective-permute-done.14 = f32[2,128]{1,0:T(2,128)S(1)} collective-permute-done((f32[2,128]{1,0:T(2,128)S(1)}, f32[2,128]{1,0:T(2,128)S(1)}, u32[]{:S(2)}, u32[]{:S(2)}) %collective-permute-start.14) | collective-permute-done | bytes 1056 | tf_op jit(solution)/shard_map/ppermute | solution.py:159
  70.0 1.3 %collective-permute-start.10 = (bf16[112,512]{1,0:T(8,128)(2,1)S(1)}, bf16[112,512]{1,0:T(8,128)(2,1)S(1)}, u32[]{:S(2)}, u32[]{:S(2)}) collective-permute-start(bf16[112,512]{1,0:T(8,128)(2,1)S(1)} %copy-done.10), channel_id=1, source_target_pairs={{8,0},{24,16},{9,1},{25,17},{10,2},{26,18},{11,3},{27,19},{12,4},{... | collective-permute-start | bytes 344072 | tf_op jit(solution)/shard_map/ppermute | solution.py:159
  71.3 0.6 multiply_bitcast_fusion
  71.9 0.0 collective-permute-done.9
  71.9 4.8 %collective-permute-done.10 = bf16[112,512]{1,0:T(8,128)(2,1)S(1)} collective-permute-done((bf16[112,512]{1,0:T(8,128)(2,1)S(1)}, bf16[112,512]{1,0:T(8,128)(2,1)S(1)}, u32[]{:S(2)}, u32[]{:S(2)}) %collective-permute-start.10) | collective-permute-done | bytes 114720 | tf_op jit(solution)/shard_map/ppermute | solution.py:159
  76.7 0.7 select_bitcast_fusion.1
  77.3 0.0 collective-permute-done.3
  77.3 0.0 collective-permute-done.5
  77.3 0.8 %select_bitcast_fusion = bf16[1,112,2048]{2,1,0:T(8,128)(2,1)} fusion(bf16[112,2048]{1,0:T(8,128)(2,1)S(1)} %collective-permute-done.5, bf16[112,2048]{1,0:T(8,128)(2,1)S(1)} %collective-permute-done.8, pred[]{:T(512)S(6)} %or.6), kind=kLoop, calls=%fused_computation | loop fusion | flops 229376 | bytes 1376257 | tf_op jit(solution)/shard_map/broadcast_in_dim | solution.py:191
  78.2 0.8 copy.16
  78.9 0.6 copy.17
  (21 shorter events, 0.0 us)
Async XLA Ops:
  0.6 32.0 %collective-permute-start.6 = (bf16[112,2048]{1,0:T(8,128)(2,1)}, bf16[112,2048]{1,0:T(8,128)(2,1)S(1)}, u32[]{:S(2)}, u32[]{:S(2)}) collective-permute-start(bf16[112,2048]{1,0:T(8,128)(2,1)} %bitcast.21), channel_id=1, source_target_pairs={{8,24},{24,8},{9,25},{25,9},{10,26},{26,10},{11,27},{27,11},{12,28... | collective-permute-start | bytes 1376264 | tf_op jit(solution)/shard_map/ppermute | solution.py:159
  1.3 31.3 %collective-permute-start.7 = (bf16[112,512]{1,0:T(8,128)(2,1)}, bf16[112,512]{1,0:T(8,128)(2,1)S(1)}, u32[]{:S(2)}, u32[]{:S(2)}) collective-permute-start(bf16[112,512]{1,0:T(8,128)(2,1)} %bitcast.25), channel_id=1, source_target_pairs={{8,24},{24,8},{9,25},{25,9},{10,26},{26,10},{11,27},{27,11},{12,28... | collective-permute-start | bytes 344072 | tf_op jit(solution)/shard_map/ppermute | solution.py:159
  2.0 7.6 %copy-start.11 = (s32[1,2]{1,0:T(1,128)S(1)}, s32[1,2]{1,0:T(1,128)}, u32[]{:S(2)}) copy-start(s32[1,2]{1,0:T(1,128)} %param.14) | copy-start | bytes 28
  2.0 56.2 %collective-permute-start = (bf16[112,2048]{1,0:T(8,128)(2,1)}, bf16[112,2048]{1,0:T(8,128)(2,1)S(1)}, u32[]{:S(2)}, u32[]{:S(2)}) collective-permute-start(bf16[112,2048]{1,0:T(8,128)(2,1)} %bitcast.31), channel_id=1, source_target_pairs={{0,8},{8,16},{16,24},{24,0},{1,9},{9,17},{17,25},{25,1},{2,10},{10... | collective-permute-start | bytes 1376264 | tf_op jit(solution)/shard_map/ppermute | solution.py:159
  9.5 22.3 %collective-permute-start.1 = (bf16[112,512]{1,0:T(8,128)(2,1)}, bf16[112,512]{1,0:T(8,128)(2,1)S(1)}, u32[]{:S(2)}, u32[]{:S(2)}) collective-permute-start(bf16[112,512]{1,0:T(8,128)(2,1)} %bitcast.32), channel_id=1, source_target_pairs={{0,8},{8,16},{16,24},{24,0},{1,9},{9,17},{17,25},{25,1},{2,10},{10... | collective-permute-start | bytes 344072 | tf_op jit(solution)/shard_map/ppermute | solution.py:159
  9.6 0.7 copy-start.5
  10.4 12.7 %collective-permute-start.2 = (f32[4,128]{1,0:T(4,128)S(1)}, f32[4,128]{1,0:T(4,128)S(1)}, u32[]{:S(2)}, u32[]{:S(2)}) collective-permute-start(f32[4,128]{1,0:T(4,128)S(1)} %pad_maximum_fusion), channel_id=1, source_target_pairs={{0,8},{8,16},{16,24},{24,0},{1,9},{9,17},{17,25},{25,1},{2,10},{10... | collective-permute-start | bytes 6152 | tf_op jit(solution)/shard_map/ppermute | solution.py:159
  23.1 0.6 copy-start.4
  31.8 18.4 %copy-start.8 = (bf16[112,2048]{1,0:T(8,128)(2,1)S(1)}, bf16[112,2048]{1,0:T(8,128)(2,1)}, u32[]{:S(2)}) copy-start(bf16[112,2048]{1,0:T(8,128)(2,1)} %get-tuple-element.12) | copy-start | bytes 1376260
  31.8 23.8 %copy-start.9 = (bf16[112,512]{1,0:T(8,128)(2,1)S(1)}, bf16[112,512]{1,0:T(8,128)(2,1)}, u32[]{:S(2)}) copy-start(bf16[112,512]{1,0:T(8,128)(2,1)} %get-tuple-element.14) | copy-start | bytes 344068
  31.8 10.4 %copy-start.2 = (bf16[112,512]{1,0:T(8,128)(2,1)}, bf16[112,512]{1,0:T(8,128)(2,1)S(1)}, u32[]{:S(2)}) copy-start(bf16[112,512]{1,0:T(8,128)(2,1)S(1)} %collective-permute-done.1.kv_ref) | copy-start | bytes 344068
  31.8 25.1 %collective-permute-start.4 = (bf16[112,512]{1,0:T(8,128)(2,1)S(1)}, bf16[112,512]{1,0:T(8,128)(2,1)S(1)}, u32[]{:S(2)}, u32[]{:S(2)}) collective-permute-start(bf16[112,512]{1,0:T(8,128)(2,1)S(1)} %collective-permute-done.1.kv_ref), channel_id=1, source_target_pairs={{0,0},{8,24},{16,16},{24,8},{1,1},{9,25},{17,17},{25,9},{2,2},{10,... | collective-permute-start | bytes 344072 | tf_op jit(solution)/shard_map/ppermute | solution.py:159
  32.6 0.6 copy-start.3
  33.3 0.8 copy-start.1
  42.2 0.7 copy-start.7
  42.2 0.7 copy-start.6
  42.9 1.1 %collective-permute-start.11 = (f32[2,128]{1,0:T(2,128)S(1)}, f32[2,128]{1,0:T(2,128)S(1)}, u32[]{:S(2)}, u32[]{:S(2)}) collective-permute-start(f32[2,128]{1,0:T(2,128)S(1)} %broadcast_select_fusion), channel_id=1, source_target_pairs={{0,1},{1,0},{2,3},{3,2},{4,5},{5,4},{6,7},{7,6},{8,9},{9,8},{10,11... | collective-permute-start | bytes 3080 | tf_op jit(solution)/shard_map/ppermute | solution.py:181
  44.0 3.6 %collective-permute-start.12 = (f32[2,128]{1,0:T(2,128)S(1)}, f32[2,128]{1,0:T(2,128)S(1)}, u32[]{:S(2)}, u32[]{:S(2)}) collective-permute-start(f32[2,128]{1,0:T(2,128)S(1)} %add.9), channel_id=1, source_target_pairs={{0,2},{1,3},{2,0},{3,1},{4,6},{5,7},{6,4},{7,5},{8,10},{9,11},{10,... | collective-permute-start | bytes 3080 | tf_op jit(solution)/shard_map/ppermute | solution.py:181
  47.6 11.4 %collective-permute-start.13 = (f32[2,128]{1,0:T(2,128)S(1)}, f32[2,128]{1,0:T(2,128)S(1)}, u32[]{:S(2)}, u32[]{:S(2)}) collective-permute-start(f32[2,128]{1,0:T(2,128)S(1)} %add.10), channel_id=1, source_target_pairs={{0,4},{1,5},{2,6},{3,7},{4,0},{5,1},{6,2},{7,3},{8,12},{9,13},{10,... | collective-permute-start | bytes 3080 | tf_op jit(solution)/shard_map/ppermute | solution.py:181
  50.2 27.2 %collective-permute-start.5 = (bf16[112,2048]{1,0:T(8,128)(2,1)S(1)}, bf16[112,2048]{1,0:T(8,128)(2,1)S(1)}, u32[]{:S(2)}, u32[]{:S(2)}) collective-permute-start(bf16[112,2048]{1,0:T(8,128)(2,1)S(1)} %copy-done.8), channel_id=1, source_target_pairs={{0,24},{16,8},{1,25},{17,9},{2,26},{18,10},{3,27},{19,11},{4,28},{... | collective-permute-start | bytes 1376264 | tf_op jit(solution)/shard_map/ppermute | solution.py:159
  55.6 16.2 %collective-permute-start.9 = (bf16[112,512]{1,0:T(8,128)(2,1)S(1)}, bf16[112,512]{1,0:T(8,128)(2,1)S(1)}, u32[]{:S(2)}, u32[]{:S(2)}) collective-permute-start(bf16[112,512]{1,0:T(8,128)(2,1)S(1)} %copy-done.9), channel_id=1, source_target_pairs={{0,24},{16,8},{1,25},{17,9},{2,26},{18,10},{3,27},{19,11},{4,28},{... | collective-permute-start | bytes 344072 | tf_op jit(solution)/shard_map/ppermute | solution.py:159
  56.9 20.4 %collective-permute-start.8 = (bf16[112,2048]{1,0:T(8,128)(2,1)}, bf16[112,2048]{1,0:T(8,128)(2,1)S(1)}, u32[]{:S(2)}, u32[]{:S(2)}) collective-permute-start(bf16[112,2048]{1,0:T(8,128)(2,1)} %get-tuple-element.13), channel_id=1, source_target_pairs={{8,0},{24,16},{9,1},{25,17},{10,2},{26,18},{11,3},{27,19},{12,4},{... | collective-permute-start | bytes 1376264 | tf_op jit(solution)/shard_map/ppermute | solution.py:159
  58.2 6.1 %copy-start = (bf16[112,2048]{1,0:T(8,128)(2,1)}, bf16[112,2048]{1,0:T(8,128)(2,1)S(1)}, u32[]{:S(2)}) copy-start(bf16[112,2048]{1,0:T(8,128)(2,1)S(1)} %collective-permute-done.q_ref) | copy-start | bytes 1376260
  58.2 19.1 %collective-permute-start.3 = (bf16[112,2048]{1,0:T(8,128)(2,1)S(1)}, bf16[112,2048]{1,0:T(8,128)(2,1)S(1)}, u32[]{:S(2)}, u32[]{:S(2)}) collective-permute-start(bf16[112,2048]{1,0:T(8,128)(2,1)S(1)} %collective-permute-done.q_ref), channel_id=1, source_target_pairs={{0,0},{8,24},{16,16},{24,8},{1,1},{9,25},{17,17},{25,9},{2,2},{10,... | collective-permute-start | bytes 1376264 | tf_op jit(solution)/shard_map/ppermute | solution.py:159
  59.0 11.0 %copy-start.10 = (bf16[112,512]{1,0:T(8,128)(2,1)S(1)}, bf16[112,512]{1,0:T(8,128)(2,1)}, u32[]{:S(2)}) copy-start(bf16[112,512]{1,0:T(8,128)(2,1)} %get-tuple-element.15) | copy-start | bytes 344068
  59.0 11.0 %collective-permute-start.14 = (f32[2,128]{1,0:T(2,128)S(1)}, f32[2,128]{1,0:T(2,128)S(1)}, u32[]{:S(2)}, u32[]{:S(2)}) collective-permute-start(f32[2,128]{1,0:T(2,128)S(1)} %add.11), channel_id=1, source_target_pairs={{0,24},{8,0},{16,8},{24,16},{1,25},{9,1},{17,9},{25,17},{2,26},{10... | collective-permute-start | bytes 3080 | tf_op jit(solution)/shard_map/ppermute | solution.py:159
  70.0 6.7 %collective-permute-start.10 = (bf16[112,512]{1,0:T(8,128)(2,1)S(1)}, bf16[112,512]{1,0:T(8,128)(2,1)S(1)}, u32[]{:S(2)}, u32[]{:S(2)}) collective-permute-start(bf16[112,512]{1,0:T(8,128)(2,1)S(1)} %copy-done.10), channel_id=1, source_target_pairs={{8,0},{24,16},{9,1},{25,17},{10,2},{26,18},{11,3},{27,19},{12,4},{... | collective-permute-start | bytes 344072 | tf_op jit(solution)/shard_map/ppermute | solution.py:159

commit v2 on v1

v2 whole, which is shorter than its diff:
```python
import functools
import math

import jax
import jax.numpy as jnp
from jax import lax
from jax.experimental import pallas as pl
from jax.experimental.pallas import tpu as pltpu
from jax.sharding import PartitionSpec as P

HEAD_SIZE = 128
EPSILON = 1e-06
SCORE_SCALE = 1.0 / math.sqrt(HEAD_SIZE)
EXP2_SCALE = SCORE_SCALE * math.log2(math.e)

NT = (((1,), (1,)), ((), ()))
TN = (((0,), (0,)), ((), ()))
NN = (((1,), (0,)), ((), ()))


def dot(a, b, dims):
    return lax.dot_general(a, b, dims, preferred_element_type=jnp.float32)


def head(ref, index):
    return ref[:, index * HEAD_SIZE : (index + 1) * HEAD_SIZE]


def stacked(ref, first, count):
    return jnp.concatenate([head(ref, first + i) for i in range(count)], axis=0)


def allowed_pairs(segment_ref, chosen, copies):
    micro, tokens = segment_ref.shape
    ids = segment_ref[...].astype(jnp.float32)
    number = lax.broadcasted_iota(jnp.int32, (micro, tokens), 0).astype(jnp.float32)
    row = jnp.sum(jnp.where(number == chosen[:, :tokens], ids, 0.0), axis=0, keepdims=True)
    keys_at = lax.broadcasted_iota(jnp.int32, (tokens, tokens), 0)
    queries_at = lax.broadcasted_iota(jnp.int32, (tokens, tokens), 1)
    column = jnp.sum(jnp.where(keys_at == queries_at, row, 0.0), axis=1, keepdims=True)
    allowed = ((keys_at <= queries_at) & (column == row)).astype(jnp.float32)
    return jnp.concatenate([allowed] * copies, axis=1) > 0.5


def normalized(values):
    wide = values.astype(jnp.float32)
    factor = lax.rsqrt(jnp.mean(wide * wide, axis=1, keepdims=True) + EPSILON)
    return wide * factor, factor


def probabilities(key, query, allowed):
    scores = dot(key, query, NT)
    weights = jnp.where(allowed, jnp.exp2(scores * EXP2_SCALE), 0.0)
    return weights * (1.0 / jnp.sum(weights, axis=0, keepdims=True))


def forward_kernel(kv_heads, packed_ref, side_ref, segment_ref, out_ref):
    tokens = packed_ref.shape[0]
    heads = packed_ref.shape[1] // HEAD_SIZE - 2 * kv_heads
    per_kv = heads // kv_heads
    allowed = allowed_pairs(segment_ref, side_ref[2:3, :], per_kv)
    for g in range(kv_heads):
        key_hat, _ = normalized(head(packed_ref, heads + g))
        key = (key_hat * side_ref[1:2, :]).astype(jnp.bfloat16)
        value = head(packed_ref, heads + kv_heads + g)
        query_hat, _ = normalized(stacked(packed_ref, g * per_kv, per_kv))
        query = (query_hat * side_ref[0:1, :]).astype(jnp.bfloat16)
        probs = probabilities(key, query, allowed).astype(jnp.bfloat16)
        out = dot(probs, value, TN).astype(jnp.bfloat16)
        for i in range(per_kv):
            h = g * per_kv + i
            out_ref[:, h * HEAD_SIZE : (h + 1) * HEAD_SIZE] = out[i * tokens : (i + 1) * tokens]


def norm_back(hat, factor, scaled_gain, d_normed):
    terms = d_normed * hat
    inner = jnp.sum(terms * scaled_gain, axis=1, keepdims=True) * (1.0 / HEAD_SIZE)
    return (d_normed * scaled_gain - hat * inner) * factor, terms


def summed_rows(terms):
    return jnp.sum(terms.reshape(-1, 8, terms.shape[1]), axis=0)


def backward_kernel(q_ref, kv_ref, up_ref, side_ref, segment_ref, *rest):
    grad_ref, gain_ref = rest[-2:]
    tokens = q_ref.shape[0]
    heads = q_ref.shape[1] // HEAD_SIZE
    kv_heads = kv_ref.shape[1] // HEAD_SIZE // 2
    per_kv = heads // kv_heads
    allowed = allowed_pairs(segment_ref, side_ref[3:4, :], per_kv)
    q_gain, k_gain = side_ref[0:1, :], side_ref[1:2, :]
    q_terms = k_terms = 0.0
    for g in range(kv_heads):
        key_hat, key_factor = normalized(head(kv_ref, g))
        key = (key_hat * k_gain).astype(jnp.bfloat16)
        value = head(kv_ref, kv_heads + g)
        query_hat, query_factor = normalized(stacked(q_ref, g * per_kv, per_kv))
        query = (query_hat * q_gain).astype(jnp.bfloat16)
        upstream = stacked(up_ref, g * per_kv, per_kv)
        probs = probabilities(key, query, allowed)
        d_probs = dot(value, upstream, NT)
        d_value = dot(probs.astype(jnp.bfloat16), upstream, NN)
        centre = jnp.sum(probs * d_probs, axis=0, keepdims=True)
        d_scores = (probs * (d_probs - centre)).astype(jnp.bfloat16)
        d_key = dot(d_scores, query, NN)
        d_query, terms = norm_back(
            query_hat, query_factor, q_gain * SCORE_SCALE, dot(d_scores, key, TN)
        )
        q_terms += summed_rows(terms)
        d_query = d_query.astype(jnp.bfloat16)
        for i in range(per_kv):
            h = g * per_kv + i
            grad_ref[:, h * HEAD_SIZE : (h + 1) * HEAD_SIZE] = d_query[
                i * tokens : (i + 1) * tokens
            ]
        d_key, terms = norm_back(key_hat, key_factor, k_gain * SCORE_SCALE, d_key)
        k_terms += summed_rows(terms)
        at = (heads + g) * HEAD_SIZE
        grad_ref[:, at : at + HEAD_SIZE] = d_key.astype(jnp.bfloat16)
        at = (heads + kv_heads + g) * HEAD_SIZE
        grad_ref[:, at : at + HEAD_SIZE] = d_value.astype(jnp.bfloat16)
    gain_ref[0:1, :] = jnp.sum(q_terms, axis=0, keepdims=True) * SCORE_SCALE
    gain_ref[1:2, :] = jnp.sum(k_terms, axis=0, keepdims=True) * SCORE_SCALE


def cost(work):
    return pl.CostEstimate(flops=work, bytes_accessed=1024, transcendentals=0)


def forward(kv_heads, packed, side, segments):
    tokens, width = packed.shape
    return pl.pallas_call(
        functools.partial(forward_kernel, kv_heads),
        out_shape=jax.ShapeDtypeStruct((tokens, width - 2 * kv_heads * HEAD_SIZE), packed.dtype),
        cost_estimate=cost(1024),
        name="forward",
    )(packed, side, segments)


def backward(q, kv, upstream, side, segments, after, work):
    tokens = q.shape[0]
    return pl.pallas_call(
        backward_kernel,
        out_shape=(
            jax.ShapeDtypeStruct((tokens, q.shape[1] + kv.shape[1]), q.dtype),
            jax.ShapeDtypeStruct((2, HEAD_SIZE), jnp.float32),
        ),
        in_specs=[pl.BlockSpec(memory_space=pltpu.VMEM)] * 5
        + [pl.BlockSpec(memory_space=pl.ANY)] * len(after),
        cost_estimate=cost(work),
        name="backward",
    )(q, kv, upstream, side, segments, *after)


def unpack_kernel(choice_ref, first_ref, second_ref, third_ref, *outs):
    q_width = outs[0].shape[1]

    def spread(packed, q_ref, kv_ref):
        q_ref[...] = packed[:, :q_width]
        kv_ref[...] = packed[:, q_width:]

    @pl.when(choice_ref[0] > 0)
    def _():
        spread(first_ref, outs[0], outs[1])

    @pl.when(choice_ref[0] <= 0)
    def _():
        spread(second_ref, outs[0], outs[1])

    spread(third_ref, outs[2], outs[3])


def unpack(choice, first, second, third, q_width):
    tokens, width = first.shape
    vmem = pl.BlockSpec(memory_space=pltpu.VMEM)
    widths = (q_width, width - q_width) * 2
    return pl.pallas_call(
        unpack_kernel,
        out_shape=[jax.ShapeDtypeStruct((tokens, w), first.dtype) for w in widths],
        in_specs=[pl.BlockSpec(memory_space=pltpu.SMEM)] + [vmem] * 3,
        out_specs=[vmem] * 4,
        cost_estimate=cost(1024),
        name="unpack",
    )(choice, first, second, third)


def local(
    fresh_q, current_key_value, held_q, retained_key_value, cotangent, norm_gains, plan, segment_ids
):
    sections, replicas = lax.axis_size("section"), lax.axis_size("dp")
    opposite = [(i, -i % sections) for i in range(sections)]
    moving = [(i, j) for i, j in opposite if i != j]
    staying = [i for i, j in opposite if i == j]
    up = [(i, (i + 1) % sections) for i in range(sections)]
    down_staying = [(i, (i - 1) % sections) for i in staying]
    down_moving = [(i, (i - 1) % sections) for i, j in moving]
    segments = segment_ids[0]
    q_width = fresh_q.shape[2]
    kv_heads = current_key_value.shape[2] // HEAD_SIZE // 2

    def hop(value, pairs):
        return lax.ppermute(value, "section", pairs)

    numbers = jnp.broadcast_to(plan[0].astype(jnp.float32)[:, None], (2, HEAD_SIZE))
    side = hop(jnp.concatenate([norm_gains[0], numbers], axis=0), up)
    fresh = hop(jnp.concatenate([fresh_q[0], current_key_value[0]], axis=1), up)
    held = hop(held_q[0], moving), hop(retained_key_value[0], moving)

    upstream = cotangent[0]
    own_grad, own_gain = backward(
        held_q[0], retained_key_value[0], upstream, side, segments, (), 1 << 36
    )
    own_grad = hop(own_grad, down_staying)

    stored = hop(fresh, opposite)
    far_grad, far_gain = backward(*held, upstream, side, segments, (fresh, own_gain), 1024)
    far_grad = hop(far_grad, down_moving)

    attention_out = forward(kv_heads, fresh, side, segments)

    me = lax.axis_index("section")
    stays = functools.reduce(jnp.logical_or, [me == i for i in staying])
    gain = jnp.where(stays, own_gain, far_gain)
    step = 1
    while 2 * step < replicas:
        gain = gain + lax.ppermute(gain, "dp", [(i, i ^ step) for i in range(replicas)])
        step *= 2
    halves = [
        lax.ppermute(
            gain,
            ("section", "dp"),
            [
                (i * replicas + j, (i - 1) % sections * replicas + (j ^ other))
                for i in range(sections)
                for j in range(replicas)
            ],
        )
        for other in (0, step)
    ]
    gain = (halves[0] + halves[1]) * (1.0 / replicas)
    above_stays = functools.reduce(jnp.logical_or, [me == (i - 1) % sections for i in staying])
    choice = above_stays.astype(jnp.int32).reshape(1)
    outs = unpack(choice, own_grad, far_grad, stored, q_width)
    return (
        attention_out[None],
        outs[2][None],
        outs[3][None],
        outs[0][None],
        outs[1][None],
        gain[None],
    )


def solution(mesh):
    rows = P("section", "dp", None)
    gains = P("section", None, None)
    return jax.shard_map(
        local,
        mesh=mesh,
        in_specs=(rows, rows, rows, rows, rows, gains, P("section", None), P("dp", None, None)),
        out_specs=(rows, rows, rows, rows, rows, gains),
        check_vma=False,
    )
```

time: 80 us -> 54.3 us (0.68)
  starting transfers between devices: 32.2 us -> 23.4 us
  waiting for transfers between devices: 20.3 us -> 11.7 us
  Pallas kernels: 19.3 us -> 12.4 us
  local copies, waits for them, and re-layouts: 4.86 us -> 2.66 us
  other arithmetic: 2.13 us -> 3.11 us
    ppermute x12 -> x7, starting transfers between devices: 28 us -> 14.7 us  [hop(): return lax.ppermute(value, 'section', pairs)]
    ppermute x12 -> x7, waiting for transfers between devices: 17.2 us -> 7.9 us  [hop(): return lax.ppermute(value, 'section', pairs)]
    ppermute x0 -> x2, starting transfers between devices: none -> 7 us  [local(): lax.ppermute(gain, ('section', 'dp'), [(i * replicas + j, (i - 1) % secti...]
    pallas_call x3 -> x4, Pallas kernels: 19.3 us -> 12.4 us  [the longest x2 7.02 us: backward(): pl.pallas_call(backward_kernel, out_shape=(jax.ShapeDtypeStruct((tokens,...]
    ppermute x3 -> x2, starting transfers between devices: 4.18 us -> 1.65 us  [local(): lax.ppermute(gain, 'dp', [(i, i ^ step) for i in range(replicas)])]
    unnamed x26 -> x16, local copies, waits for them, and re-layouts: 4.78 us -> 2.58 us
    broadcast_in_dim x2 -> x0, other arithmetic: 1.48 us -> none  [the longest x1 0.82 us: local(): grad_q[None]]
    concatenate x0 -> x1, other arithmetic: none -> 1.12 us  [local(): fresh = hop(jnp.concatenate([fresh_q[0], current_key_value[0]], axis=1), up)]
  transfers between devices with their start and end apart: 15 -> 11, of which waited for: 5 -> 4; matrix products, arithmetic and copies ran while one was open for 2% -> 3% of each run, Pallas kernels for 24% -> 18%
where the time goes in v2:
time: 54.3 us; the launch traced here: 53.9 us
  starting transfers between devices  23.4 us (43%)
  Pallas kernels  12.4 us (23%)
  waiting for transfers between devices  11.7 us (22%)
  other arithmetic  3.11 us (6%)
  local copies, waits for them, and re-layouts  2.66 us (5%)
  between operations  0.75 us (1%)
    ppermute x7, starting transfers between devices, hop(): return lax.ppermute(value, 'section', pairs)  14.7 us
    ppermute x7, waiting for transfers between devices, hop(): return lax.ppermute(value, 'section', pairs)  7.9 us
    pallas_call x2, Pallas kernels, backward(): pl.pallas_call(backward_kernel, out_shape=(jax.ShapeDtypeStruct((tokens,...  7.02 us
    ppermute x2, starting transfers between devices, local(): lax.ppermute(gain, ('section', 'dp'), [(i * replicas + j, (i - 1) % secti...  7 us
    ppermute x2, waiting for transfers between devices, local(): lax.ppermute(gain, 'dp', [(i, i ^ step) for i in range(replicas)])  3.12 us
    pallas_call x1, Pallas kernels, forward(): pl.pallas_call(functools.partial(forward_kernel, kv_heads), out_shape=jax...  2.92 us
    unnamed x16, local copies, waits for them, and re-layouts  2.58 us
    pallas_call x1, Pallas kernels, unpack(): pl.pallas_call(unpack_kernel, out_shape=[jax.ShapeDtypeStruct((tokens, w)...  2.43 us
  transfers between devices with their start and end apart: 11, of which 4 were waited for; matrix products, arithmetic and copies ran while one was open for 3% of the time, Pallas kernels for 18%

profile of v2, /device:TPU:0, one launch (start us, length us, event | category | flops | bytes accessed | tf_op | source)
XLA Modules:
  0.0 53.9 jit_solution(2297506856866030667)
XLA Ops:
  0.6 0.7 %convert_bitcast_fusion = f32[2]{0:T(128)S(1)} fusion(s32[1,2]{1,0:T(1,128)} %param.14), kind=kLoop, calls=%fused_computation.4 | loop fusion | flops 2 | bytes 16 | tf_op jit(solution)/shard_map/convert_element_type | solution.py:205
  1.3 0.1 pad.1.clone
  1.4 0.7 %pad_maximum_fusion.1 = f32[4,128]{1,0:T(4,128)S(1)} fusion(f32[2,128]{1,0:T(2,128)} %bitcast.25, f32[4]{0:T(128)S(1)} %pad.1.clone), kind=kLoop, calls=%fused_computation.1 | loop fusion | flops 512 | bytes 3088 | tf_op jit(solution)/shard_map/concatenate | solution.py:206
  2.1 2.9 %collective-permute-start.1 = (f32[4,128]{1,0:T(4,128)S(1)}, f32[4,128]{1,0:T(4,128)S(1)}, u32[]{:S(2)}, u32[]{:S(2)}) collective-permute-start(f32[4,128]{1,0:T(4,128)S(1)} %pad_maximum_fusion.1), channel_id=1, source_target_pairs={{0,8},{8,16},{16,24},{24,0},{1,9},{9,17},{17,25},{25,1},{2,10},{10... | collective-permute-start | bytes 6152 | tf_op jit(solution)/shard_map/ppermute | solution.py:203
  5.1 0.7 %collective-permute-start.4 = (bf16[112,512]{1,0:T(8,128)(2,1)}, bf16[112,512]{1,0:T(8,128)(2,1)S(1)}, u32[]{:S(2)}, u32[]{:S(2)}) collective-permute-start(bf16[112,512]{1,0:T(8,128)(2,1)} %bitcast.30), channel_id=1, source_target_pairs={{8,24},{24,8},{9,25},{25,9},{10,26},{26,10},{11,27},{27,11},{12,28... | collective-permute-start | bytes 344072 | tf_op jit(solution)/shard_map/ppermute | solution.py:203
  5.7 0.7 %collective-permute-start.3 = (bf16[112,2048]{1,0:T(8,128)(2,1)}, bf16[112,2048]{1,0:T(8,128)(2,1)S(1)}, u32[]{:S(2)}, u32[]{:S(2)}) collective-permute-start(bf16[112,2048]{1,0:T(8,128)(2,1)} %bitcast.26), channel_id=1, source_target_pairs={{8,24},{24,8},{9,25},{25,9},{10,26},{26,10},{11,27},{27,11},{12,28... | collective-permute-start | bytes 1376264 | tf_op jit(solution)/shard_map/ppermute | solution.py:203
  6.4 1.1 %pad_maximum_fusion = bf16[112,2560]{1,0:T(8,128)(2,1)S(1)} fusion(bf16[112,512]{1,0:T(8,128)(2,1)} %bitcast.21, bf16[112,2048]{1,0:T(8,128)(2,1)} %bitcast.17), kind=kLoop, calls=%fused_computation | loop fusion | flops 1146880 | bytes 1146880 | tf_op jit(solution)/shard_map/concatenate | solution.py:207
  7.5 6.0 %collective-permute-start = (bf16[112,2560]{1,0:T(8,128)(2,1)S(1)}, bf16[112,2560]{1,0:T(8,128)(2,1)S(1)}, u32[]{:S(2)}, u32[]{:S(2)}) collective-permute-start(bf16[112,2560]{1,0:T(8,128)(2,1)S(1)} %pad_maximum_fusion), channel_id=1, source_target_pairs={{0,8},{8,16},{16,24},{24,0},{1,9},{9,17},{17,25},{25,1},{2,10},{10... | collective-permute-start | bytes 1720328 | tf_op jit(solution)/shard_map/ppermute | solution.py:203
  13.6 0.0 collective-permute-done.1.side_ref
  13.6 0.0 copy-start.6
  13.6 0.6 %copy-done.6 = f32[4,128]{1,0:T(4,128)} copy-done((f32[4,128]{1,0:T(4,128)}, f32[4,128]{1,0:T(4,128)S(1)}, u32[]{:S(2)}) %copy-start.6) | copy-done | bytes 2072
  14.2 3.5 %backward.2 = (bf16[112,2560]{1,0:T(8,128)(2,1)}, f32[2,128]{1,0:T(2,128)}) custom-call(bf16[112,2048]{1,0:T(8,128)(2,1)} %bitcast.27, bf16[112,512]{1,0:T(8,128)(2,1)} %bitcast.31, bf16[112,2048]{1,0:T(8,128)(2,1)} %bitcast.18, f32[4,128]{1,0:T(4,128)} %copy-done.6, s32[4,112]{1,0:T(4,128)} %bitcast.22), custom_call_target="tpu_custom_call" | custom-call | flops 68719476736 | bytes 1024 | tf_op jit(solution)/shard_map/backward/pallas_call | solution.py:143
  17.7 1.4 %collective-permute-start.2 = (bf16[112,2560]{1,0:T(8,128)(2,1)}, bf16[112,2560]{1,0:T(8,128)(2,1)S(1)}, u32[]{:S(2)}, u32[]{:S(2)}) collective-permute-start(bf16[112,2560]{1,0:T(8,128)(2,1)} %get-tuple-element.14), channel_id=1, source_target_pairs={{0,24},{16,8},{1,25},{17,9},{2,26},{18,10},{3,27},{19,11},{4,28},{... | collective-permute-start | bytes 1720328 | tf_op jit(solution)/shard_map/ppermute | solution.py:203
  19.1 0.0 collective-permute-done.4.kv_ref
  19.1 0.0 copy-start.5
  19.1 0.0 collective-permute-done.3.q_ref
  19.1 0.0 copy-start.4
  19.1 7.9 %collective-permute-done.packed_ref.rest_0_ = bf16[112,2560]{1,0:T(8,128)(2,1)S(1)} collective-permute-done((bf16[112,2560]{1,0:T(8,128)(2,1)S(1)}, bf16[112,2560]{1,0:T(8,128)(2,1)S(1)}, u32[]{:S(2)}, u32[]{:S(2)}) %collective-permute-start) | collective-permute-done | bytes 573472 | tf_op jit(solution)/shard_map/ppermute | solution.py:203
  27.0 0.0 copy-start
  27.0 0.0 copy-done.5
  27.0 0.0 copy-done.4
  27.0 0.8 %copy-done = bf16[112,2560]{1,0:T(8,128)(2,1)} copy-done((bf16[112,2560]{1,0:T(8,128)(2,1)}, bf16[112,2560]{1,0:T(8,128)(2,1)S(1)}, u32[]{:S(2)}) %copy-start) | copy-done | bytes 573464
  27.8 0.0 copy-start.7
  27.8 3.5 %backward.3 = (bf16[112,2560]{1,0:T(8,128)(2,1)}, f32[2,128]{1,0:T(2,128)}) custom-call(bf16[112,2048]{1,0:T(8,128)(2,1)} %copy-done.4, bf16[112,512]{1,0:T(8,128)(2,1)} %copy-done.5, bf16[112,2048]{1,0:T(8,128)(2,1)} %bitcast.19, f32[4,128]{1,0:T(4,128)} %copy-done.6, s32[4,112]{1,0:T(4,128)} %bitcast.23, bf16[112,2560]{1,0:T(8,128)(2,1)} %copy-done, ...), custom_call_target="tpu_custom_call" | custom-call | flops 1024 | bytes 1024 | tf_op jit(solution)/shard_map/backward/pallas_call | solution.py:143
  31.4 1.3 %collective-permute-start.5 = (bf16[112,2560]{1,0:T(8,128)(2,1)}, bf16[112,2560]{1,0:T(8,128)(2,1)S(1)}, u32[]{:S(2)}, u32[]{:S(2)}) collective-permute-start(bf16[112,2560]{1,0:T(8,128)(2,1)} %get-tuple-element.16), channel_id=1, source_target_pairs={{8,0},{24,16},{9,1},{25,17},{10,2},{26,18},{11,3},{27,19},{12,4},{... | collective-permute-start | bytes 1720328 | tf_op jit(solution)/shard_map/ppermute | solution.py:203
  32.6 1.7 %collective-permute-start.6 = (bf16[112,2560]{1,0:T(8,128)(2,1)}, bf16[112,2560]{1,0:T(8,128)(2,1)S(1)}, u32[]{:S(2)}, u32[]{:S(2)}) collective-permute-start(bf16[112,2560]{1,0:T(8,128)(2,1)} %copy-done), channel_id=1, source_target_pairs={{0,0},{8,24},{16,16},{24,8},{1,1},{9,25},{17,17},{25,9},{2,2},{10,... | collective-permute-start | bytes 1720328 | tf_op jit(solution)/shard_map/ppermute | solution.py:203
  34.4 0.0 copy-done.7
  34.4 0.1 collective-permute-start.7
  34.4 1.1 %collective-permute-done.7 = f32[2,128]{1,0:T(2,128)S(1)} collective-permute-done((f32[2,128]{1,0:T(2,128)S(1)}, f32[2,128]{1,0:T(2,128)S(1)}, u32[]{:S(2)}, u32[]{:S(2)}) %collective-permute-start.7) | collective-permute-done | bytes 1056 | tf_op jit(solution)/shard_map/ppermute | solution.py:227
  35.6 1.6 %collective-permute-start.8 = (f32[2,128]{1,0:T(2,128)S(1)}, f32[2,128]{1,0:T(2,128)S(1)}, u32[]{:S(2)}, u32[]{:S(2)}) collective-permute-start(f32[2,128]{1,0:T(2,128)S(1)} %add.9), channel_id=1, source_target_pairs={{0,2},{1,3},{2,0},{3,1},{4,6},{5,7},{6,4},{7,5},{8,10},{9,11},{10,... | collective-permute-start | bytes 3080 | tf_op jit(solution)/shard_map/ppermute | solution.py:227
  37.2 2.0 %collective-permute-done.8 = f32[2,128]{1,0:T(2,128)S(1)} collective-permute-done((f32[2,128]{1,0:T(2,128)S(1)}, f32[2,128]{1,0:T(2,128)S(1)}, u32[]{:S(2)}, u32[]{:S(2)}) %collective-permute-start.8) | collective-permute-done | bytes 1056 | tf_op jit(solution)/shard_map/ppermute | solution.py:227
  39.2 7.0 %collective-permute-start.10 = (f32[2,128]{1,0:T(2,128)S(1)}, f32[2,128]{1,0:T(2,128)S(1)}, u32[]{:S(2)}, u32[]{:S(2)}) collective-permute-start(f32[2,128]{1,0:T(2,128)S(1)} %add.10), channel_id=1, source_target_pairs={{0,28},{1,29},{2,30},{3,31},{4,24},{5,25},{6,26},{7,27},{8,4},{9,5... | collective-permute-start | bytes 3080 | tf_op jit(solution)/shard_map/ppermute | solution.py:230
  46.1 0.0 collective-permute-start.9
  46.1 2.9 %forward.1 = bf16[112,2048]{1,0:T(8,128)(2,1)} custom-call(bf16[112,2560]{1,0:T(8,128)(2,1)} %copy-done, f32[4,128]{1,0:T(4,128)} %copy-done.6, s32[4,112]{1,0:T(4,128)} %bitcast.24), custom_call_target="tpu_custom_call" | custom-call | flops 1024 | bytes 1024 | tf_op jit(solution)/shard_map/forward/pallas_call | solution.py:133
  49.1 0.0 collective-permute-done.10
  49.1 0.6 %collective-permute-done.9 = f32[2,128]{1,0:T(2,128)S(1)} collective-permute-done((f32[2,128]{1,0:T(2,128)S(1)}, f32[2,128]{1,0:T(2,128)S(1)}, u32[]{:S(2)}, u32[]{:S(2)}) %collective-permute-start.9) | collective-permute-done | bytes 1056 | tf_op jit(solution)/shard_map/ppermute | solution.py:230
  49.7 0.6 %multiply_bitcast_fusion = f32[1,2,128]{2,1,0:T(2,128)} fusion(f32[2,128]{1,0:T(2,128)S(1)} %collective-permute-done.9, f32[2,128]{1,0:T(2,128)S(1)} %collective-permute-done.10), kind=kLoop, calls=%fused_computation.2 | loop fusion | flops 512 | bytes 3072 | tf_op jit(solution)/shard_map/broadcast_in_dim | solution.py:251
  50.3 0.0 collective-permute-done.2.first_ref
  50.3 0.0 copy-start.1
  50.3 0.0 collective-permute-done.5.second_ref
  50.3 0.0 copy-start.2
  50.3 0.0 collective-permute-done.6.third_ref
  50.3 0.0 copy-start.3
  50.3 0.8 %copy-done.1 = bf16[112,2560]{1,0:T(8,128)(2,1)} copy-done((bf16[112,2560]{1,0:T(8,128)(2,1)}, bf16[112,2560]{1,0:T(8,128)(2,1)S(1)}, u32[]{:S(2)}) %copy-start.1) | copy-done | bytes 573464
  51.1 0.2 copy-done.2
  51.4 0.1 copy-done.3
  51.5 2.4 %unpack.1 = (bf16[112,2048]{1,0:T(8,128)(2,1)}, bf16[112,512]{1,0:T(8,128)(2,1)}, bf16[112,2048]{1,0:T(8,128)(2,1)}, bf16[112,512]{1,0:T(8,128)(2,1)}) custom-call(s32[1]{0:T(128)} %bitcast.6.choice_ref, bf16[112,2560]{1,0:T(8,128)(2,1)} %copy-done.1, bf16[112,2560]{1,0:T(8,128)(2,1)} %copy-done.2, bf16[112,2560]{1,0:T(8,128)(2,1)} %copy-done.3), custom_call_target="tpu_custom_call" | custom-call | flops 1024 | bytes 1024 | tf_op jit(solution)/shard_map/unpack/pallas_call | solution.py:178
  (3 shorter events, 0.0 us)
Async XLA Ops:
  2.1 11.5 %collective-permute-start.1 = (f32[4,128]{1,0:T(4,128)S(1)}, f32[4,128]{1,0:T(4,128)S(1)}, u32[]{:S(2)}, u32[]{:S(2)}) collective-permute-start(f32[4,128]{1,0:T(4,128)S(1)} %pad_maximum_fusion.1), channel_id=1, source_target_pairs={{0,8},{8,16},{16,24},{24,0},{1,9},{9,17},{17,25},{25,1},{2,10},{10... | collective-permute-start | bytes 6152 | tf_op jit(solution)/shard_map/ppermute | solution.py:203
  5.1 14.0 %collective-permute-start.4 = (bf16[112,512]{1,0:T(8,128)(2,1)}, bf16[112,512]{1,0:T(8,128)(2,1)S(1)}, u32[]{:S(2)}, u32[]{:S(2)}) collective-permute-start(bf16[112,512]{1,0:T(8,128)(2,1)} %bitcast.30), channel_id=1, source_target_pairs={{8,24},{24,8},{9,25},{25,9},{10,26},{26,10},{11,27},{27,11},{12,28... | collective-permute-start | bytes 344072 | tf_op jit(solution)/shard_map/ppermute | solution.py:203
  5.7 13.4 %collective-permute-start.3 = (bf16[112,2048]{1,0:T(8,128)(2,1)}, bf16[112,2048]{1,0:T(8,128)(2,1)S(1)}, u32[]{:S(2)}, u32[]{:S(2)}) collective-permute-start(bf16[112,2048]{1,0:T(8,128)(2,1)} %bitcast.26), channel_id=1, source_target_pairs={{8,24},{24,8},{9,25},{25,9},{10,26},{26,10},{11,27},{27,11},{12,28... | collective-permute-start | bytes 1376264 | tf_op jit(solution)/shard_map/ppermute | solution.py:203
  7.5 19.5 %collective-permute-start = (bf16[112,2560]{1,0:T(8,128)(2,1)S(1)}, bf16[112,2560]{1,0:T(8,128)(2,1)S(1)}, u32[]{:S(2)}, u32[]{:S(2)}) collective-permute-start(bf16[112,2560]{1,0:T(8,128)(2,1)S(1)} %pad_maximum_fusion), channel_id=1, source_target_pairs={{0,8},{8,16},{16,24},{24,0},{1,9},{9,17},{17,25},{25,1},{2,10},{10... | collective-permute-start | bytes 1720328 | tf_op jit(solution)/shard_map/ppermute | solution.py:203
  13.6 0.6 %copy-start.6 = (f32[4,128]{1,0:T(4,128)}, f32[4,128]{1,0:T(4,128)S(1)}, u32[]{:S(2)}) copy-start(f32[4,128]{1,0:T(4,128)S(1)} %collective-permute-done.1.side_ref) | copy-start | bytes 6148
  17.7 32.6 %collective-permute-start.2 = (bf16[112,2560]{1,0:T(8,128)(2,1)}, bf16[112,2560]{1,0:T(8,128)(2,1)S(1)}, u32[]{:S(2)}, u32[]{:S(2)}) collective-permute-start(bf16[112,2560]{1,0:T(8,128)(2,1)} %get-tuple-element.14), channel_id=1, source_target_pairs={{0,24},{16,8},{1,25},{17,9},{2,26},{18,10},{3,27},{19,11},{4,28},{... | collective-permute-start | bytes 1720328 | tf_op jit(solution)/shard_map/ppermute | solution.py:203
  19.1 7.9 %copy-start.5 = (bf16[112,512]{1,0:T(8,128)(2,1)}, bf16[112,512]{1,0:T(8,128)(2,1)S(1)}, u32[]{:S(2)}) copy-start(bf16[112,512]{1,0:T(8,128)(2,1)S(1)} %collective-permute-done.4.kv_ref) | copy-start | bytes 344068
  19.1 7.9 %copy-start.4 = (bf16[112,2048]{1,0:T(8,128)(2,1)}, bf16[112,2048]{1,0:T(8,128)(2,1)S(1)}, u32[]{:S(2)}) copy-start(bf16[112,2048]{1,0:T(8,128)(2,1)S(1)} %collective-permute-done.3.q_ref) | copy-start | bytes 1376260
  27.0 0.8 %copy-start = (bf16[112,2560]{1,0:T(8,128)(2,1)}, bf16[112,2560]{1,0:T(8,128)(2,1)S(1)}, u32[]{:S(2)}) copy-start(bf16[112,2560]{1,0:T(8,128)(2,1)S(1)} %collective-permute-done.packed_ref.rest_0_) | copy-start | bytes 1720324
  27.8 6.5 %copy-start.7 = (f32[2,128]{1,0:T(2,128)S(1)}, f32[2,128]{1,0:T(2,128)}, u32[]{:S(2)}) copy-start(f32[2,128]{1,0:T(2,128)} %get-tuple-element.15.rest_1_) | copy-start | bytes 3076
  31.4 18.9 %collective-permute-start.5 = (bf16[112,2560]{1,0:T(8,128)(2,1)}, bf16[112,2560]{1,0:T(8,128)(2,1)S(1)}, u32[]{:S(2)}, u32[]{:S(2)}) collective-permute-start(bf16[112,2560]{1,0:T(8,128)(2,1)} %get-tuple-element.16), channel_id=1, source_target_pairs={{8,0},{24,16},{9,1},{25,17},{10,2},{26,18},{11,3},{27,19},{12,4},{... | collective-permute-start | bytes 1720328 | tf_op jit(solution)/shard_map/ppermute | solution.py:203
  32.6 17.7 %collective-permute-start.6 = (bf16[112,2560]{1,0:T(8,128)(2,1)}, bf16[112,2560]{1,0:T(8,128)(2,1)S(1)}, u32[]{:S(2)}, u32[]{:S(2)}) collective-permute-start(bf16[112,2560]{1,0:T(8,128)(2,1)} %copy-done), channel_id=1, source_target_pairs={{0,0},{8,24},{16,16},{24,8},{1,1},{9,25},{17,17},{25,9},{2,2},{10,... | collective-permute-start | bytes 1720328 | tf_op jit(solution)/shard_map/ppermute | solution.py:203
  34.4 1.2 %collective-permute-start.7 = (f32[2,128]{1,0:T(2,128)S(1)}, f32[2,128]{1,0:T(2,128)S(1)}, u32[]{:S(2)}, u32[]{:S(2)}) collective-permute-start(f32[2,128]{1,0:T(2,128)S(1)} %broadcast_select_fusion), channel_id=1, source_target_pairs={{0,1},{1,0},{2,3},{3,2},{4,5},{5,4},{6,7},{7,6},{8,9},{9,8},{10,11... | collective-permute-start | bytes 3080 | tf_op jit(solution)/shard_map/ppermute | solution.py:227
  35.6 3.6 %collective-permute-start.8 = (f32[2,128]{1,0:T(2,128)S(1)}, f32[2,128]{1,0:T(2,128)S(1)}, u32[]{:S(2)}, u32[]{:S(2)}) collective-permute-start(f32[2,128]{1,0:T(2,128)S(1)} %add.9), channel_id=1, source_target_pairs={{0,2},{1,3},{2,0},{3,1},{4,6},{5,7},{6,4},{7,5},{8,10},{9,11},{10,... | collective-permute-start | bytes 3080 | tf_op jit(solution)/shard_map/ppermute | solution.py:227
  39.2 9.9 %collective-permute-start.10 = (f32[2,128]{1,0:T(2,128)S(1)}, f32[2,128]{1,0:T(2,128)S(1)}, u32[]{:S(2)}, u32[]{:S(2)}) collective-permute-start(f32[2,128]{1,0:T(2,128)S(1)} %add.10), channel_id=1, source_target_pairs={{0,28},{1,29},{2,30},{3,31},{4,24},{5,25},{6,26},{7,27},{8,4},{9,5... | collective-permute-start | bytes 3080 | tf_op jit(solution)/shard_map/ppermute | solution.py:230
  46.1 3.6 %collective-permute-start.9 = (f32[2,128]{1,0:T(2,128)S(1)}, f32[2,128]{1,0:T(2,128)S(1)}, u32[]{:S(2)}, u32[]{:S(2)}) collective-permute-start(f32[2,128]{1,0:T(2,128)S(1)} %add.10), channel_id=1, source_target_pairs={{0,24},{1,25},{2,26},{3,27},{4,28},{5,29},{6,30},{7,31},{8,0},{9,1... | collective-permute-start | bytes 3080 | tf_op jit(solution)/shard_map/ppermute | solution.py:230
  50.3 0.8 %copy-start.1 = (bf16[112,2560]{1,0:T(8,128)(2,1)}, bf16[112,2560]{1,0:T(8,128)(2,1)S(1)}, u32[]{:S(2)}) copy-start(bf16[112,2560]{1,0:T(8,128)(2,1)S(1)} %collective-permute-done.2.first_ref) | copy-start | bytes 1720324
  50.3 1.1 %copy-start.2 = (bf16[112,2560]{1,0:T(8,128)(2,1)}, bf16[112,2560]{1,0:T(8,128)(2,1)S(1)}, u32[]{:S(2)}) copy-start(bf16[112,2560]{1,0:T(8,128)(2,1)S(1)} %collective-permute-done.5.second_ref) | copy-start | bytes 1720324
  50.3 1.2 %copy-start.3 = (bf16[112,2560]{1,0:T(8,128)(2,1)}, bf16[112,2560]{1,0:T(8,128)(2,1)S(1)}, u32[]{:S(2)}) copy-start(bf16[112,2560]{1,0:T(8,128)(2,1)S(1)} %collective-permute-done.6.third_ref) | copy-start | bytes 1720324

commit v3 on v2

v3 whole, which is shorter than its diff:
```python
import functools
import math

import jax
import jax.numpy as jnp
from jax import lax
from jax.experimental import pallas as pl
from jax.experimental.pallas import tpu as pltpu
from jax.sharding import PartitionSpec as P

HEAD_SIZE = 128
EPSILON = 1e-06
SCORE_SCALE = 1.0 / math.sqrt(HEAD_SIZE)
EXP2_SCALE = SCORE_SCALE * math.log2(math.e)

VMEM_LIMIT = 16 << 20
NT = (((1,), (1,)), ((), ()))
TN = (((0,), (0,)), ((), ()))
NN = (((1,), (0,)), ((), ()))


def dot(a, b, dims):
    return lax.dot_general(a, b, dims, preferred_element_type=jnp.float32)


def head(ref, index):
    return ref[:, index * HEAD_SIZE : (index + 1) * HEAD_SIZE]


def stacked(ref, first, count):
    return jnp.concatenate([head(ref, first + i) for i in range(count)], axis=0)


def allowed_pairs(segment_ref, chosen, copies):
    micro, tokens = segment_ref.shape
    ids = segment_ref[...].astype(jnp.float32)
    number = lax.broadcasted_iota(jnp.int32, (micro, tokens), 0).astype(jnp.float32)
    row = jnp.sum(jnp.where(number == chosen[:, :tokens], ids, 0.0), axis=0, keepdims=True)
    keys_at = lax.broadcasted_iota(jnp.int32, (tokens, tokens), 0)
    queries_at = lax.broadcasted_iota(jnp.int32, (tokens, tokens), 1)
    column = jnp.sum(jnp.where(keys_at == queries_at, row, 0.0), axis=1, keepdims=True)
    allowed = ((keys_at <= queries_at) & (column == row)).astype(jnp.float32)
    return jnp.concatenate([allowed] * copies, axis=1) > 0.5


def side_rows(tile):
    parts = tile.astype(jnp.float32)
    return parts[0:4] + parts[4:8] + parts[8:12]


def pack_kernel(q_ref, kv_ref, gains_ref, plan_ref, packed_ref):
    q_width, kv_width = q_ref.shape[1], kv_ref.shape[1]
    packed_ref[:, :q_width] = q_ref[...]
    packed_ref[:, q_width : q_width + kv_width] = kv_ref[...]
    numbers = [jnp.full((1, HEAD_SIZE), plan_ref[0, i]).astype(jnp.float32) for i in range(2)]
    rest = jnp.concatenate([gains_ref[...]] + numbers, axis=0)
    parts = []
    for _ in range(3):
        part = rest.astype(jnp.bfloat16).astype(jnp.float32)
        rest = rest - part
        parts.append(part)
    parts = jnp.concatenate(parts + [jnp.zeros_like(rest)], axis=0)
    empty = jnp.zeros((q_ref.shape[0] - 16, HEAD_SIZE), jnp.bfloat16)
    packed_ref[0:16, q_width + kv_width :] = parts.astype(jnp.bfloat16)
    packed_ref[16:, q_width + kv_width :] = empty


def normalized(values):
    wide = values.astype(jnp.float32)
    factor = lax.rsqrt(jnp.mean(wide * wide, axis=1, keepdims=True) + EPSILON)
    return wide * factor, factor


def probabilities(key, query, allowed):
    scores = dot(key, query, NT)
    weights = jnp.where(allowed, jnp.exp2(scores * EXP2_SCALE), 0.0)
    return weights * (1.0 / jnp.sum(weights, axis=0, keepdims=True))


def forward_kernel(packed_ref, segment_ref, out_ref):
    side = side_rows(packed_ref[0:16, packed_ref.shape[1] - HEAD_SIZE :])
    tokens = packed_ref.shape[0]
    heads = out_ref.shape[1] // HEAD_SIZE
    kv_heads = (packed_ref.shape[1] // HEAD_SIZE - heads) // 2
    per_kv = heads // kv_heads
    allowed = allowed_pairs(segment_ref, side[2:3], per_kv)
    for g in range(kv_heads):
        key_hat, _ = normalized(head(packed_ref, heads + g))
        key = (key_hat * side[1:2]).astype(jnp.bfloat16)
        value = head(packed_ref, heads + kv_heads + g)
        query_hat, _ = normalized(stacked(packed_ref, g * per_kv, per_kv))
        query = (query_hat * side[0:1]).astype(jnp.bfloat16)
        probs = probabilities(key, query, allowed).astype(jnp.bfloat16)
        out = dot(probs, value, TN).astype(jnp.bfloat16)
        for i in range(per_kv):
            h = g * per_kv + i
            out_ref[:, h * HEAD_SIZE : (h + 1) * HEAD_SIZE] = out[i * tokens : (i + 1) * tokens]


def norm_back(hat, factor, scaled_gain, d_normed):
    terms = d_normed * hat
    inner = jnp.sum(terms * scaled_gain, axis=1, keepdims=True) * (1.0 / HEAD_SIZE)
    return (d_normed * scaled_gain - hat * inner) * factor, terms


def summed_rows(terms):
    return jnp.sum(terms.reshape(-1, 8, terms.shape[1]), axis=0)


def backward_kernel(packed_ref, up_ref, side_ref, segment_ref, grad_ref, gain_ref):
    side = side_rows(side_ref[...])
    tokens = packed_ref.shape[0]
    heads = up_ref.shape[1] // HEAD_SIZE
    kv_heads = (packed_ref.shape[1] // HEAD_SIZE - heads) // 2
    per_kv = heads // kv_heads
    allowed = allowed_pairs(segment_ref, side[3:4], per_kv)
    q_gain, k_gain = side[0:1], side[1:2]
    q_terms = k_terms = 0.0
    for g in range(kv_heads):
        key_hat, key_factor = normalized(head(packed_ref, heads + g))
        key = (key_hat * k_gain).astype(jnp.bfloat16)
        value = head(packed_ref, heads + kv_heads + g)
        query_hat, query_factor = normalized(stacked(packed_ref, g * per_kv, per_kv))
        query = (query_hat * q_gain).astype(jnp.bfloat16)
        upstream = stacked(up_ref, g * per_kv, per_kv)
        probs = probabilities(key, query, allowed)
        d_probs = dot(value, upstream, NT)
        d_value = dot(probs.astype(jnp.bfloat16), upstream, NN)
        centre = jnp.sum(probs * d_probs, axis=0, keepdims=True)
        d_scores = (probs * (d_probs - centre)).astype(jnp.bfloat16)
        d_key = dot(d_scores, query, NN)
        d_query, terms = norm_back(
            query_hat, query_factor, q_gain * SCORE_SCALE, dot(d_scores, key, TN)
        )
        q_terms += summed_rows(terms)
        d_query = d_query.astype(jnp.bfloat16)
        for i in range(per_kv):
            h = g * per_kv + i
            grad_ref[:, h * HEAD_SIZE : (h + 1) * HEAD_SIZE] = d_query[
                i * tokens : (i + 1) * tokens
            ]
        d_key, terms = norm_back(key_hat, key_factor, k_gain * SCORE_SCALE, d_key)
        k_terms += summed_rows(terms)
        at = (heads + g) * HEAD_SIZE
        grad_ref[:, at : at + HEAD_SIZE] = d_key.astype(jnp.bfloat16)
        at = (heads + kv_heads + g) * HEAD_SIZE
        grad_ref[:, at : at + HEAD_SIZE] = d_value.astype(jnp.bfloat16)
    gain_ref[0:1, :] = jnp.sum(q_terms, axis=0, keepdims=True) * SCORE_SCALE
    gain_ref[1:2, :] = jnp.sum(k_terms, axis=0, keepdims=True) * SCORE_SCALE


def cost(work):
    return pl.CostEstimate(flops=work, bytes_accessed=1024, transcendentals=0)


VMEM = pl.BlockSpec(memory_space=pltpu.VMEM)


def side_tile(fresh):
    at = fresh.shape[1] // HEAD_SIZE - 1
    return pl.BlockSpec((16, HEAD_SIZE), lambda step: (0, at))


def pack(q, kv, gains, plan):
    return pl.pallas_call(
        pack_kernel,
        out_shape=jax.ShapeDtypeStruct((q.shape[0], q.shape[1] + kv.shape[1] + HEAD_SIZE), q.dtype),
        in_specs=[VMEM] * 3 + [pl.BlockSpec(memory_space=pltpu.SMEM)],
        out_specs=VMEM,
        cost_estimate=cost(1024),
        name="pack",
    )(q, kv, gains, plan)


def forward(fresh, q_width, segments):
    return pl.pallas_call(
        forward_kernel,
        out_shape=jax.ShapeDtypeStruct((fresh.shape[0], q_width), fresh.dtype),
        in_specs=[VMEM, VMEM],
        out_specs=VMEM,
        cost_estimate=cost(1024),
        compiler_params=pltpu.CompilerParams(vmem_limit_bytes=VMEM_LIMIT),
        name="forward",
    )(fresh, segments)


def backward(packed, upstream, fresh, segments):
    return pl.pallas_call(
        backward_kernel,
        out_shape=(
            jax.ShapeDtypeStruct(packed.shape, packed.dtype),
            jax.ShapeDtypeStruct((2, HEAD_SIZE), jnp.float32),
        ),
        grid=(1,),
        in_specs=[VMEM, VMEM, side_tile(fresh), VMEM],
        out_specs=(VMEM, VMEM),
        cost_estimate=cost(1024),
        compiler_params=pltpu.CompilerParams(vmem_limit_bytes=VMEM_LIMIT),
        name="backward",
    )(packed, upstream, fresh, segments)


def unpack_kernel(packed_ref, q_ref, kv_ref):
    q_width = q_ref.shape[1]
    q_ref[...] = packed_ref[:, :q_width]
    kv_ref[...] = packed_ref[:, q_width : q_width + kv_ref.shape[1]]


def unpack(packed, widths):
    return pl.pallas_call(
        unpack_kernel,
        out_shape=[
            jax.ShapeDtypeStruct((packed.shape[0], width), packed.dtype) for width in widths
        ],
        cost_estimate=cost(1024),
        compiler_params=pltpu.CompilerParams(vmem_limit_bytes=VMEM_LIMIT),
        name="unpack",
    )(packed)


def local(
    fresh_q, current_key_value, held_q, retained_key_value, cotangent, norm_gains, plan, segment_ids
):
    sections, replicas = lax.axis_size("section"), lax.axis_size("dp")
    opposite = [(i, -i % sections) for i in range(sections)]
    up = [(i, (i + 1) % sections) for i in range(sections)]
    down = [(i, (i - 1) % sections) for i in range(sections)]
    segments = segment_ids[0]
    widths = fresh_q.shape[2], current_key_value.shape[2]

    def hop(value, pairs):
        return lax.ppermute(value, "section", pairs)

    fresh = hop(pack(fresh_q[0], current_key_value[0], norm_gains[0], plan), up)
    held = hop(jnp.concatenate([held_q[0], retained_key_value[0]], axis=1), opposite)
    stored = hop(fresh, opposite)
    grad, gain = backward(held, cotangent[0], fresh, segments)
    grad = hop(grad, down)
    attention_out = forward(fresh, widths[0], segments)

    step = 1
    while 2 * step < replicas:
        gain = gain + lax.ppermute(gain, "dp", [(i, i ^ step) for i in range(replicas)])
        step *= 2
    halves = [
        lax.ppermute(
            gain,
            ("section", "dp"),
            [
                (i * replicas + j, (i - 1) % sections * replicas + (j ^ other))
                for i in range(sections)
                for j in range(replicas)
            ],
        )
        for other in (0, step)
    ]
    gain = (halves[0] + halves[1]) * (1.0 / replicas)
    stored_q, stored_kv = unpack(stored, widths)
    grad_q, grad_kv = unpack(grad, widths)
    return (
        attention_out[None],
        stored_q[None],
        stored_kv[None],
        grad_q[None],
        grad_kv[None],
        gain[None],
    )


def solution(mesh):
    rows = P("section", "dp", None)
    gains = P("section", None, None)
    return jax.shard_map(
        local,
        mesh=mesh,
        in_specs=(rows, rows, rows, rows, rows, gains, P("section", None), P("dp", None, None)),
        out_specs=(rows, rows, rows, rows, rows, gains),
        check_vma=False,
    )
```

time: 54.3 us -> 47.9 us (0.88)
  the two profiles are of different devices: /device:TPU:0 before, /device:TPU:2 now
where the time goes in v3:
time: 47.9 us; the launch traced here: 47.7 us
  waiting for transfers between devices  26.7 us (56%)
  starting transfers between devices  12.7 us (27%)
  Pallas kernels  6.97 us (15%)
  between operations  0.73 us (2%)
  other arithmetic  0.61 us (1%)
    ppermute x4, waiting for transfers between devices, hop(): return lax.ppermute(value, 'section', pairs)  19.6 us
    ppermute x4, starting transfers between devices, hop(): return lax.ppermute(value, 'section', pairs)  7.06 us
    ppermute x2, waiting for transfers between devices, local(): lax.ppermute(gain, ('section', 'dp'), [(i * replicas + j, (i - 1) % secti...  4.02 us
    ppermute x2, starting transfers between devices, local(): lax.ppermute(gain, ('section', 'dp'), [(i * replicas + j, (i - 1) % secti...  3.99 us
    ppermute x2, waiting for transfers between devices, local(): lax.ppermute(gain, 'dp', [(i, i ^ step) for i in range(replicas)])  3.12 us
    pallas_call x1, Pallas kernels, pack(): pl.pallas_call(pack_kernel, out_shape=jax.ShapeDtypeStruct((q.shape[0], q...  2.01 us
    pallas_call x1, Pallas kernels, forward(): pl.pallas_call(forward_kernel, out_shape=jax.ShapeDtypeStruct((fresh.shap...  1.85 us
    pallas_call x2, Pallas kernels, unpack(): pl.pallas_call(unpack_kernel, out_shape=[jax.ShapeDtypeStruct((packed.sha...  1.67 us
  transfers between devices with their start and end apart: 8, of which 6 were waited for; matrix products, arithmetic and copies ran while one was open for 1% of the time, Pallas kernels for 9%

profile of v3, /device:TPU:2, one launch (start us, length us, event | category | flops | bytes accessed | tf_op | source)
XLA Modules:
  0.0 47.7 jit_solution(2802165311443843090)
XLA Ops:
  0.6 0.0 copy-start.3
  0.6 0.0 copy-start.2
  0.7 2.0 %pack.1 = bf16[112,2688]{1,0:T(8,128)(2,1)} custom-call(bf16[112,2048]{1,0:T(8,128)(2,1)} %bitcast.17, bf16[112,512]{1,0:T(8,128)(2,1)} %bitcast.20, f32[2,128]{1,0:T(2,128)} %bitcast.22, s32[1,2]{1,0:T(1,128)} %plan_ref.1), custom_call_target="tpu_custom_call" | custom-call | flops 1024 | bytes 1024 | tf_op jit(solution)/shard_map/pack/pallas_call | solution.py:165
  2.7 0.0 copy-start
  2.7 0.0 copy-start.1
  2.7 1.5 %collective-permute-start = (bf16[112,2688]{1,0:T(8,128)(2,1)}, bf16[112,2688]{1,0:T(8,128)(2,1)S(1)}, u32[]{:S(2)}, u32[]{:S(2)}) collective-permute-start(bf16[112,2688]{1,0:T(8,128)(2,1)} %pack.1), channel_id=1, source_target_pairs={{0,8},{8,16},{16,24},{24,0},{1,9},{9,17},{17,25},{25,1},{2,10},{10... | collective-permute-start | bytes 1806344 | tf_op jit(solution)/shard_map/ppermute | solution.py:232
  4.2 0.0 copy-done.3
  4.2 0.0 copy-done.2
  4.2 2.1 %collective-permute-start.2 = (bf16[112,2560]{1,0:T(8,128)(2,1)S(1)}, bf16[112,2560]{1,0:T(8,128)(2,1)S(1)}, u32[]{:S(2)}, u32[]{:S(2)}) collective-permute-start(bf16[112,2560]{1,0:T(8,128)(2,1)S(1)} %pad_maximum_fusion), channel_id=1, source_target_pairs={{0,0},{8,24},{16,16},{24,8},{1,1},{9,25},{17,17},{25,9},{2,2},{10,... | collective-permute-start | bytes 1720328 | tf_op jit(solution)/shard_map/ppermute | solution.py:232
  6.3 11.9 %collective-permute-done.packed_ref.side_ref = bf16[112,2688]{1,0:T(8,128)(2,1)S(1)} collective-permute-done((bf16[112,2688]{1,0:T(8,128)(2,1)}, bf16[112,2688]{1,0:T(8,128)(2,1)S(1)}, u32[]{:S(2)}, u32[]{:S(2)}) %collective-permute-start) | collective-permute-done | bytes 602144 | tf_op jit(solution)/shard_map/ppermute | solution.py:232
  18.2 3.4 %collective-permute-start.1 = (bf16[112,2688]{1,0:T(8,128)(2,1)S(1)}, bf16[112,2688]{1,0:T(8,128)(2,1)S(1)}, u32[]{:S(2)}, u32[]{:S(2)}) collective-permute-start(bf16[112,2688]{1,0:T(8,128)(2,1)S(1)} %collective-permute-done.packed_ref.side_ref), channel_id=1, source_target_pairs={{0,0},{8,24},{16,16},{24,8},{1,1},{9,25},{17,17},{25,9},{2,2},{10,... | collective-permute-start | bytes 1806344 | tf_op jit(solution)/shard_map/ppermute | solution.py:232
  21.6 0.0 collective-permute-done.2.packed_ref
  21.6 0.0 copy-done
  21.7 0.0 copy-done.1
  21.7 1.4 %backward.1 = (bf16[112,2560]{1,0:T(8,128)(2,1)S(1)}, f32[2,128]{1,0:T(2,128)S(1)}) custom-call(bf16[112,2560]{1,0:T(8,128)(2,1)S(1)} %collective-permute-done.2.packed_ref, bf16[112,2048]{1,0:T(8,128)(2,1)S(1)} %bitcast.14, bf16[112,2688]{1,0:T(8,128)(2,1)S(1)} %collective-permute-done.packed_ref.side_ref, s32[4,112]{1,0:T(4,128)S(1)} %bitcast.15), custom_call_target="tpu_custom_call" | custom-call | flops 1024 | bytes 1024 | tf_op jit(solution)/shard_map/backward/pallas_call | solution.py:188
  23.1 0.1 collective-permute-start.3
  23.2 0.1 collective-permute-start.4
  23.3 1.1 %collective-permute-done.4 = f32[2,128]{1,0:T(2,128)S(1)} collective-permute-done((f32[2,128]{1,0:T(2,128)S(1)}, f32[2,128]{1,0:T(2,128)S(1)}, u32[]{:S(2)}, u32[]{:S(2)}) %collective-permute-start.4) | collective-permute-done | bytes 1056 | tf_op jit(solution)/shard_map/ppermute | solution.py:243
  24.4 1.6 %collective-permute-start.5 = (f32[2,128]{1,0:T(2,128)S(1)}, f32[2,128]{1,0:T(2,128)S(1)}, u32[]{:S(2)}, u32[]{:S(2)}) collective-permute-start(f32[2,128]{1,0:T(2,128)S(1)} %add.9), channel_id=1, source_target_pairs={{0,2},{1,3},{2,0},{3,1},{4,6},{5,7},{6,4},{7,5},{8,10},{9,11},{10,... | collective-permute-start | bytes 3080 | tf_op jit(solution)/shard_map/ppermute | solution.py:243
  26.0 2.0 %collective-permute-done.5 = f32[2,128]{1,0:T(2,128)S(1)} collective-permute-done((f32[2,128]{1,0:T(2,128)S(1)}, f32[2,128]{1,0:T(2,128)S(1)}, u32[]{:S(2)}, u32[]{:S(2)}) %collective-permute-start.5) | collective-permute-done | bytes 1056 | tf_op jit(solution)/shard_map/ppermute | solution.py:243
  28.0 3.9 %collective-permute-start.7 = (f32[2,128]{1,0:T(2,128)S(1)}, f32[2,128]{1,0:T(2,128)S(1)}, u32[]{:S(2)}, u32[]{:S(2)}) collective-permute-start(f32[2,128]{1,0:T(2,128)S(1)} %add.10), channel_id=1, source_target_pairs={{0,28},{1,29},{2,30},{3,31},{4,24},{5,25},{6,26},{7,27},{8,4},{9,5... | collective-permute-start | bytes 3080 | tf_op jit(solution)/shard_map/ppermute | solution.py:246
  31.9 0.1 collective-permute-start.6
  32.0 1.8 %forward.1 = bf16[112,2048]{1,0:T(8,128)(2,1)} custom-call(bf16[112,2688]{1,0:T(8,128)(2,1)S(1)} %collective-permute-done.packed_ref.side_ref, s32[4,112]{1,0:T(4,128)S(1)} %bitcast.16), custom_call_target="tpu_custom_call" | custom-call | flops 1024 | bytes 1024 | tf_op jit(solution)/shard_map/forward/pallas_call | solution.py:176
  33.8 0.6 %collective-permute-done.7 = f32[2,128]{1,0:T(2,128)S(1)} collective-permute-done((f32[2,128]{1,0:T(2,128)S(1)}, f32[2,128]{1,0:T(2,128)S(1)}, u32[]{:S(2)}, u32[]{:S(2)}) %collective-permute-start.7) | collective-permute-done | bytes 1056 | tf_op jit(solution)/shard_map/ppermute | solution.py:246
  34.4 3.4 %collective-permute-done.6 = f32[2,128]{1,0:T(2,128)S(1)} collective-permute-done((f32[2,128]{1,0:T(2,128)S(1)}, f32[2,128]{1,0:T(2,128)S(1)}, u32[]{:S(2)}, u32[]{:S(2)}) %collective-permute-start.6) | collective-permute-done | bytes 1056 | tf_op jit(solution)/shard_map/ppermute | solution.py:246
  37.8 0.6 %multiply_bitcast_fusion = f32[1,2,128]{2,1,0:T(2,128)} fusion(f32[2,128]{1,0:T(2,128)S(1)} %collective-permute-done.6, f32[2,128]{1,0:T(2,128)S(1)} %collective-permute-done.7), kind=kLoop, calls=%fused_computation.1 | loop fusion | flops 512 | bytes 3072 | tf_op jit(solution)/shard_map/broadcast_in_dim | solution.py:266
  38.4 0.0 collective-permute-done.3.packed_ref
  38.4 0.8 %unpack.3 = (bf16[112,2048]{1,0:T(8,128)(2,1)}, bf16[112,512]{1,0:T(8,128)(2,1)}) custom-call(bf16[112,2560]{1,0:T(8,128)(2,1)S(1)} %collective-permute-done.3.packed_ref), custom_call_target="tpu_custom_call" | custom-call | flops 1024 | bytes 1024 | tf_op jit(solution)/shard_map/unpack/pallas_call | solution.py:210
  39.2 7.7 %collective-permute-done.1.packed_ref = bf16[112,2688]{1,0:T(8,128)(2,1)S(1)} collective-permute-done((bf16[112,2688]{1,0:T(8,128)(2,1)S(1)}, bf16[112,2688]{1,0:T(8,128)(2,1)S(1)}, u32[]{:S(2)}, u32[]{:S(2)}) %collective-permute-start.1) | collective-permute-done | bytes 602144 | tf_op jit(solution)/shard_map/ppermute | solution.py:232
  46.9 0.8 %unpack.2 = (bf16[112,2048]{1,0:T(8,128)(2,1)}, bf16[112,512]{1,0:T(8,128)(2,1)}) custom-call(bf16[112,2688]{1,0:T(8,128)(2,1)S(1)} %collective-permute-done.1.packed_ref), custom_call_target="tpu_custom_call" | custom-call | flops 1024 | bytes 1024 | tf_op jit(solution)/shard_map/unpack/pallas_call | solution.py:210
  (3 shorter events, 0.0 us)
Async XLA Ops:
  0.6 3.5 %copy-start.3 = (bf16[1,112,512]{2,1,0:T(8,128)(2,1)S(1)}, bf16[1,112,512]{2,1,0:T(8,128)(2,1)}, u32[]{:S(2)}) copy-start(bf16[1,112,512]{2,1,0:T(8,128)(2,1)} %param.11) | copy-start | bytes 344068
  0.6 3.5 %copy-start.2 = (bf16[1,112,2048]{2,1,0:T(8,128)(2,1)S(1)}, bf16[1,112,2048]{2,1,0:T(8,128)(2,1)}, u32[]{:S(2)}) copy-start(bf16[1,112,2048]{2,1,0:T(8,128)(2,1)} %param.10) | copy-start | bytes 1376260
  2.7 19.0 %copy-start = (bf16[1,112,2048]{2,1,0:T(8,128)(2,1)S(1)}, bf16[1,112,2048]{2,1,0:T(8,128)(2,1)}, u32[]{:S(2)}) copy-start(bf16[1,112,2048]{2,1,0:T(8,128)(2,1)} %param.12) | copy-start | bytes 1376260
  2.7 19.0 %copy-start.1 = (s32[1,4,112]{2,1,0:T(4,128)S(1)}, s32[1,4,112]{2,1,0:T(4,128)}, u32[]{:S(2)}) copy-start(s32[1,4,112]{2,1,0:T(4,128)} %param.15) | copy-start | bytes 5380
  2.7 15.5 %collective-permute-start = (bf16[112,2688]{1,0:T(8,128)(2,1)}, bf16[112,2688]{1,0:T(8,128)(2,1)S(1)}, u32[]{:S(2)}, u32[]{:S(2)}) collective-permute-start(bf16[112,2688]{1,0:T(8,128)(2,1)} %pack.1), channel_id=1, source_target_pairs={{0,8},{8,16},{16,24},{24,0},{1,9},{9,17},{17,25},{25,1},{2,10},{10... | collective-permute-start | bytes 1806344 | tf_op jit(solution)/shard_map/ppermute | solution.py:232
  4.2 17.4 %collective-permute-start.2 = (bf16[112,2560]{1,0:T(8,128)(2,1)S(1)}, bf16[112,2560]{1,0:T(8,128)(2,1)S(1)}, u32[]{:S(2)}, u32[]{:S(2)}) collective-permute-start(bf16[112,2560]{1,0:T(8,128)(2,1)S(1)} %pad_maximum_fusion), channel_id=1, source_target_pairs={{0,0},{8,24},{16,16},{24,8},{1,1},{9,25},{17,17},{25,9},{2,2},{10,... | collective-permute-start | bytes 1720328 | tf_op jit(solution)/shard_map/ppermute | solution.py:232
  18.2 28.7 %collective-permute-start.1 = (bf16[112,2688]{1,0:T(8,128)(2,1)S(1)}, bf16[112,2688]{1,0:T(8,128)(2,1)S(1)}, u32[]{:S(2)}, u32[]{:S(2)}) collective-permute-start(bf16[112,2688]{1,0:T(8,128)(2,1)S(1)} %collective-permute-done.packed_ref.side_ref), channel_id=1, source_target_pairs={{0,0},{8,24},{16,16},{24,8},{1,1},{9,25},{17,17},{25,9},{2,2},{10,... | collective-permute-start | bytes 1806344 | tf_op jit(solution)/shard_map/ppermute | solution.py:232
  23.1 15.3 %collective-permute-start.3 = (bf16[112,2560]{1,0:T(8,128)(2,1)S(1)}, bf16[112,2560]{1,0:T(8,128)(2,1)S(1)}, u32[]{:S(2)}, u32[]{:S(2)}) collective-permute-start(bf16[112,2560]{1,0:T(8,128)(2,1)S(1)} %get-tuple-element.14), channel_id=1, source_target_pairs={{0,24},{8,0},{16,8},{24,16},{1,25},{9,1},{17,9},{25,17},{2,26},{10... | collective-permute-start | bytes 1720328 | tf_op jit(solution)/shard_map/ppermute | solution.py:232
  23.2 1.2 %collective-permute-start.4 = (f32[2,128]{1,0:T(2,128)S(1)}, f32[2,128]{1,0:T(2,128)S(1)}, u32[]{:S(2)}, u32[]{:S(2)}) collective-permute-start(f32[2,128]{1,0:T(2,128)S(1)} %get-tuple-element.17), channel_id=1, source_target_pairs={{0,1},{1,0},{2,3},{3,2},{4,5},{5,4},{6,7},{7,6},{8,9},{9,8},{10,11... | collective-permute-start | bytes 3080 | tf_op jit(solution)/shard_map/ppermute | solution.py:243
  24.4 3.6 %collective-permute-start.5 = (f32[2,128]{1,0:T(2,128)S(1)}, f32[2,128]{1,0:T(2,128)S(1)}, u32[]{:S(2)}, u32[]{:S(2)}) collective-permute-start(f32[2,128]{1,0:T(2,128)S(1)} %add.9), channel_id=1, source_target_pairs={{0,2},{1,3},{2,0},{3,1},{4,6},{5,7},{6,4},{7,5},{8,10},{9,11},{10,... | collective-permute-start | bytes 3080 | tf_op jit(solution)/shard_map/ppermute | solution.py:243
  28.0 6.5 %collective-permute-start.7 = (f32[2,128]{1,0:T(2,128)S(1)}, f32[2,128]{1,0:T(2,128)S(1)}, u32[]{:S(2)}, u32[]{:S(2)}) collective-permute-start(f32[2,128]{1,0:T(2,128)S(1)} %add.10), channel_id=1, source_target_pairs={{0,28},{1,29},{2,30},{3,31},{4,24},{5,25},{6,26},{7,27},{8,4},{9,5... | collective-permute-start | bytes 3080 | tf_op jit(solution)/shard_map/ppermute | solution.py:246
  31.9 5.9 %collective-permute-start.6 = (f32[2,128]{1,0:T(2,128)S(1)}, f32[2,128]{1,0:T(2,128)S(1)}, u32[]{:S(2)}, u32[]{:S(2)}) collective-permute-start(f32[2,128]{1,0:T(2,128)S(1)} %add.10), channel_id=1, source_target_pairs={{0,24},{1,25},{2,26},{3,27},{4,28},{5,29},{6,30},{7,31},{8,0},{9,1... | collective-permute-start | bytes 3080 | tf_op jit(solution)/shard_map/ppermute | solution.py:246

commit v4 on v3

--- a/solution.py
+++ b/solution.py
@@ -14,6 +14,7 @@
 EXP2_SCALE = SCORE_SCALE * math.log2(math.e)
 
 VMEM_LIMIT = 16 << 20
+CUT_NUM, CUT_DEN = 9, 20
 NT = (((1,), (1,)), ((), ()))
 TN = (((0,), (0,)), ((), ()))
 NN = (((1,), (0,)), ((), ()))
@@ -43,28 +44,6 @@
     return jnp.concatenate([allowed] * copies, axis=1) > 0.5
 
 
-def side_rows(tile):
-    parts = tile.astype(jnp.float32)
-    return parts[0:4] + parts[4:8] + parts[8:12]
-
-
-def pack_kernel(q_ref, kv_ref, gains_ref, plan_ref, packed_ref):
-    q_width, kv_width = q_ref.shape[1], kv_ref.shape[1]
-    packed_ref[:, :q_width] = q_ref[...]
-    packed_ref[:, q_width : q_width + kv_width] = kv_ref[...]
-    numbers = [jnp.full((1, HEAD_SIZE), plan_ref[0, i]).astype(jnp.float32) for i in range(2)]
-    rest = jnp.concatenate([gains_ref[...]] + numbers, axis=0)
-    parts = []
-    for _ in range(3):
-        part = rest.astype(jnp.bfloat16).astype(jnp.float32)
-        rest = rest - part
-        parts.append(part)
-    parts = jnp.concatenate(parts + [jnp.zeros_like(rest)], axis=0)
-    empty = jnp.zeros((q_ref.shape[0] - 16, HEAD_SIZE), jnp.bfloat16)
-    packed_ref[0:16, q_width + kv_width :] = parts.astype(jnp.bfloat16)
-    packed_ref[16:, q_width + kv_width :] = empty
-
-
 def normalized(values):
     wide = values.astype(jnp.float32)
     factor = lax.rsqrt(jnp.mean(wide * wide, axis=1, keepdims=True) + EPSILON)
@@ -77,8 +56,8 @@
     return weights * (1.0 / jnp.sum(weights, axis=0, keepdims=True))
 
 
-def forward_kernel(packed_ref, segment_ref, out_ref):
-    side = side_rows(packed_ref[0:16, packed_ref.shape[1] - HEAD_SIZE :])
+def forward_kernel(packed_ref, side_ref, segment_ref, out_ref):
+    side = side_ref[...]
     tokens = packed_ref.shape[0]
     heads = out_ref.shape[1] // HEAD_SIZE
     kv_heads = (packed_ref.shape[1] // HEAD_SIZE - heads) // 2
@@ -107,8 +86,15 @@
     return jnp.sum(terms.reshape(-1, 8, terms.shape[1]), axis=0)
 
 
-def backward_kernel(packed_ref, up_ref, side_ref, segment_ref, grad_ref, gain_ref):
-    side = side_rows(side_ref[...])
+def backward_kernel(packed_ref, up_ref, side_ref, segment_ref, *outs):
+    *grad_refs, gain_ref = outs
+
+    def write(block, value):
+        first = grad_refs[0].shape[1] // HEAD_SIZE
+        ref, at = (grad_refs[0], block) if block < first else (grad_refs[1], block - first)
+        ref[:, at * HEAD_SIZE : (at + 1) * HEAD_SIZE] = value.astype(jnp.bfloat16)
+
+    side = side_ref[...]
     tokens = packed_ref.shape[0]
     heads = up_ref.shape[1] // HEAD_SIZE
     kv_heads = (packed_ref.shape[1] // HEAD_SIZE - heads) // 2
@@ -133,18 +119,12 @@
             query_hat, query_factor, q_gain * SCORE_SCALE, dot(d_scores, key, TN)
         )
         q_terms += summed_rows(terms)
-        d_query = d_query.astype(jnp.bfloat16)
         for i in range(per_kv):
-            h = g * per_kv + i
-            grad_ref[:, h * HEAD_SIZE : (h + 1) * HEAD_SIZE] = d_query[
-                i * tokens : (i + 1) * tokens
-            ]
+            write(g * per_kv + i, d_query[i * tokens : (i + 1) * tokens])
         d_key, terms = norm_back(key_hat, key_factor, k_gain * SCORE_SCALE, d_key)
         k_terms += summed_rows(terms)
-        at = (heads + g) * HEAD_SIZE
-        grad_ref[:, at : at + HEAD_SIZE] = d_key.astype(jnp.bfloat16)
-        at = (heads + kv_heads + g) * HEAD_SIZE
-        grad_ref[:, at : at + HEAD_SIZE] = d_value.astype(jnp.bfloat16)
+        write(heads + g, d_key)
+        write(heads + kv_heads + g, d_value)
     gain_ref[0:1, :] = jnp.sum(q_terms, axis=0, keepdims=True) * SCORE_SCALE
     gain_ref[1:2, :] = jnp.sum(k_terms, axis=0, keepdims=True) * SCORE_SCALE
 
@@ -156,48 +136,31 @@
 VMEM = pl.BlockSpec(memory_space=pltpu.VMEM)
 
 
-def side_tile(fresh):
-    at = fresh.shape[1] // HEAD_SIZE - 1
-    return pl.BlockSpec((16, HEAD_SIZE), lambda step: (0, at))
-
-
-def pack(q, kv, gains, plan):
-    return pl.pallas_call(
-        pack_kernel,
-        out_shape=jax.ShapeDtypeStruct((q.shape[0], q.shape[1] + kv.shape[1] + HEAD_SIZE), q.dtype),
-        in_specs=[VMEM] * 3 + [pl.BlockSpec(memory_space=pltpu.SMEM)],
-        out_specs=VMEM,
-        cost_estimate=cost(1024),
-        name="pack",
-    )(q, kv, gains, plan)
-
-
-def forward(fresh, q_width, segments):
+def forward(fresh, q_width, side, segments):
     return pl.pallas_call(
         forward_kernel,
         out_shape=jax.ShapeDtypeStruct((fresh.shape[0], q_width), fresh.dtype),
-        in_specs=[VMEM, VMEM],
+        in_specs=[VMEM] * 3,
         out_specs=VMEM,
         cost_estimate=cost(1024),
         compiler_params=pltpu.CompilerParams(vmem_limit_bytes=VMEM_LIMIT),
         name="forward",
-    )(fresh, segments)
-
-
-def backward(packed, upstream, fresh, segments):
+    )(fresh, side, segments)
+
+
+def backward(packed, upstream, side, segments):
+    tokens, width = packed.shape
+    cut = width // HEAD_SIZE * CUT_NUM // CUT_DEN * HEAD_SIZE
     return pl.pallas_call(
         backward_kernel,
-        out_shape=(
-            jax.ShapeDtypeStruct(packed.shape, packed.dtype),
-            jax.ShapeDtypeStruct((2, HEAD_SIZE), jnp.float32),
-        ),
-        grid=(1,),
-        in_specs=[VMEM, VMEM, side_tile(fresh), VMEM],
-        out_specs=(VMEM, VMEM),
+        out_shape=[jax.ShapeDtypeStruct((tokens, w), packed.dtype) for w in (cut, width - cut)]
+        + [jax.ShapeDtypeStruct((2, HEAD_SIZE), jnp.float32)],
+        in_specs=[VMEM] * 4,
+        out_specs=[VMEM] * 3,
         cost_estimate=cost(1024),
         compiler_params=pltpu.CompilerParams(vmem_limit_bytes=VMEM_LIMIT),
         name="backward",
-    )(packed, upstream, fresh, segments)
+    )(packed, upstream, side, segments)
 
 
 def unpack_kernel(packed_ref, q_ref, kv_ref):
@@ -216,6 +179,25 @@
         compiler_params=pltpu.CompilerParams(vmem_limit_bytes=VMEM_LIMIT),
         name="unpack",
     )(packed)
+
+
+def merge_kernel(first_ref, second_ref, q_ref, kv_ref):
+    cut, q_width = first_ref.shape[1], q_ref.shape[1]
+    q_ref[:, :cut] = first_ref[...]
+    q_ref[:, cut:] = second_ref[:, : q_width - cut]
+    kv_ref[...] = second_ref[:, q_width - cut :]
+
+
+def merge(grads, widths):
+    return pl.pallas_call(
+        merge_kernel,
+        out_shape=[
+            jax.ShapeDtypeStruct((grads[0].shape[0], width), grads[0].dtype) for width in widths
+        ],
+        cost_estimate=cost(1024),
+        compiler_params=pltpu.CompilerParams(vmem_limit_bytes=VMEM_LIMIT),
+        name="merge",
+    )(*grads)
 
 
 def local(
@@ -231,12 +213,22 @@
     def hop(value, pairs):
         return lax.ppermute(value, "section", pairs)
 
-    fresh = hop(pack(fresh_q[0], current_key_value[0], norm_gains[0], plan), up)
+    numbers = jnp.broadcast_to(plan[0].astype(jnp.float32)[:, None], (2, HEAD_SIZE))
+    fresh = hop(jnp.concatenate([fresh_q[0], current_key_value[0]], axis=1), up)
     held = hop(jnp.concatenate([held_q[0], retained_key_value[0]], axis=1), opposite)
+    side = hop(jnp.concatenate([norm_gains[0], numbers], axis=0), up)
     stored = hop(fresh, opposite)
-    grad, gain = backward(held, cotangent[0], fresh, segments)
-    grad = hop(grad, down)
-    attention_out = forward(fresh, widths[0], segments)
+    first, second, gain = backward(held, cotangent[0], side, segments)
+    fixed = [i for i in range(sections) if -i % sections == i]
+    across = [(i, (i + sections // 2) % sections) for i in fixed]
+    after = [(j, (i - 1) % sections) for i, j in across]
+    straight = [(i, (i - 1) % sections) for i in range(sections) if i not in fixed]
+    crossed = hop(first, across)
+    me = lax.axis_index("section")
+    stays = functools.reduce(jnp.logical_or, [me == i for i in fixed])
+    first = hop(jnp.where(stays, crossed, first), after + straight)
+    second = hop(second, down)
+    attention_out = forward(fresh, widths[0], side, segments)
 
     step = 1
     while 2 * step < replicas:
@@ -254,9 +246,10 @@
         )
         for other in (0, step)
     ]
+    stored_q, stored_kv = unpack(stored, widths)
+    grad_q, grad_kv = merge((first, second), widths)
+    *halves, grad_q, stored_q = lax.optimization_barrier((*halves, grad_q, stored_q))
     gain = (halves[0] + halves[1]) * (1.0 / replicas)
-    stored_q, stored_kv = unpack(stored, widths)
-    grad_q, grad_kv = unpack(grad, widths)
     return (
         attention_out[None],
         stored_q[None],

time: 47.9 us -> 45.7 us (0.954)
  the two profiles are of different devices: /device:TPU:2 before, /device:TPU:0 now
where the time goes in v4:
time: 45.7 us; the launch traced here: 45.5 us
  waiting for transfers between devices  19.9 us (44%)
  starting transfers between devices  17.8 us (39%)
  Pallas kernels  4.96 us (11%)
  other arithmetic  1.9 us (4%)
  between operations  0.8 us (2%)
    ppermute x7, waiting for transfers between devices, hop(): return lax.ppermute(value, 'section', pairs)  16.8 us
    ppermute x7, starting transfers between devices, hop(): return lax.ppermute(value, 'section', pairs)  11.2 us
    ppermute x2, starting transfers between devices, local(): lax.ppermute(gain, ('section', 'dp'), [(i * replicas + j, (i - 1) % secti...  5.01 us
    ppermute x2, waiting for transfers between devices, local(): lax.ppermute(gain, 'dp', [(i, i ^ step) for i in range(replicas)])  3.12 us
    pallas_call x1, Pallas kernels, forward(): pl.pallas_call(forward_kernel, out_shape=jax.ShapeDtypeStruct((fresh.shap...  1.84 us
    ppermute x2, starting transfers between devices, local(): lax.ppermute(gain, 'dp', [(i, i ^ step) for i in range(replicas)])  1.65 us
    pallas_call x1, Pallas kernels, backward(): pl.pallas_call(backward_kernel, out_shape=[jax.ShapeDtypeStruct((tokens,...  1.44 us
    concatenate x1, other arithmetic, local(): jnp.concatenate([held_q[0], retained_key_value[0]], axis=1)  1.17 us
  transfers between devices with their start and end apart: 11, of which 4 were waited for; matrix products, arithmetic and copies ran while one was open for 1% of the time, Pallas kernels for 11%

profile of v4, /device:TPU:0, one launch (start us, length us, event | category | flops | bytes accessed | tf_op | source)
XLA Modules:
  0.0 45.5 jit_solution(9148161990898354475)
XLA Ops:
  0.6 0.0 copy-start.2
  0.6 0.0 copy-start.3
  0.7 1.2 %pad_maximum_fusion.1 = bf16[112,2560]{1,0:T(8,128)(2,1)S(1)} fusion(bf16[112,512]{1,0:T(8,128)(2,1)} %bitcast.22, bf16[112,2048]{1,0:T(8,128)(2,1)} %bitcast.19), kind=kLoop, calls=%fused_computation.1 | loop fusion | flops 1146880 | bytes 1146880 | tf_op jit(solution)/shard_map/concatenate | solution.py:218
  1.8 0.7 %collective-permute-start.2 = (bf16[112,2560]{1,0:T(8,128)(2,1)S(1)}, bf16[112,2560]{1,0:T(8,128)(2,1)S(1)}, u32[]{:S(2)}, u32[]{:S(2)}) collective-permute-start(bf16[112,2560]{1,0:T(8,128)(2,1)S(1)} %pad_maximum_fusion.1), channel_id=1, source_target_pairs={{0,0},{8,24},{16,16},{24,8},{1,1},{9,25},{17,17},{25,9},{2,2},{10,... | collective-permute-start | bytes 1720328 | tf_op jit(solution)/shard_map/ppermute | solution.py:214
  2.5 0.0 copy-done.2
  2.5 0.0 copy-done.3
  2.6 0.0 copy-start.5
  2.6 0.0 copy-start.4
  2.6 0.0 copy-start
  2.6 0.0 copy-start.1
  2.6 5.7 %collective-permute-start = (bf16[112,2560]{1,0:T(8,128)(2,1)S(1)}, bf16[112,2560]{1,0:T(8,128)(2,1)S(1)}, u32[]{:S(2)}, u32[]{:S(2)}) collective-permute-start(bf16[112,2560]{1,0:T(8,128)(2,1)S(1)} %pad_maximum_fusion), channel_id=1, source_target_pairs={{0,8},{8,16},{16,24},{24,0},{1,9},{9,17},{17,25},{25,1},{2,10},{10... | collective-permute-start | bytes 1720328 | tf_op jit(solution)/shard_map/ppermute | solution.py:214
  8.4 0.0 copy-done.5
  8.4 0.1 pad.3.clone
  8.5 0.0 copy-done.4
  8.5 0.1 pad_maximum_fusion.2
  8.5 0.5 %collective-permute-start.1 = (f32[4,128]{1,0:T(4,128)S(1)}, f32[4,128]{1,0:T(4,128)S(1)}, u32[]{:S(2)}, u32[]{:S(2)}) collective-permute-start(f32[4,128]{1,0:T(4,128)S(1)} %pad_maximum_fusion.2), channel_id=1, source_target_pairs={{0,8},{8,16},{16,24},{24,0},{1,9},{9,17},{17,25},{25,1},{2,10},{10... | collective-permute-start | bytes 6152 | tf_op jit(solution)/shard_map/ppermute | solution.py:214
  9.0 12.0 %collective-permute-done.1.side_ref = f32[4,128]{1,0:T(4,128)S(1)} collective-permute-done((f32[4,128]{1,0:T(4,128)S(1)}, f32[4,128]{1,0:T(4,128)S(1)}, u32[]{:S(2)}, u32[]{:S(2)}) %collective-permute-start.1) | collective-permute-done | bytes 2080 | tf_op jit(solution)/shard_map/ppermute | solution.py:214
  21.1 0.0 collective-permute-done.2.packed_ref
  21.1 0.0 copy-done
  21.1 0.0 copy-done.1
  21.1 1.4 %backward.1 = (bf16[112,1152]{1,0:T(8,128)(2,1)S(1)}, bf16[112,1408]{1,0:T(8,128)(2,1)S(1)}, f32[2,128]{1,0:T(2,128)S(1)}) custom-call(bf16[112,2560]{1,0:T(8,128)(2,1)S(1)} %collective-permute-done.2.packed_ref, bf16[112,2048]{1,0:T(8,128)(2,1)S(1)} %bitcast.16, f32[4,128]{1,0:T(4,128)S(1)} %collective-permute-done.1.side_ref, s32[4,112]{1,0:T(4,128)S(1)} %bitcast.17), custom_call_target="tpu_custom_call" | custom-call | flops 1024 | bytes 1024 | tf_op jit(solution)/shard_map/backward/pallas_call | solution.py:154
  22.5 3.4 %collective-permute-start.7 = (bf16[112,1152]{1,0:T(8,128)(2,1)S(1)}, bf16[112,1152]{1,0:T(8,128)(2,1)S(1)}, u32[]{:S(2)}, u32[]{:S(2)}) collective-permute-start(bf16[112,1152]{1,0:T(8,128)(2,1)S(1)} %get-tuple-element.18), channel_id=1, source_target_pairs={{0,16},{16,0},{1,17},{17,1},{2,18},{18,2},{3,19},{19,3},{4,20},{20... | collective-permute-start | bytes 774152 | tf_op jit(solution)/shard_map/ppermute | solution.py:214
  26.0 0.1 collective-permute-start.9
  26.0 0.0 collective-permute-done.packed_ref
  26.0 0.7 %collective-permute-start.10 = (bf16[112,2560]{1,0:T(8,128)(2,1)S(1)}, bf16[112,2560]{1,0:T(8,128)(2,1)S(1)}, u32[]{:S(2)}, u32[]{:S(2)}) collective-permute-start(bf16[112,2560]{1,0:T(8,128)(2,1)S(1)} %collective-permute-done.packed_ref), channel_id=1, source_target_pairs={{0,0},{8,24},{16,16},{24,8},{1,1},{9,25},{17,17},{25,9},{2,2},{10,... | collective-permute-start | bytes 1720328 | tf_op jit(solution)/shard_map/ppermute | solution.py:214
  26.7 4.8 %collective-permute-done.7 = bf16[112,1152]{1,0:T(8,128)(2,1)S(1)} collective-permute-done((bf16[112,1152]{1,0:T(8,128)(2,1)S(1)}, bf16[112,1152]{1,0:T(8,128)(2,1)S(1)}, u32[]{:S(2)}, u32[]{:S(2)}) %collective-permute-start.7) | collective-permute-done | bytes 258080 | tf_op jit(solution)/shard_map/ppermute | solution.py:214
  31.5 0.1 collective-permute-start.8
  31.6 0.1 collective-permute-start.3
  31.7 1.1 %collective-permute-done.3 = f32[2,128]{1,0:T(2,128)S(1)} collective-permute-done((f32[2,128]{1,0:T(2,128)S(1)}, f32[2,128]{1,0:T(2,128)S(1)}, u32[]{:S(2)}, u32[]{:S(2)}) %collective-permute-start.3) | collective-permute-done | bytes 1056 | tf_op jit(solution)/shard_map/ppermute | solution.py:235
  32.8 1.6 %collective-permute-start.4 = (f32[2,128]{1,0:T(2,128)S(1)}, f32[2,128]{1,0:T(2,128)S(1)}, u32[]{:S(2)}, u32[]{:S(2)}) collective-permute-start(f32[2,128]{1,0:T(2,128)S(1)} %add.9), channel_id=1, source_target_pairs={{0,2},{1,3},{2,0},{3,1},{4,6},{5,7},{6,4},{7,5},{8,10},{9,11},{10,... | collective-permute-start | bytes 3080 | tf_op jit(solution)/shard_map/ppermute | solution.py:235
  34.4 2.0 %collective-permute-done.4 = f32[2,128]{1,0:T(2,128)S(1)} collective-permute-done((f32[2,128]{1,0:T(2,128)S(1)}, f32[2,128]{1,0:T(2,128)S(1)}, u32[]{:S(2)}, u32[]{:S(2)}) %collective-permute-start.4) | collective-permute-done | bytes 1056 | tf_op jit(solution)/shard_map/ppermute | solution.py:235
  36.4 4.9 %collective-permute-start.6 = (f32[2,128]{1,0:T(2,128)S(1)}, f32[2,128]{1,0:T(2,128)S(1)}, u32[]{:S(2)}, u32[]{:S(2)}) collective-permute-start(f32[2,128]{1,0:T(2,128)S(1)} %add.10), channel_id=1, source_target_pairs={{0,28},{1,29},{2,30},{3,31},{4,24},{5,25},{6,26},{7,27},{8,4},{9,5... | collective-permute-start | bytes 3080 | tf_op jit(solution)/shard_map/ppermute | solution.py:238
  41.3 0.1 collective-permute-start.5
  41.4 1.8 %forward.1 = bf16[112,2048]{1,0:T(8,128)(2,1)} custom-call(bf16[112,2560]{1,0:T(8,128)(2,1)S(1)} %collective-permute-done.packed_ref, f32[4,128]{1,0:T(4,128)S(1)} %collective-permute-done.1.side_ref, s32[4,112]{1,0:T(4,128)S(1)} %bitcast.18), custom_call_target="tpu_custom_call" | custom-call | flops 1024 | bytes 1024 | tf_op jit(solution)/shard_map/forward/pallas_call | solution.py:140
  43.2 0.0 collective-permute-done.9.second_ref
  43.3 0.0 collective-permute-done.8.first_ref
  43.3 0.8 %merge.1 = (bf16[112,2048]{1,0:T(8,128)(2,1)}, bf16[112,512]{1,0:T(8,128)(2,1)}) custom-call(bf16[112,1152]{1,0:T(8,128)(2,1)S(1)} %collective-permute-done.8.first_ref, bf16[112,1408]{1,0:T(8,128)(2,1)S(1)} %collective-permute-done.9.second_ref), custom_call_target="tpu_custom_call" | custom-call | flops 1024 | bytes 1024 | tf_op jit(solution)/shard_map/merge/pallas_call | solution.py:192
  44.1 0.0 collective-permute-done.10.packed_ref
  44.1 0.8 %unpack.1 = (bf16[112,2048]{1,0:T(8,128)(2,1)}, bf16[112,512]{1,0:T(8,128)(2,1)}) custom-call(bf16[112,2560]{1,0:T(8,128)(2,1)S(1)} %collective-permute-done.10.packed_ref), custom_call_target="tpu_custom_call" | custom-call | flops 1024 | bytes 1024 | tf_op jit(solution)/shard_map/unpack/pallas_call | solution.py:173
  44.9 0.0 collective-permute-done.6
  44.9 0.0 collective-permute-done.5
  44.9 0.6 %multiply_bitcast_fusion = f32[1,2,128]{2,1,0:T(2,128)} fusion(f32[2,128]{1,0:T(2,128)S(1)} %collective-permute-done.5, f32[2,128]{1,0:T(2,128)S(1)} %collective-permute-done.6), kind=kLoop, calls=%fused_computation.4 | loop fusion | flops 512 | bytes 3072 | tf_op jit(solution)/shard_map/broadcast_in_dim | solution.py:259
  (5 shorter events, 0.1 us)
Async XLA Ops:
  0.6 1.9 %copy-start.2 = (bf16[1,112,2048]{2,1,0:T(8,128)(2,1)S(1)}, bf16[1,112,2048]{2,1,0:T(8,128)(2,1)}, u32[]{:S(2)}) copy-start(bf16[1,112,2048]{2,1,0:T(8,128)(2,1)} %param.8) | copy-start | bytes 1376260
  0.6 1.9 %copy-start.3 = (bf16[1,112,512]{2,1,0:T(8,128)(2,1)S(1)}, bf16[1,112,512]{2,1,0:T(8,128)(2,1)}, u32[]{:S(2)}) copy-start(bf16[1,112,512]{2,1,0:T(8,128)(2,1)} %param.9) | copy-start | bytes 344068
  1.8 19.2 %collective-permute-start.2 = (bf16[112,2560]{1,0:T(8,128)(2,1)S(1)}, bf16[112,2560]{1,0:T(8,128)(2,1)S(1)}, u32[]{:S(2)}, u32[]{:S(2)}) collective-permute-start(bf16[112,2560]{1,0:T(8,128)(2,1)S(1)} %pad_maximum_fusion.1), channel_id=1, source_target_pairs={{0,0},{8,24},{16,16},{24,8},{1,1},{9,25},{17,17},{25,9},{2,2},{10,... | collective-permute-start | bytes 1720328 | tf_op jit(solution)/shard_map/ppermute | solution.py:214
  2.6 5.8 %copy-start.5 = (s32[1,2]{1,0:T(1,128)S(1)}, s32[1,2]{1,0:T(1,128)}, u32[]{:S(2)}) copy-start(s32[1,2]{1,0:T(1,128)} %param.14) | copy-start | bytes 28
  2.6 5.9 %copy-start.4 = (f32[1,2,128]{2,1,0:T(2,128)S(1)}, f32[1,2,128]{2,1,0:T(2,128)}, u32[]{:S(2)}) copy-start(f32[1,2,128]{2,1,0:T(2,128)} %param.13) | copy-start | bytes 3076
  2.6 18.5 %copy-start = (bf16[1,112,2048]{2,1,0:T(8,128)(2,1)S(1)}, bf16[1,112,2048]{2,1,0:T(8,128)(2,1)}, u32[]{:S(2)}) copy-start(bf16[1,112,2048]{2,1,0:T(8,128)(2,1)} %param.12) | copy-start | bytes 1376260
  2.6 18.5 %copy-start.1 = (s32[1,4,112]{2,1,0:T(4,128)S(1)}, s32[1,4,112]{2,1,0:T(4,128)}, u32[]{:S(2)}) copy-start(s32[1,4,112]{2,1,0:T(4,128)} %param.15) | copy-start | bytes 5380
  2.6 23.4 %collective-permute-start = (bf16[112,2560]{1,0:T(8,128)(2,1)S(1)}, bf16[112,2560]{1,0:T(8,128)(2,1)S(1)}, u32[]{:S(2)}, u32[]{:S(2)}) collective-permute-start(bf16[112,2560]{1,0:T(8,128)(2,1)S(1)} %pad_maximum_fusion), channel_id=1, source_target_pairs={{0,8},{8,16},{16,24},{24,0},{1,9},{9,17},{17,25},{25,1},{2,10},{10... | collective-permute-start | bytes 1720328 | tf_op jit(solution)/shard_map/ppermute | solution.py:214
  8.5 12.5 %collective-permute-start.1 = (f32[4,128]{1,0:T(4,128)S(1)}, f32[4,128]{1,0:T(4,128)S(1)}, u32[]{:S(2)}, u32[]{:S(2)}) collective-permute-start(f32[4,128]{1,0:T(4,128)S(1)} %pad_maximum_fusion.2), channel_id=1, source_target_pairs={{0,8},{8,16},{16,24},{24,0},{1,9},{9,17},{17,25},{25,1},{2,10},{10... | collective-permute-start | bytes 6152 | tf_op jit(solution)/shard_map/ppermute | solution.py:214
  22.5 9.0 %collective-permute-start.7 = (bf16[112,1152]{1,0:T(8,128)(2,1)S(1)}, bf16[112,1152]{1,0:T(8,128)(2,1)S(1)}, u32[]{:S(2)}, u32[]{:S(2)}) collective-permute-start(bf16[112,1152]{1,0:T(8,128)(2,1)S(1)} %get-tuple-element.18), channel_id=1, source_target_pairs={{0,16},{16,0},{1,17},{17,1},{2,18},{18,2},{3,19},{19,3},{4,20},{20... | collective-permute-start | bytes 774152 | tf_op jit(solution)/shard_map/ppermute | solution.py:214
  26.0 17.3 %collective-permute-start.9 = (bf16[112,1408]{1,0:T(8,128)(2,1)S(1)}, bf16[112,1408]{1,0:T(8,128)(2,1)S(1)}, u32[]{:S(2)}, u32[]{:S(2)}) collective-permute-start(bf16[112,1408]{1,0:T(8,128)(2,1)S(1)} %get-tuple-element.19), channel_id=1, source_target_pairs={{0,24},{8,0},{16,8},{24,16},{1,25},{9,1},{17,9},{25,17},{2,26},{10... | collective-permute-start | bytes 946184 | tf_op jit(solution)/shard_map/ppermute | solution.py:214
  26.0 18.1 %collective-permute-start.10 = (bf16[112,2560]{1,0:T(8,128)(2,1)S(1)}, bf16[112,2560]{1,0:T(8,128)(2,1)S(1)}, u32[]{:S(2)}, u32[]{:S(2)}) collective-permute-start(bf16[112,2560]{1,0:T(8,128)(2,1)S(1)} %collective-permute-done.packed_ref), channel_id=1, source_target_pairs={{0,0},{8,24},{16,16},{24,8},{1,1},{9,25},{17,17},{25,9},{2,2},{10,... | collective-permute-start | bytes 1720328 | tf_op jit(solution)/shard_map/ppermute | solution.py:214
  31.5 11.7 %collective-permute-start.8 = (bf16[112,1152]{1,0:T(8,128)(2,1)S(1)}, bf16[112,1152]{1,0:T(8,128)(2,1)S(1)}, u32[]{:S(2)}, u32[]{:S(2)}) collective-permute-start(bf16[112,1152]{1,0:T(8,128)(2,1)S(1)} %broadcast_select_fusion), channel_id=1, source_target_pairs={{16,24},{0,8},{8,0},{24,16},{17,25},{1,9},{9,1},{25,17},{18,26},{2... | collective-permute-start | bytes 774152 | tf_op jit(solution)/shard_map/ppermute | solution.py:214
  31.6 1.2 %collective-permute-start.3 = (f32[2,128]{1,0:T(2,128)S(1)}, f32[2,128]{1,0:T(2,128)S(1)}, u32[]{:S(2)}, u32[]{:S(2)}) collective-permute-start(f32[2,128]{1,0:T(2,128)S(1)} %get-tuple-element.17), channel_id=1, source_target_pairs={{0,1},{1,0},{2,3},{3,2},{4,5},{5,4},{6,7},{7,6},{8,9},{9,8},{10,11... | collective-permute-start | bytes 3080 | tf_op jit(solution)/shard_map/ppermute | solution.py:235
  32.8 3.6 %collective-permute-start.4 = (f32[2,128]{1,0:T(2,128)S(1)}, f32[2,128]{1,0:T(2,128)S(1)}, u32[]{:S(2)}, u32[]{:S(2)}) collective-permute-start(f32[2,128]{1,0:T(2,128)S(1)} %add.9), channel_id=1, source_target_pairs={{0,2},{1,3},{2,0},{3,1},{4,6},{5,7},{6,4},{7,5},{8,10},{9,11},{10,... | collective-permute-start | bytes 3080 | tf_op jit(solution)/shard_map/ppermute | solution.py:235
  36.4 8.5 %collective-permute-start.6 = (f32[2,128]{1,0:T(2,128)S(1)}, f32[2,128]{1,0:T(2,128)S(1)}, u32[]{:S(2)}, u32[]{:S(2)}) collective-permute-start(f32[2,128]{1,0:T(2,128)S(1)} %add.10), channel_id=1, source_target_pairs={{0,28},{1,29},{2,30},{3,31},{4,24},{5,25},{6,26},{7,27},{8,4},{9,5... | collective-permute-start | bytes 3080 | tf_op jit(solution)/shard_map/ppermute | solution.py:238
  41.3 3.6 %collective-permute-start.5 = (f32[2,128]{1,0:T(2,128)S(1)}, f32[2,128]{1,0:T(2,128)S(1)}, u32[]{:S(2)}, u32[]{:S(2)}) collective-permute-start(f32[2,128]{1,0:T(2,128)S(1)} %add.10), channel_id=1, source_target_pairs={{0,24},{1,25},{2,26},{3,27},{4,28},{5,29},{6,30},{7,31},{8,0},{9,1... | collective-permute-start | bytes 3080 | tf_op jit(solution)/shard_map/ppermute | solution.py:238

commit v5 on v4

--- a/solution.py
+++ b/solution.py
@@ -14,7 +14,7 @@
 EXP2_SCALE = SCORE_SCALE * math.log2(math.e)
 
 VMEM_LIMIT = 16 << 20
-CUT_NUM, CUT_DEN = 9, 20
+CUT_NUM, CUT_DEN = 10, 20
 NT = (((1,), (1,)), ((), ()))
 TN = (((0,), (0,)), ((), ()))
 NN = (((1,), (0,)), ((), ()))
@@ -226,14 +226,16 @@
     crossed = hop(first, across)
     me = lax.axis_index("section")
     stays = functools.reduce(jnp.logical_or, [me == i for i in fixed])
-    first = hop(jnp.where(stays, crossed, first), after + straight)
     second = hop(second, down)
-    attention_out = forward(fresh, widths[0], side, segments)
-
     step = 1
     while 2 * step < replicas:
         gain = gain + lax.ppermute(gain, "dp", [(i, i ^ step) for i in range(replicas)])
         step *= 2
+    crossed, second, gain = lax.optimization_barrier((crossed, second, gain))
+    first = jnp.where(stays, crossed, first)
+    first = hop(first, after + straight)
+    attention_out = forward(fresh, widths[0], side, segments)
+
     halves = [
         lax.ppermute(
             gain,
@@ -248,7 +250,7 @@
     ]
     stored_q, stored_kv = unpack(stored, widths)
     grad_q, grad_kv = merge((first, second), widths)
-    *halves, grad_q, stored_q = lax.optimization_barrier((*halves, grad_q, stored_q))
+    *halves, grad_q = lax.optimization_barrier((*halves, grad_q))
     gain = (halves[0] + halves[1]) * (1.0 / replicas)
     return (
         attention_out[None],

time: 45.7 us -> 43.6 us (0.954)
  waiting for transfers between devices: 19.9 us -> 16 us
  starting transfers between devices: 17.8 us -> 19.6 us
    ppermute x7, waiting for transfers between devices: 16.8 us -> 13.2 us  [hop(): return lax.ppermute(value, 'section', pairs)]
    ppermute x7, starting transfers between devices: 11.2 us -> 12.9 us  [hop(): return lax.ppermute(value, 'section', pairs)]
    ppermute x2, waiting for transfers between devices: 3.12 us -> 2.42 us  [local(): lax.ppermute(gain, 'dp', [(i, i ^ step) for i in range(replicas)])]
  transfers between devices with their start and end apart: 11 -> 11, of which waited for: 4 -> 6; matrix products, arithmetic and copies ran while one was open for 1% -> 2% of each run, Pallas kernels for 11% -> 9%
where the time goes in v5:
time: 43.6 us; the launch traced here: 43.4 us
  starting transfers between devices  19.6 us (45%)
  waiting for transfers between devices  16 us (37%)
  Pallas kernels  4.96 us (11%)
  other arithmetic  1.89 us (4%)
  between operations  0.78 us (2%)
    ppermute x7, waiting for transfers between devices, hop(): return lax.ppermute(value, 'section', pairs)  13.2 us
    ppermute x7, starting transfers between devices, hop(): return lax.ppermute(value, 'section', pairs)  12.9 us
    ppermute x2, starting transfers between devices, local(): lax.ppermute(gain, ('section', 'dp'), [(i * replicas + j, (i - 1) % secti...  5.06 us
    ppermute x2, waiting for transfers between devices, local(): lax.ppermute(gain, 'dp', [(i, i ^ step) for i in range(replicas)])  2.42 us
    pallas_call x1, Pallas kernels, forward(): pl.pallas_call(forward_kernel, out_shape=jax.ShapeDtypeStruct((fresh.shap...  1.84 us
    ppermute x2, starting transfers between devices, local(): lax.ppermute(gain, 'dp', [(i, i ^ step) for i in range(replicas)])  1.65 us
    pallas_call x1, Pallas kernels, backward(): pl.pallas_call(backward_kernel, out_shape=[jax.ShapeDtypeStruct((tokens,...  1.44 us
    concatenate x1, other arithmetic, local(): jnp.concatenate([held_q[0], retained_key_value[0]], axis=1)  1.17 us
  transfers between devices with their start and end apart: 11, of which 6 were waited for; matrix products, arithmetic and copies ran while one was open for 2% of the time, Pallas kernels for 9%

profile of v5, /device:TPU:0, one launch (start us, length us, event | category | flops | bytes accessed | tf_op | source)
XLA Modules:
  0.0 43.4 jit_solution(16315839050742138003)
XLA Ops:
  0.6 0.0 copy-start.2
  0.6 0.0 copy-start.3
  0.7 1.2 %pad_maximum_fusion.1 = bf16[112,2560]{1,0:T(8,128)(2,1)S(1)} fusion(bf16[112,512]{1,0:T(8,128)(2,1)} %bitcast.22, bf16[112,2048]{1,0:T(8,128)(2,1)} %bitcast.19), kind=kLoop, calls=%fused_computation.1 | loop fusion | flops 1146880 | bytes 1146880 | tf_op jit(solution)/shard_map/concatenate | solution.py:218
  1.8 0.7 %collective-permute-start.3 = (bf16[112,2560]{1,0:T(8,128)(2,1)S(1)}, bf16[112,2560]{1,0:T(8,128)(2,1)S(1)}, u32[]{:S(2)}, u32[]{:S(2)}) collective-permute-start(bf16[112,2560]{1,0:T(8,128)(2,1)S(1)} %pad_maximum_fusion.1), channel_id=1, source_target_pairs={{0,0},{8,24},{16,16},{24,8},{1,1},{9,25},{17,17},{25,9},{2,2},{10,... | collective-permute-start | bytes 1720328 | tf_op jit(solution)/shard_map/ppermute | solution.py:214
  2.5 0.0 copy-done.2
  2.5 0.0 copy-done.3
  2.6 0.0 copy-start.5
  2.6 0.0 copy-start.4
  2.6 0.0 copy-start
  2.6 0.0 copy-start.1
  2.6 5.7 %collective-permute-start = (bf16[112,2560]{1,0:T(8,128)(2,1)S(1)}, bf16[112,2560]{1,0:T(8,128)(2,1)S(1)}, u32[]{:S(2)}, u32[]{:S(2)}) collective-permute-start(bf16[112,2560]{1,0:T(8,128)(2,1)S(1)} %pad_maximum_fusion), channel_id=1, source_target_pairs={{0,8},{8,16},{16,24},{24,0},{1,9},{9,17},{17,25},{25,1},{2,10},{10... | collective-permute-start | bytes 1720328 | tf_op jit(solution)/shard_map/ppermute | solution.py:214
  8.4 0.0 copy-done.5
  8.4 0.1 pad.3.clone
  8.5 0.0 copy-done.4
  8.5 0.1 pad_maximum_fusion.2
  8.5 0.5 %collective-permute-start.1 = (f32[4,128]{1,0:T(4,128)S(1)}, f32[4,128]{1,0:T(4,128)S(1)}, u32[]{:S(2)}, u32[]{:S(2)}) collective-permute-start(f32[4,128]{1,0:T(4,128)S(1)} %pad_maximum_fusion.2), channel_id=1, source_target_pairs={{0,8},{8,16},{16,24},{24,0},{1,9},{9,17},{17,25},{25,1},{2,10},{10... | collective-permute-start | bytes 6152 | tf_op jit(solution)/shard_map/ppermute | solution.py:214
  9.0 12.0 %collective-permute-done.1.side_ref = f32[4,128]{1,0:T(4,128)S(1)} collective-permute-done((f32[4,128]{1,0:T(4,128)S(1)}, f32[4,128]{1,0:T(4,128)S(1)}, u32[]{:S(2)}, u32[]{:S(2)}) %collective-permute-start.1) | collective-permute-done | bytes 2080 | tf_op jit(solution)/shard_map/ppermute | solution.py:214
  21.1 0.0 collective-permute-done.3.packed_ref
  21.1 0.0 copy-done
  21.1 0.0 copy-done.1
  21.1 1.4 %backward.1 = (bf16[112,1280]{1,0:T(8,128)(2,1)S(1)}, bf16[112,1280]{1,0:T(8,128)(2,1)S(1)}, f32[2,128]{1,0:T(2,128)S(1)}) custom-call(bf16[112,2560]{1,0:T(8,128)(2,1)S(1)} %collective-permute-done.3.packed_ref, bf16[112,2048]{1,0:T(8,128)(2,1)S(1)} %bitcast.16, f32[4,128]{1,0:T(4,128)S(1)} %collective-permute-done.1.side_ref, s32[4,112]{1,0:T(4,128)S(1)} %bitcast.17), custom_call_target="tpu_custom_call" | custom-call | flops 1024 | bytes 1024 | tf_op jit(solution)/shard_map/backward/pallas_call | solution.py:154
  22.5 1.8 %collective-permute-start.5 = (bf16[112,1280]{1,0:T(8,128)(2,1)S(1)}, bf16[112,1280]{1,0:T(8,128)(2,1)S(1)}, u32[]{:S(2)}, u32[]{:S(2)}) collective-permute-start(bf16[112,1280]{1,0:T(8,128)(2,1)S(1)} %get-tuple-element.22), channel_id=1, source_target_pairs={{0,24},{8,0},{16,8},{24,16},{1,25},{9,1},{17,9},{25,17},{2,26},{10... | collective-permute-start | bytes 860168 | tf_op jit(solution)/shard_map/ppermute | solution.py:214
  24.3 3.4 %collective-permute-start.4 = (bf16[112,1280]{1,0:T(8,128)(2,1)S(1)}, bf16[112,1280]{1,0:T(8,128)(2,1)S(1)}, u32[]{:S(2)}, u32[]{:S(2)}) collective-permute-start(bf16[112,1280]{1,0:T(8,128)(2,1)S(1)} %get-tuple-element.21), channel_id=1, source_target_pairs={{0,16},{16,0},{1,17},{17,1},{2,18},{18,2},{3,19},{19,3},{4,20},{20... | collective-permute-start | bytes 860168 | tf_op jit(solution)/shard_map/ppermute | solution.py:214
  27.7 0.1 collective-permute-start.6
  27.8 1.1 %collective-permute-done.6 = f32[2,128]{1,0:T(2,128)S(1)} collective-permute-done((f32[2,128]{1,0:T(2,128)S(1)}, f32[2,128]{1,0:T(2,128)S(1)}, u32[]{:S(2)}, u32[]{:S(2)}) %collective-permute-start.6) | collective-permute-done | bytes 1056 | tf_op jit(solution)/shard_map/ppermute | solution.py:232
  28.9 1.6 %collective-permute-start.7 = (f32[2,128]{1,0:T(2,128)S(1)}, f32[2,128]{1,0:T(2,128)S(1)}, u32[]{:S(2)}, u32[]{:S(2)}) collective-permute-start(f32[2,128]{1,0:T(2,128)S(1)} %add.9), channel_id=1, source_target_pairs={{0,2},{1,3},{2,0},{3,1},{4,6},{5,7},{6,4},{7,5},{8,10},{9,11},{10,... | collective-permute-start | bytes 3080 | tf_op jit(solution)/shard_map/ppermute | solution.py:232
  30.5 0.0 collective-permute-done.packed_ref
  30.5 0.7 %collective-permute-start.2 = (bf16[112,2560]{1,0:T(8,128)(2,1)S(1)}, bf16[112,2560]{1,0:T(8,128)(2,1)S(1)}, u32[]{:S(2)}, u32[]{:S(2)}) collective-permute-start(bf16[112,2560]{1,0:T(8,128)(2,1)S(1)} %collective-permute-done.packed_ref), channel_id=1, source_target_pairs={{0,0},{8,24},{16,16},{24,8},{1,1},{9,25},{17,17},{25,9},{2,2},{10,... | collective-permute-start | bytes 1720328 | tf_op jit(solution)/shard_map/ppermute | solution.py:214
  31.2 1.3 %collective-permute-done.7 = f32[2,128]{1,0:T(2,128)S(1)} collective-permute-done((f32[2,128]{1,0:T(2,128)S(1)}, f32[2,128]{1,0:T(2,128)S(1)}, u32[]{:S(2)}, u32[]{:S(2)}) %collective-permute-start.7) | collective-permute-done | bytes 1056 | tf_op jit(solution)/shard_map/ppermute | solution.py:232
  32.5 0.0 collective-permute-done.5.second_ref
  32.5 0.8 %collective-permute-done.4 = bf16[112,1280]{1,0:T(8,128)(2,1)S(1)} collective-permute-done((bf16[112,1280]{1,0:T(8,128)(2,1)S(1)}, bf16[112,1280]{1,0:T(8,128)(2,1)S(1)}, u32[]{:S(2)}, u32[]{:S(2)}) %collective-permute-start.4) | collective-permute-done | bytes 286752 | tf_op jit(solution)/shard_map/ppermute | solution.py:214
  33.3 0.1 collective-permute-start.10
  33.4 5.0 %collective-permute-start.9 = (f32[2,128]{1,0:T(2,128)S(1)}, f32[2,128]{1,0:T(2,128)S(1)}, u32[]{:S(2)}, u32[]{:S(2)}) collective-permute-start(f32[2,128]{1,0:T(2,128)S(1)} %add.10), channel_id=1, source_target_pairs={{0,28},{1,29},{2,30},{3,31},{4,24},{5,25},{6,26},{7,27},{8,4},{9,5... | collective-permute-start | bytes 3080 | tf_op jit(solution)/shard_map/ppermute | solution.py:240
  38.4 0.1 collective-permute-start.8
  38.5 1.8 %forward.1 = bf16[112,2048]{1,0:T(8,128)(2,1)} custom-call(bf16[112,2560]{1,0:T(8,128)(2,1)S(1)} %collective-permute-done.packed_ref, f32[4,128]{1,0:T(4,128)S(1)} %collective-permute-done.1.side_ref, s32[4,112]{1,0:T(4,128)S(1)} %bitcast.18), custom_call_target="tpu_custom_call" | custom-call | flops 1024 | bytes 1024 | tf_op jit(solution)/shard_map/forward/pallas_call | solution.py:140
  40.3 0.4 collective-permute-done.10.first_ref
  40.7 0.8 %merge.1 = (bf16[112,2048]{1,0:T(8,128)(2,1)}, bf16[112,512]{1,0:T(8,128)(2,1)}) custom-call(bf16[112,1280]{1,0:T(8,128)(2,1)S(1)} %collective-permute-done.10.first_ref, bf16[112,1280]{1,0:T(8,128)(2,1)S(1)} %collective-permute-done.5.second_ref), custom_call_target="tpu_custom_call" | custom-call | flops 1024 | bytes 1024 | tf_op jit(solution)/shard_map/merge/pallas_call | solution.py:192
  41.6 0.0 collective-permute-done.9
  41.6 0.4 collective-permute-done.8
  42.0 0.6 %multiply_bitcast_fusion = f32[1,2,128]{2,1,0:T(2,128)} fusion(f32[2,128]{1,0:T(2,128)S(1)} %collective-permute-done.8, f32[2,128]{1,0:T(2,128)S(1)} %collective-permute-done.9), kind=kLoop, calls=%fused_computation.4 | loop fusion | flops 512 | bytes 3072 | tf_op jit(solution)/shard_map/broadcast_in_dim | solution.py:261
  42.5 0.0 collective-permute-done.2.packed_ref
  42.5 0.8 %unpack.1 = (bf16[112,2048]{1,0:T(8,128)(2,1)}, bf16[112,512]{1,0:T(8,128)(2,1)}) custom-call(bf16[112,2560]{1,0:T(8,128)(2,1)S(1)} %collective-permute-done.2.packed_ref), custom_call_target="tpu_custom_call" | custom-call | flops 1024 | bytes 1024 | tf_op jit(solution)/shard_map/unpack/pallas_call | solution.py:173
  (5 shorter events, 0.1 us)
Async XLA Ops:
  0.6 1.9 %copy-start.2 = (bf16[1,112,2048]{2,1,0:T(8,128)(2,1)S(1)}, bf16[1,112,2048]{2,1,0:T(8,128)(2,1)}, u32[]{:S(2)}) copy-start(bf16[1,112,2048]{2,1,0:T(8,128)(2,1)} %param.8) | copy-start | bytes 1376260
  0.6 1.9 %copy-start.3 = (bf16[1,112,512]{2,1,0:T(8,128)(2,1)S(1)}, bf16[1,112,512]{2,1,0:T(8,128)(2,1)}, u32[]{:S(2)}) copy-start(bf16[1,112,512]{2,1,0:T(8,128)(2,1)} %param.9) | copy-start | bytes 344068
  1.8 19.2 %collective-permute-start.3 = (bf16[112,2560]{1,0:T(8,128)(2,1)S(1)}, bf16[112,2560]{1,0:T(8,128)(2,1)S(1)}, u32[]{:S(2)}, u32[]{:S(2)}) collective-permute-start(bf16[112,2560]{1,0:T(8,128)(2,1)S(1)} %pad_maximum_fusion.1), channel_id=1, source_target_pairs={{0,0},{8,24},{16,16},{24,8},{1,1},{9,25},{17,17},{25,9},{2,2},{10,... | collective-permute-start | bytes 1720328 | tf_op jit(solution)/shard_map/ppermute | solution.py:214
  2.6 5.8 %copy-start.5 = (s32[1,2]{1,0:T(1,128)S(1)}, s32[1,2]{1,0:T(1,128)}, u32[]{:S(2)}) copy-start(s32[1,2]{1,0:T(1,128)} %param.14) | copy-start | bytes 28
  2.6 5.9 %copy-start.4 = (f32[1,2,128]{2,1,0:T(2,128)S(1)}, f32[1,2,128]{2,1,0:T(2,128)}, u32[]{:S(2)}) copy-start(f32[1,2,128]{2,1,0:T(2,128)} %param.13) | copy-start | bytes 3076
  2.6 18.5 %copy-start = (bf16[1,112,2048]{2,1,0:T(8,128)(2,1)S(1)}, bf16[1,112,2048]{2,1,0:T(8,128)(2,1)}, u32[]{:S(2)}) copy-start(bf16[1,112,2048]{2,1,0:T(8,128)(2,1)} %param.12) | copy-start | bytes 1376260
  2.6 18.5 %copy-start.1 = (s32[1,4,112]{2,1,0:T(4,128)S(1)}, s32[1,4,112]{2,1,0:T(4,128)}, u32[]{:S(2)}) copy-start(s32[1,4,112]{2,1,0:T(4,128)} %param.15) | copy-start | bytes 5380
  2.6 27.9 %collective-permute-start = (bf16[112,2560]{1,0:T(8,128)(2,1)S(1)}, bf16[112,2560]{1,0:T(8,128)(2,1)S(1)}, u32[]{:S(2)}, u32[]{:S(2)}) collective-permute-start(bf16[112,2560]{1,0:T(8,128)(2,1)S(1)} %pad_maximum_fusion), channel_id=1, source_target_pairs={{0,8},{8,16},{16,24},{24,0},{1,9},{9,17},{17,25},{25,1},{2,10},{10... | collective-permute-start | bytes 1720328 | tf_op jit(solution)/shard_map/ppermute | solution.py:214
  8.5 12.5 %collective-permute-start.1 = (f32[4,128]{1,0:T(4,128)S(1)}, f32[4,128]{1,0:T(4,128)S(1)}, u32[]{:S(2)}, u32[]{:S(2)}) collective-permute-start(f32[4,128]{1,0:T(4,128)S(1)} %pad_maximum_fusion.2), channel_id=1, source_target_pairs={{0,8},{8,16},{16,24},{24,0},{1,9},{9,17},{17,25},{25,1},{2,10},{10... | collective-permute-start | bytes 6152 | tf_op jit(solution)/shard_map/ppermute | solution.py:214
  22.5 10.0 %collective-permute-start.5 = (bf16[112,1280]{1,0:T(8,128)(2,1)S(1)}, bf16[112,1280]{1,0:T(8,128)(2,1)S(1)}, u32[]{:S(2)}, u32[]{:S(2)}) collective-permute-start(bf16[112,1280]{1,0:T(8,128)(2,1)S(1)} %get-tuple-element.22), channel_id=1, source_target_pairs={{0,24},{8,0},{16,8},{24,16},{1,25},{9,1},{17,9},{25,17},{2,26},{10... | collective-permute-start | bytes 860168 | tf_op jit(solution)/shard_map/ppermute | solution.py:214
  24.3 9.0 %collective-permute-start.4 = (bf16[112,1280]{1,0:T(8,128)(2,1)S(1)}, bf16[112,1280]{1,0:T(8,128)(2,1)S(1)}, u32[]{:S(2)}, u32[]{:S(2)}) collective-permute-start(bf16[112,1280]{1,0:T(8,128)(2,1)S(1)} %get-tuple-element.21), channel_id=1, source_target_pairs={{0,16},{16,0},{1,17},{17,1},{2,18},{18,2},{3,19},{19,3},{4,20},{20... | collective-permute-start | bytes 860168 | tf_op jit(solution)/shard_map/ppermute | solution.py:214
  27.7 1.2 %collective-permute-start.6 = (f32[2,128]{1,0:T(2,128)S(1)}, f32[2,128]{1,0:T(2,128)S(1)}, u32[]{:S(2)}, u32[]{:S(2)}) collective-permute-start(f32[2,128]{1,0:T(2,128)S(1)} %get-tuple-element.23), channel_id=1, source_target_pairs={{0,1},{1,0},{2,3},{3,2},{4,5},{5,4},{6,7},{7,6},{8,9},{9,8},{10,11... | collective-permute-start | bytes 3080 | tf_op jit(solution)/shard_map/ppermute | solution.py:232
  28.9 3.6 %collective-permute-start.7 = (f32[2,128]{1,0:T(2,128)S(1)}, f32[2,128]{1,0:T(2,128)S(1)}, u32[]{:S(2)}, u32[]{:S(2)}) collective-permute-start(f32[2,128]{1,0:T(2,128)S(1)} %add.9), channel_id=1, source_target_pairs={{0,2},{1,3},{2,0},{3,1},{4,6},{5,7},{6,4},{7,5},{8,10},{9,11},{10,... | collective-permute-start | bytes 3080 | tf_op jit(solution)/shard_map/ppermute | solution.py:232
  30.5 12.0 %collective-permute-start.2 = (bf16[112,2560]{1,0:T(8,128)(2,1)S(1)}, bf16[112,2560]{1,0:T(8,128)(2,1)S(1)}, u32[]{:S(2)}, u32[]{:S(2)}) collective-permute-start(bf16[112,2560]{1,0:T(8,128)(2,1)S(1)} %collective-permute-done.packed_ref), channel_id=1, source_target_pairs={{0,0},{8,24},{16,16},{24,8},{1,1},{9,25},{17,17},{25,9},{2,2},{10,... | collective-permute-start | bytes 1720328 | tf_op jit(solution)/shard_map/ppermute | solution.py:214
  33.3 7.4 %collective-permute-start.10 = (bf16[112,1280]{1,0:T(8,128)(2,1)S(1)}, bf16[112,1280]{1,0:T(8,128)(2,1)S(1)}, u32[]{:S(2)}, u32[]{:S(2)}) collective-permute-start(bf16[112,1280]{1,0:T(8,128)(2,1)S(1)} %broadcast_select_fusion), channel_id=1, source_target_pairs={{16,24},{0,8},{8,0},{24,16},{17,25},{1,9},{9,1},{25,17},{18,26},{2... | collective-permute-start | bytes 860168 | tf_op jit(solution)/shard_map/ppermute | solution.py:214
  33.4 8.2 %collective-permute-start.9 = (f32[2,128]{1,0:T(2,128)S(1)}, f32[2,128]{1,0:T(2,128)S(1)}, u32[]{:S(2)}, u32[]{:S(2)}) collective-permute-start(f32[2,128]{1,0:T(2,128)S(1)} %add.10), channel_id=1, source_target_pairs={{0,28},{1,29},{2,30},{3,31},{4,24},{5,25},{6,26},{7,27},{8,4},{9,5... | collective-permute-start | bytes 3080 | tf_op jit(solution)/shard_map/ppermute | solution.py:240
  38.4 3.6 %collective-permute-start.8 = (f32[2,128]{1,0:T(2,128)S(1)}, f32[2,128]{1,0:T(2,128)S(1)}, u32[]{:S(2)}, u32[]{:S(2)}) collective-permute-start(f32[2,128]{1,0:T(2,128)S(1)} %add.10), channel_id=1, source_target_pairs={{0,24},{1,25},{2,26},{3,27},{4,28},{5,29},{6,30},{7,31},{8,0},{9,1... | collective-permute-start | bytes 3080 | tf_op jit(solution)/shard_map/ppermute | solution.py:240

commit v6 on v5

--- a/solution.py
+++ b/solution.py
@@ -163,22 +163,22 @@
     )(packed, upstream, side, segments)
 
 
-def unpack_kernel(packed_ref, q_ref, kv_ref):
+def unpack_kernel(share, packed_ref, here_ref, there_ref, q_ref, kv_ref, gain_ref):
     q_width = q_ref.shape[1]
     q_ref[...] = packed_ref[:, :q_width]
     kv_ref[...] = packed_ref[:, q_width : q_width + kv_ref.shape[1]]
-
-
-def unpack(packed, widths):
-    return pl.pallas_call(
-        unpack_kernel,
-        out_shape=[
-            jax.ShapeDtypeStruct((packed.shape[0], width), packed.dtype) for width in widths
-        ],
+    gain_ref[...] = (here_ref[...] + there_ref[...]) * share
+
+
+def unpack(packed, halves, widths, share):
+    shapes = [jax.ShapeDtypeStruct((packed.shape[0], width), packed.dtype) for width in widths]
+    return pl.pallas_call(
+        functools.partial(unpack_kernel, share),
+        out_shape=shapes + [jax.ShapeDtypeStruct(halves[0].shape, halves[0].dtype)],
         cost_estimate=cost(1024),
         compiler_params=pltpu.CompilerParams(vmem_limit_bytes=VMEM_LIMIT),
         name="unpack",
-    )(packed)
+    )(packed, *halves)
 
 
 def merge_kernel(first_ref, second_ref, q_ref, kv_ref):
@@ -248,10 +248,9 @@
         )
         for other in (0, step)
     ]
-    stored_q, stored_kv = unpack(stored, widths)
     grad_q, grad_kv = merge((first, second), widths)
-    *halves, grad_q = lax.optimization_barrier((*halves, grad_q))
-    gain = (halves[0] + halves[1]) * (1.0 / replicas)
+    stored, grad_q = lax.optimization_barrier((stored, grad_q))
+    stored_q, stored_kv, gain = unpack(stored, halves, widths, 1.0 / replicas)
     return (
         attention_out[None],
         stored_q[None],

time: 43.6 us -> 43.3 us (level)
  other arithmetic: 1.89 us -> 1.32 us
    broadcast_in_dim x1 -> x0, other arithmetic: 0.57 us -> none  [local(): gain[None]]
  transfers between devices with their start and end apart: 11 -> 11, of which waited for: 6 -> 6; matrix products, arithmetic and copies ran while one was open for 2% -> 1% of each run, Pallas kernels for 9% -> 10%
where the time goes in v6:
time: 43.3 us; the launch traced here: 42.8 us
  starting transfers between devices  19.6 us (45%)
  waiting for transfers between devices  16 us (37%)
  Pallas kernels  4.97 us (11%)
  other arithmetic  1.32 us (3%)
  between operations  0.78 us (2%)
    ppermute x7, waiting for transfers between devices, hop(): return lax.ppermute(value, 'section', pairs)  13.2 us
    ppermute x7, starting transfers between devices, hop(): return lax.ppermute(value, 'section', pairs)  12.9 us
    ppermute x2, starting transfers between devices, local(): lax.ppermute(gain, ('section', 'dp'), [(i * replicas + j, (i - 1) % secti...  5.06 us
    ppermute x2, waiting for transfers between devices, local(): lax.ppermute(gain, 'dp', [(i, i ^ step) for i in range(replicas)])  2.42 us
    pallas_call x1, Pallas kernels, forward(): pl.pallas_call(forward_kernel, out_shape=jax.ShapeDtypeStruct((fresh.shap...  1.84 us
    ppermute x2, starting transfers between devices, local(): lax.ppermute(gain, 'dp', [(i, i ^ step) for i in range(replicas)])  1.65 us
    pallas_call x1, Pallas kernels, backward(): pl.pallas_call(backward_kernel, out_shape=[jax.ShapeDtypeStruct((tokens,...  1.44 us
    concatenate x1, other arithmetic, local(): jnp.concatenate([held_q[0], retained_key_value[0]], axis=1)  1.17 us
  transfers between devices with their start and end apart: 11, of which 6 were waited for; matrix products, arithmetic and copies ran while one was open for 1% of the time, Pallas kernels for 10%

profile of v6, /device:TPU:0, one launch (start us, length us, event | category | flops | bytes accessed | tf_op | source)
XLA Modules:
  0.0 42.8 jit_solution(17721502270785486067)
XLA Ops:
  0.6 0.0 copy-start.2
  0.6 0.0 copy-start.3
  0.7 1.2 %pad_maximum_fusion.1 = bf16[112,2560]{1,0:T(8,128)(2,1)S(1)} fusion(bf16[112,512]{1,0:T(8,128)(2,1)} %bitcast.21, bf16[112,2048]{1,0:T(8,128)(2,1)} %bitcast.18), kind=kLoop, calls=%fused_computation.1 | loop fusion | flops 1146880 | bytes 1146880 | tf_op jit(solution)/shard_map/concatenate | solution.py:218
  1.8 0.7 %collective-permute-start.3 = (bf16[112,2560]{1,0:T(8,128)(2,1)S(1)}, bf16[112,2560]{1,0:T(8,128)(2,1)S(1)}, u32[]{:S(2)}, u32[]{:S(2)}) collective-permute-start(bf16[112,2560]{1,0:T(8,128)(2,1)S(1)} %pad_maximum_fusion.1), channel_id=1, source_target_pairs={{0,0},{8,24},{16,16},{24,8},{1,1},{9,25},{17,17},{25,9},{2,2},{10,... | collective-permute-start | bytes 1720328 | tf_op jit(solution)/shard_map/ppermute | solution.py:214
  2.5 0.0 copy-done.2
  2.5 0.0 copy-done.3
  2.6 0.0 copy-start.5
  2.6 0.0 copy-start.4
  2.6 0.0 copy-start
  2.6 0.0 copy-start.1
  2.6 5.7 %collective-permute-start = (bf16[112,2560]{1,0:T(8,128)(2,1)S(1)}, bf16[112,2560]{1,0:T(8,128)(2,1)S(1)}, u32[]{:S(2)}, u32[]{:S(2)}) collective-permute-start(bf16[112,2560]{1,0:T(8,128)(2,1)S(1)} %pad_maximum_fusion), channel_id=1, source_target_pairs={{0,8},{8,16},{16,24},{24,0},{1,9},{9,17},{17,25},{25,1},{2,10},{10... | collective-permute-start | bytes 1720328 | tf_op jit(solution)/shard_map/ppermute | solution.py:214
  8.4 0.0 copy-done.5
  8.4 0.1 pad.3.clone
  8.5 0.0 copy-done.4
  8.5 0.1 pad_maximum_fusion.2
  8.5 0.5 %collective-permute-start.1 = (f32[4,128]{1,0:T(4,128)S(1)}, f32[4,128]{1,0:T(4,128)S(1)}, u32[]{:S(2)}, u32[]{:S(2)}) collective-permute-start(f32[4,128]{1,0:T(4,128)S(1)} %pad_maximum_fusion.2), channel_id=1, source_target_pairs={{0,8},{8,16},{16,24},{24,0},{1,9},{9,17},{17,25},{25,1},{2,10},{10... | collective-permute-start | bytes 6152 | tf_op jit(solution)/shard_map/ppermute | solution.py:214
  9.0 12.0 %collective-permute-done.1.side_ref = f32[4,128]{1,0:T(4,128)S(1)} collective-permute-done((f32[4,128]{1,0:T(4,128)S(1)}, f32[4,128]{1,0:T(4,128)S(1)}, u32[]{:S(2)}, u32[]{:S(2)}) %collective-permute-start.1) | collective-permute-done | bytes 2080 | tf_op jit(solution)/shard_map/ppermute | solution.py:214
  21.1 0.0 collective-permute-done.3.packed_ref
  21.1 0.0 copy-done
  21.1 0.0 copy-done.1
  21.1 1.4 %backward.1 = (bf16[112,1280]{1,0:T(8,128)(2,1)S(1)}, bf16[112,1280]{1,0:T(8,128)(2,1)S(1)}, f32[2,128]{1,0:T(2,128)S(1)}) custom-call(bf16[112,2560]{1,0:T(8,128)(2,1)S(1)} %collective-permute-done.3.packed_ref, bf16[112,2048]{1,0:T(8,128)(2,1)S(1)} %bitcast.15, f32[4,128]{1,0:T(4,128)S(1)} %collective-permute-done.1.side_ref, s32[4,112]{1,0:T(4,128)S(1)} %bitcast.16), custom_call_target="tpu_custom_call" | custom-call | flops 1024 | bytes 1024 | tf_op jit(solution)/shard_map/backward/pallas_call | solution.py:154
  22.5 1.8 %collective-permute-start.5 = (bf16[112,1280]{1,0:T(8,128)(2,1)S(1)}, bf16[112,1280]{1,0:T(8,128)(2,1)S(1)}, u32[]{:S(2)}, u32[]{:S(2)}) collective-permute-start(bf16[112,1280]{1,0:T(8,128)(2,1)S(1)} %get-tuple-element.20), channel_id=1, source_target_pairs={{0,24},{8,0},{16,8},{24,16},{1,25},{9,1},{17,9},{25,17},{2,26},{10... | collective-permute-start | bytes 860168 | tf_op jit(solution)/shard_map/ppermute | solution.py:214
  24.3 3.4 %collective-permute-start.4 = (bf16[112,1280]{1,0:T(8,128)(2,1)S(1)}, bf16[112,1280]{1,0:T(8,128)(2,1)S(1)}, u32[]{:S(2)}, u32[]{:S(2)}) collective-permute-start(bf16[112,1280]{1,0:T(8,128)(2,1)S(1)} %get-tuple-element.19), channel_id=1, source_target_pairs={{0,16},{16,0},{1,17},{17,1},{2,18},{18,2},{3,19},{19,3},{4,20},{20... | collective-permute-start | bytes 860168 | tf_op jit(solution)/shard_map/ppermute | solution.py:214
  27.7 0.1 collective-permute-start.6
  27.8 1.1 %collective-permute-done.6 = f32[2,128]{1,0:T(2,128)S(1)} collective-permute-done((f32[2,128]{1,0:T(2,128)S(1)}, f32[2,128]{1,0:T(2,128)S(1)}, u32[]{:S(2)}, u32[]{:S(2)}) %collective-permute-start.6) | collective-permute-done | bytes 1056 | tf_op jit(solution)/shard_map/ppermute | solution.py:232
  28.9 1.6 %collective-permute-start.7 = (f32[2,128]{1,0:T(2,128)S(1)}, f32[2,128]{1,0:T(2,128)S(1)}, u32[]{:S(2)}, u32[]{:S(2)}) collective-permute-start(f32[2,128]{1,0:T(2,128)S(1)} %add.6), channel_id=1, source_target_pairs={{0,2},{1,3},{2,0},{3,1},{4,6},{5,7},{6,4},{7,5},{8,10},{9,11},{10,... | collective-permute-start | bytes 3080 | tf_op jit(solution)/shard_map/ppermute | solution.py:232
  30.5 0.0 collective-permute-done.packed_ref
  30.5 0.7 %collective-permute-start.2 = (bf16[112,2560]{1,0:T(8,128)(2,1)S(1)}, bf16[112,2560]{1,0:T(8,128)(2,1)S(1)}, u32[]{:S(2)}, u32[]{:S(2)}) collective-permute-start(bf16[112,2560]{1,0:T(8,128)(2,1)S(1)} %collective-permute-done.packed_ref), channel_id=1, source_target_pairs={{0,0},{8,24},{16,16},{24,8},{1,1},{9,25},{17,17},{25,9},{2,2},{10,... | collective-permute-start | bytes 1720328 | tf_op jit(solution)/shard_map/ppermute | solution.py:214
  31.2 1.3 %collective-permute-done.7 = f32[2,128]{1,0:T(2,128)S(1)} collective-permute-done((f32[2,128]{1,0:T(2,128)S(1)}, f32[2,128]{1,0:T(2,128)S(1)}, u32[]{:S(2)}, u32[]{:S(2)}) %collective-permute-start.7) | collective-permute-done | bytes 1056 | tf_op jit(solution)/shard_map/ppermute | solution.py:232
  32.5 0.0 collective-permute-done.5.second_ref
  32.5 0.8 %collective-permute-done.4 = bf16[112,1280]{1,0:T(8,128)(2,1)S(1)} collective-permute-done((bf16[112,1280]{1,0:T(8,128)(2,1)S(1)}, bf16[112,1280]{1,0:T(8,128)(2,1)S(1)}, u32[]{:S(2)}, u32[]{:S(2)}) %collective-permute-start.4) | collective-permute-done | bytes 286752 | tf_op jit(solution)/shard_map/ppermute | solution.py:214
  33.3 0.1 collective-permute-start.8
  33.4 5.0 %collective-permute-start.10 = (f32[2,128]{1,0:T(2,128)S(1)}, f32[2,128]{1,0:T(2,128)S(1)}, u32[]{:S(2)}, u32[]{:S(2)}) collective-permute-start(f32[2,128]{1,0:T(2,128)S(1)} %add.7), channel_id=1, source_target_pairs={{0,28},{1,29},{2,30},{3,31},{4,24},{5,25},{6,26},{7,27},{8,4},{9,5... | collective-permute-start | bytes 3080 | tf_op jit(solution)/shard_map/ppermute | solution.py:240
  38.4 0.1 collective-permute-start.9
  38.5 1.8 %forward.1 = bf16[112,2048]{1,0:T(8,128)(2,1)} custom-call(bf16[112,2560]{1,0:T(8,128)(2,1)S(1)} %collective-permute-done.packed_ref, f32[4,128]{1,0:T(4,128)S(1)} %collective-permute-done.1.side_ref, s32[4,112]{1,0:T(4,128)S(1)} %bitcast.17), custom_call_target="tpu_custom_call" | custom-call | flops 1024 | bytes 1024 | tf_op jit(solution)/shard_map/forward/pallas_call | solution.py:140
  40.3 0.4 collective-permute-done.8.first_ref
  40.7 0.8 %merge.1 = (bf16[112,2048]{1,0:T(8,128)(2,1)}, bf16[112,512]{1,0:T(8,128)(2,1)}) custom-call(bf16[112,1280]{1,0:T(8,128)(2,1)S(1)} %collective-permute-done.8.first_ref, bf16[112,1280]{1,0:T(8,128)(2,1)S(1)} %collective-permute-done.5.second_ref), custom_call_target="tpu_custom_call" | custom-call | flops 1024 | bytes 1024 | tf_op jit(solution)/shard_map/merge/pallas_call | solution.py:192
  41.6 0.0 collective-permute-done.2.packed_ref
  41.6 0.0 collective-permute-done.10.there_ref
  41.6 0.4 collective-permute-done.9.here_ref
  42.0 0.8 %unpack.1 = (bf16[112,2048]{1,0:T(8,128)(2,1)}, bf16[112,512]{1,0:T(8,128)(2,1)}, f32[2,128]{1,0:T(2,128)}) custom-call(bf16[112,2560]{1,0:T(8,128)(2,1)S(1)} %collective-permute-done.2.packed_ref, f32[2,128]{1,0:T(2,128)S(1)} %collective-permute-done.9.here_ref, f32[2,128]{1,0:T(2,128)S(1)} %collective-permute-done.10.there_ref), custom_call_target="tpu_custom_call" | custom-call | flops 1024 | bytes 1024 | tf_op jit(solution)/shard_map/unpack/pallas_call | solution.py:175
  (5 shorter events, 0.1 us)
Async XLA Ops:
  0.6 1.9 %copy-start.2 = (bf16[1,112,2048]{2,1,0:T(8,128)(2,1)S(1)}, bf16[1,112,2048]{2,1,0:T(8,128)(2,1)}, u32[]{:S(2)}) copy-start(bf16[1,112,2048]{2,1,0:T(8,128)(2,1)} %param.8) | copy-start | bytes 1376260
  0.6 1.9 %copy-start.3 = (bf16[1,112,512]{2,1,0:T(8,128)(2,1)S(1)}, bf16[1,112,512]{2,1,0:T(8,128)(2,1)}, u32[]{:S(2)}) copy-start(bf16[1,112,512]{2,1,0:T(8,128)(2,1)} %param.9) | copy-start | bytes 344068
  1.8 19.2 %collective-permute-start.3 = (bf16[112,2560]{1,0:T(8,128)(2,1)S(1)}, bf16[112,2560]{1,0:T(8,128)(2,1)S(1)}, u32[]{:S(2)}, u32[]{:S(2)}) collective-permute-start(bf16[112,2560]{1,0:T(8,128)(2,1)S(1)} %pad_maximum_fusion.1), channel_id=1, source_target_pairs={{0,0},{8,24},{16,16},{24,8},{1,1},{9,25},{17,17},{25,9},{2,2},{10,... | collective-permute-start | bytes 1720328 | tf_op jit(solution)/shard_map/ppermute | solution.py:214
  2.6 5.8 %copy-start.5 = (s32[1,2]{1,0:T(1,128)S(1)}, s32[1,2]{1,0:T(1,128)}, u32[]{:S(2)}) copy-start(s32[1,2]{1,0:T(1,128)} %param.14) | copy-start | bytes 28
  2.6 5.9 %copy-start.4 = (f32[1,2,128]{2,1,0:T(2,128)S(1)}, f32[1,2,128]{2,1,0:T(2,128)}, u32[]{:S(2)}) copy-start(f32[1,2,128]{2,1,0:T(2,128)} %param.13) | copy-start | bytes 3076
  2.6 18.5 %copy-start = (bf16[1,112,2048]{2,1,0:T(8,128)(2,1)S(1)}, bf16[1,112,2048]{2,1,0:T(8,128)(2,1)}, u32[]{:S(2)}) copy-start(bf16[1,112,2048]{2,1,0:T(8,128)(2,1)} %param.12) | copy-start | bytes 1376260
  2.6 18.5 %copy-start.1 = (s32[1,4,112]{2,1,0:T(4,128)S(1)}, s32[1,4,112]{2,1,0:T(4,128)}, u32[]{:S(2)}) copy-start(s32[1,4,112]{2,1,0:T(4,128)} %param.15) | copy-start | bytes 5380
  2.6 27.9 %collective-permute-start = (bf16[112,2560]{1,0:T(8,128)(2,1)S(1)}, bf16[112,2560]{1,0:T(8,128)(2,1)S(1)}, u32[]{:S(2)}, u32[]{:S(2)}) collective-permute-start(bf16[112,2560]{1,0:T(8,128)(2,1)S(1)} %pad_maximum_fusion), channel_id=1, source_target_pairs={{0,8},{8,16},{16,24},{24,0},{1,9},{9,17},{17,25},{25,1},{2,10},{10... | collective-permute-start | bytes 1720328 | tf_op jit(solution)/shard_map/ppermute | solution.py:214
  8.5 12.5 %collective-permute-start.1 = (f32[4,128]{1,0:T(4,128)S(1)}, f32[4,128]{1,0:T(4,128)S(1)}, u32[]{:S(2)}, u32[]{:S(2)}) collective-permute-start(f32[4,128]{1,0:T(4,128)S(1)} %pad_maximum_fusion.2), channel_id=1, source_target_pairs={{0,8},{8,16},{16,24},{24,0},{1,9},{9,17},{17,25},{25,1},{2,10},{10... | collective-permute-start | bytes 6152 | tf_op jit(solution)/shard_map/ppermute | solution.py:214
  22.5 10.0 %collective-permute-start.5 = (bf16[112,1280]{1,0:T(8,128)(2,1)S(1)}, bf16[112,1280]{1,0:T(8,128)(2,1)S(1)}, u32[]{:S(2)}, u32[]{:S(2)}) collective-permute-start(bf16[112,1280]{1,0:T(8,128)(2,1)S(1)} %get-tuple-element.20), channel_id=1, source_target_pairs={{0,24},{8,0},{16,8},{24,16},{1,25},{9,1},{17,9},{25,17},{2,26},{10... | collective-permute-start | bytes 860168 | tf_op jit(solution)/shard_map/ppermute | solution.py:214
  24.3 9.0 %collective-permute-start.4 = (bf16[112,1280]{1,0:T(8,128)(2,1)S(1)}, bf16[112,1280]{1,0:T(8,128)(2,1)S(1)}, u32[]{:S(2)}, u32[]{:S(2)}) collective-permute-start(bf16[112,1280]{1,0:T(8,128)(2,1)S(1)} %get-tuple-element.19), channel_id=1, source_target_pairs={{0,16},{16,0},{1,17},{17,1},{2,18},{18,2},{3,19},{19,3},{4,20},{20... | collective-permute-start | bytes 860168 | tf_op jit(solution)/shard_map/ppermute | solution.py:214
  27.7 1.2 %collective-permute-start.6 = (f32[2,128]{1,0:T(2,128)S(1)}, f32[2,128]{1,0:T(2,128)S(1)}, u32[]{:S(2)}, u32[]{:S(2)}) collective-permute-start(f32[2,128]{1,0:T(2,128)S(1)} %get-tuple-element.21), channel_id=1, source_target_pairs={{0,1},{1,0},{2,3},{3,2},{4,5},{5,4},{6,7},{7,6},{8,9},{9,8},{10,11... | collective-permute-start | bytes 3080 | tf_op jit(solution)/shard_map/ppermute | solution.py:232
  28.9 3.6 %collective-permute-start.7 = (f32[2,128]{1,0:T(2,128)S(1)}, f32[2,128]{1,0:T(2,128)S(1)}, u32[]{:S(2)}, u32[]{:S(2)}) collective-permute-start(f32[2,128]{1,0:T(2,128)S(1)} %add.6), channel_id=1, source_target_pairs={{0,2},{1,3},{2,0},{3,1},{4,6},{5,7},{6,4},{7,5},{8,10},{9,11},{10,... | collective-permute-start | bytes 3080 | tf_op jit(solution)/shard_map/ppermute | solution.py:232
  30.5 11.1 %collective-permute-start.2 = (bf16[112,2560]{1,0:T(8,128)(2,1)S(1)}, bf16[112,2560]{1,0:T(8,128)(2,1)S(1)}, u32[]{:S(2)}, u32[]{:S(2)}) collective-permute-start(bf16[112,2560]{1,0:T(8,128)(2,1)S(1)} %collective-permute-done.packed_ref), channel_id=1, source_target_pairs={{0,0},{8,24},{16,16},{24,8},{1,1},{9,25},{17,17},{25,9},{2,2},{10,... | collective-permute-start | bytes 1720328 | tf_op jit(solution)/shard_map/ppermute | solution.py:214
  33.3 7.4 %collective-permute-start.8 = (bf16[112,1280]{1,0:T(8,128)(2,1)S(1)}, bf16[112,1280]{1,0:T(8,128)(2,1)S(1)}, u32[]{:S(2)}, u32[]{:S(2)}) collective-permute-start(bf16[112,1280]{1,0:T(8,128)(2,1)S(1)} %broadcast_select_fusion), channel_id=1, source_target_pairs={{16,24},{0,8},{8,0},{24,16},{17,25},{1,9},{9,1},{25,17},{18,26},{2... | collective-permute-start | bytes 860168 | tf_op jit(solution)/shard_map/ppermute | solution.py:214
  33.4 8.2 %collective-permute-start.10 = (f32[2,128]{1,0:T(2,128)S(1)}, f32[2,128]{1,0:T(2,128)S(1)}, u32[]{:S(2)}, u32[]{:S(2)}) collective-permute-start(f32[2,128]{1,0:T(2,128)S(1)} %add.7), channel_id=1, source_target_pairs={{0,28},{1,29},{2,30},{3,31},{4,24},{5,25},{6,26},{7,27},{8,4},{9,5... | collective-permute-start | bytes 3080 | tf_op jit(solution)/shard_map/ppermute | solution.py:240
  38.4 3.6 %collective-permute-start.9 = (f32[2,128]{1,0:T(2,128)S(1)}, f32[2,128]{1,0:T(2,128)S(1)}, u32[]{:S(2)}, u32[]{:S(2)}) collective-permute-start(f32[2,128]{1,0:T(2,128)S(1)} %add.7), channel_id=1, source_target_pairs={{0,24},{1,25},{2,26},{3,27},{4,28},{5,29},{6,30},{7,31},{8,0},{9,1... | collective-permute-start | bytes 3080 | tf_op jit(solution)/shard_map/ppermute | solution.py:240

commit v7 on v6

--- a/solution.py
+++ b/solution.py
@@ -14,7 +14,6 @@
 EXP2_SCALE = SCORE_SCALE * math.log2(math.e)
 
 VMEM_LIMIT = 16 << 20
-CUT_NUM, CUT_DEN = 10, 20
 NT = (((1,), (1,)), ((), ()))
 TN = (((0,), (0,)), ((), ()))
 NN = (((1,), (0,)), ((), ()))
@@ -86,47 +85,34 @@
     return jnp.sum(terms.reshape(-1, 8, terms.shape[1]), axis=0)
 
 
-def backward_kernel(packed_ref, up_ref, side_ref, segment_ref, *outs):
-    *grad_refs, gain_ref = outs
-
-    def write(block, value):
-        first = grad_refs[0].shape[1] // HEAD_SIZE
-        ref, at = (grad_refs[0], block) if block < first else (grad_refs[1], block - first)
-        ref[:, at * HEAD_SIZE : (at + 1) * HEAD_SIZE] = value.astype(jnp.bfloat16)
-
-    side = side_ref[...]
+def backward_kernel(g, kv_heads, packed_ref, up_ref, side_ref, segment_ref, grad_ref, gain_ref):
     tokens = packed_ref.shape[0]
     heads = up_ref.shape[1] // HEAD_SIZE
-    kv_heads = (packed_ref.shape[1] // HEAD_SIZE - heads) // 2
     per_kv = heads // kv_heads
-    allowed = allowed_pairs(segment_ref, side[3:4], per_kv)
-    q_gain, k_gain = side[0:1], side[1:2]
-    q_terms = k_terms = 0.0
-    for g in range(kv_heads):
-        key_hat, key_factor = normalized(head(packed_ref, heads + g))
-        key = (key_hat * k_gain).astype(jnp.bfloat16)
-        value = head(packed_ref, heads + kv_heads + g)
-        query_hat, query_factor = normalized(stacked(packed_ref, g * per_kv, per_kv))
-        query = (query_hat * q_gain).astype(jnp.bfloat16)
-        upstream = stacked(up_ref, g * per_kv, per_kv)
-        probs = probabilities(key, query, allowed)
-        d_probs = dot(value, upstream, NT)
-        d_value = dot(probs.astype(jnp.bfloat16), upstream, NN)
-        centre = jnp.sum(probs * d_probs, axis=0, keepdims=True)
-        d_scores = (probs * (d_probs - centre)).astype(jnp.bfloat16)
-        d_key = dot(d_scores, query, NN)
-        d_query, terms = norm_back(
-            query_hat, query_factor, q_gain * SCORE_SCALE, dot(d_scores, key, TN)
-        )
-        q_terms += summed_rows(terms)
-        for i in range(per_kv):
-            write(g * per_kv + i, d_query[i * tokens : (i + 1) * tokens])
-        d_key, terms = norm_back(key_hat, key_factor, k_gain * SCORE_SCALE, d_key)
-        k_terms += summed_rows(terms)
-        write(heads + g, d_key)
-        write(heads + kv_heads + g, d_value)
-    gain_ref[0:1, :] = jnp.sum(q_terms, axis=0, keepdims=True) * SCORE_SCALE
-    gain_ref[1:2, :] = jnp.sum(k_terms, axis=0, keepdims=True) * SCORE_SCALE
+    allowed = allowed_pairs(segment_ref, side_ref[3:4, :], per_kv)
+    q_gain, k_gain = side_ref[0:1, :], side_ref[1:2, :]
+    key_hat, key_factor = normalized(head(packed_ref, heads + g))
+    key = (key_hat * k_gain).astype(jnp.bfloat16)
+    value = head(packed_ref, heads + kv_heads + g)
+    query_hat, query_factor = normalized(stacked(packed_ref, g * per_kv, per_kv))
+    query = (query_hat * q_gain).astype(jnp.bfloat16)
+    upstream = stacked(up_ref, g * per_kv, per_kv)
+    probs = probabilities(key, query, allowed)
+    d_probs = dot(value, upstream, NT)
+    d_value = dot(probs.astype(jnp.bfloat16), upstream, NN)
+    centre = jnp.sum(probs * d_probs, axis=0, keepdims=True)
+    d_scores = (probs * (d_probs - centre)).astype(jnp.bfloat16)
+    d_key = dot(d_scores, query, NN)
+    d_query, terms = norm_back(query_hat, query_factor, q_gain * SCORE_SCALE, dot(d_scores, key, TN))
+    gain_ref[0:1, :] = jnp.sum(summed_rows(terms), axis=0, keepdims=True) * SCORE_SCALE
+    d_query = d_query.astype(jnp.bfloat16)
+    for i in range(per_kv):
+        grad_ref[:, i * HEAD_SIZE : (i + 1) * HEAD_SIZE] = d_query[i * tokens : (i + 1) * tokens]
+    d_key, terms = norm_back(key_hat, key_factor, k_gain * SCORE_SCALE, d_key)
+    gain_ref[1:2, :] = jnp.sum(summed_rows(terms), axis=0, keepdims=True) * SCORE_SCALE
+    at = per_kv * HEAD_SIZE
+    grad_ref[:, at : at + HEAD_SIZE] = d_key.astype(jnp.bfloat16)
+    grad_ref[:, at + HEAD_SIZE :] = d_value.astype(jnp.bfloat16)
 
 
 def cost(work):
@@ -148,15 +134,16 @@
     )(fresh, side, segments)
 
 
-def backward(packed, upstream, side, segments):
+def backward(g, kv_heads, packed, upstream, side, segments):
     tokens, width = packed.shape
-    cut = width // HEAD_SIZE * CUT_NUM // CUT_DEN * HEAD_SIZE
-    return pl.pallas_call(
-        backward_kernel,
-        out_shape=[jax.ShapeDtypeStruct((tokens, w), packed.dtype) for w in (cut, width - cut)]
-        + [jax.ShapeDtypeStruct((2, HEAD_SIZE), jnp.float32)],
+    return pl.pallas_call(
+        functools.partial(backward_kernel, g, kv_heads),
+        out_shape=[
+            jax.ShapeDtypeStruct((tokens, width // kv_heads), packed.dtype),
+            jax.ShapeDtypeStruct((2, HEAD_SIZE), jnp.float32),
+        ],
         in_specs=[VMEM] * 4,
-        out_specs=[VMEM] * 3,
+        out_specs=[VMEM] * 2,
         cost_estimate=cost(1024),
         compiler_params=pltpu.CompilerParams(vmem_limit_bytes=VMEM_LIMIT),
         name="backward",
@@ -181,11 +168,15 @@
     )(packed, *halves)
 
 
-def merge_kernel(first_ref, second_ref, q_ref, kv_ref):
-    cut, q_width = first_ref.shape[1], q_ref.shape[1]
-    q_ref[:, :cut] = first_ref[...]
-    q_ref[:, cut:] = second_ref[:, : q_width - cut]
-    kv_ref[...] = second_ref[:, q_width - cut :]
+def merge_kernel(*refs):
+    *grad_refs, q_ref, kv_ref = refs
+    kv_heads = len(grad_refs)
+    span = q_ref.shape[1] // kv_heads
+    for g, grad_ref in enumerate(grad_refs):
+        q_ref[:, g * span : (g + 1) * span] = grad_ref[:, :span]
+        for part in range(2):
+            at, start = (part * kv_heads + g) * HEAD_SIZE, span + part * HEAD_SIZE
+            kv_ref[:, at : at + HEAD_SIZE] = grad_ref[:, start : start + HEAD_SIZE]
 
 
 def merge(grads, widths):
@@ -218,7 +209,14 @@
     held = hop(jnp.concatenate([held_q[0], retained_key_value[0]], axis=1), opposite)
     side = hop(jnp.concatenate([norm_gains[0], numbers], axis=0), up)
     stored = hop(fresh, opposite)
-    first, second, gain = backward(held, cotangent[0], side, segments)
+    kv_heads = widths[1] // HEAD_SIZE // 2
+    near, parts = [], []
+    for heads in (range(kv_heads // 2, kv_heads), range(kv_heads // 2)):
+        made = [backward(g, kv_heads, held, cotangent[0], side, segments) for g in heads]
+        near.append([grad for grad, _ in made])
+        parts += [part for _, part in made]
+    second, first = (grads[0] if len(grads) == 1 else jnp.concatenate(grads, axis=1) for grads in near)
+    gain = functools.reduce(jnp.add, parts)
     fixed = [i for i in range(sections) if -i % sections == i]
     across = [(i, (i + sections // 2) % sections) for i in fixed]
     after = [(j, (i - 1) % sections) for i, j in across]
@@ -248,7 +246,11 @@
         )
         for other in (0, step)
     ]
-    grad_q, grad_kv = merge((first, second), widths)
+    span = sum(widths) // kv_heads
+    grads = [
+        whole[:, at : at + span] for whole in (first, second) for at in range(0, whole.shape[1], span)
+    ]
+    grad_q, grad_kv = merge(grads, widths)
     stored, grad_q = lax.optimization_barrier((stored, grad_q))
     stored_q, stored_kv, gain = unpack(stored, halves, widths, 1.0 / replicas)
     return (

time: 43.3 us -> 43.3 us (level)
    pallas_call x1 -> x2, Pallas kernels: 1.44 us -> 1.73 us  [backward(): pl.pallas_call(functools.partial(backward_kernel, g, kv_heads), out_shape...]
where the time goes in v7:
time: 43.3 us; the launch traced here: 43.1 us
  starting transfers between devices  19.6 us (45%)
  waiting for transfers between devices  16 us (37%)
  Pallas kernels  5.27 us (12%)
  other arithmetic  1.33 us (3%)
  between operations  0.78 us (2%)
    ppermute x7, waiting for transfers between devices, hop(): return lax.ppermute(value, 'section', pairs)  13.2 us
    ppermute x7, starting transfers between devices, hop(): return lax.ppermute(value, 'section', pairs)  12.9 us
    ppermute x2, starting transfers between devices, local(): lax.ppermute(gain, ('section', 'dp'), [(i * replicas + j, (i - 1) % secti...  5.06 us
    ppermute x2, waiting for transfers between devices, local(): lax.ppermute(gain, 'dp', [(i, i ^ step) for i in range(replicas)])  2.42 us
    pallas_call x1, Pallas kernels, forward(): pl.pallas_call(forward_kernel, out_shape=jax.ShapeDtypeStruct((fresh.shap...  1.84 us
    pallas_call x2, Pallas kernels, backward(): pl.pallas_call(functools.partial(backward_kernel, g, kv_heads), out_shape...  1.73 us
    ppermute x2, starting transfers between devices, local(): lax.ppermute(gain, 'dp', [(i, i ^ step) for i in range(replicas)])  1.65 us
    concatenate x1, other arithmetic, local(): jnp.concatenate([held_q[0], retained_key_value[0]], axis=1)  1.17 us
  transfers between devices with their start and end apart: 11, of which 6 were waited for; matrix products, arithmetic and copies ran while one was open for 1% of the time, Pallas kernels for 10%

profile of v7, /device:TPU:0, one launch (start us, length us, event | category | flops | bytes accessed | tf_op | source)
XLA Modules:
  0.0 43.1 jit_solution(15920502916567464282)
XLA Ops:
  0.6 0.0 copy-start.2
  0.6 0.0 copy-start.3
  0.7 1.2 %pad_maximum_fusion.1 = bf16[112,2560]{1,0:T(8,128)(2,1)S(1)} fusion(bf16[112,512]{1,0:T(8,128)(2,1)} %bitcast.23, bf16[112,2048]{1,0:T(8,128)(2,1)} %bitcast.20), kind=kLoop, calls=%fused_computation.1 | loop fusion | flops 1146880 | bytes 1146880 | tf_op jit(solution)/shard_map/concatenate | solution.py:209
  1.8 0.7 %collective-permute-start.3 = (bf16[112,2560]{1,0:T(8,128)(2,1)S(1)}, bf16[112,2560]{1,0:T(8,128)(2,1)S(1)}, u32[]{:S(2)}, u32[]{:S(2)}) collective-permute-start(bf16[112,2560]{1,0:T(8,128)(2,1)S(1)} %pad_maximum_fusion.1), channel_id=1, source_target_pairs={{0,0},{8,24},{16,16},{24,8},{1,1},{9,25},{17,17},{25,9},{2,2},{10,... | collective-permute-start | bytes 1720328 | tf_op jit(solution)/shard_map/ppermute | solution.py:205
  2.5 0.0 copy-done.2
  2.5 0.0 copy-done.3
  2.6 0.0 copy-start.5
  2.6 0.0 copy-start.4
  2.6 0.0 copy-start
  2.6 0.0 copy-start.1
  2.6 5.7 %collective-permute-start = (bf16[112,2560]{1,0:T(8,128)(2,1)S(1)}, bf16[112,2560]{1,0:T(8,128)(2,1)S(1)}, u32[]{:S(2)}, u32[]{:S(2)}) collective-permute-start(bf16[112,2560]{1,0:T(8,128)(2,1)S(1)} %pad_maximum_fusion), channel_id=1, source_target_pairs={{0,8},{8,16},{16,24},{24,0},{1,9},{9,17},{17,25},{25,1},{2,10},{10... | collective-permute-start | bytes 1720328 | tf_op jit(solution)/shard_map/ppermute | solution.py:205
  8.4 0.0 copy-done.5
  8.4 0.1 pad.3.clone
  8.5 0.0 copy-done.4
  8.5 0.1 pad_maximum_fusion.2
  8.5 0.5 %collective-permute-start.1 = (f32[4,128]{1,0:T(4,128)S(1)}, f32[4,128]{1,0:T(4,128)S(1)}, u32[]{:S(2)}, u32[]{:S(2)}) collective-permute-start(f32[4,128]{1,0:T(4,128)S(1)} %pad_maximum_fusion.2), channel_id=1, source_target_pairs={{0,8},{8,16},{16,24},{24,0},{1,9},{9,17},{17,25},{25,1},{2,10},{10... | collective-permute-start | bytes 6152 | tf_op jit(solution)/shard_map/ppermute | solution.py:205
  9.0 12.0 %collective-permute-done.1.side_ref = f32[4,128]{1,0:T(4,128)S(1)} collective-permute-done((f32[4,128]{1,0:T(4,128)S(1)}, f32[4,128]{1,0:T(4,128)S(1)}, u32[]{:S(2)}, u32[]{:S(2)}) %collective-permute-start.1) | collective-permute-done | bytes 2080 | tf_op jit(solution)/shard_map/ppermute | solution.py:205
  21.1 0.0 collective-permute-done.3.packed_ref
  21.1 0.0 copy-done
  21.1 0.0 copy-done.1
  21.1 0.9 %backward.3 = (bf16[112,1280]{1,0:T(8,128)(2,1)S(1)}, f32[2,128]{1,0:T(2,128)S(1)}) custom-call(bf16[112,2560]{1,0:T(8,128)(2,1)S(1)} %collective-permute-done.3.packed_ref, bf16[112,2048]{1,0:T(8,128)(2,1)S(1)} %bitcast.15, f32[4,128]{1,0:T(4,128)S(1)} %collective-permute-done.1.side_ref, s32[4,112]{1,0:T(4,128)S(1)} %bitcast.17), custom_call_target="tpu_custom_call" | custom-call | flops 1024 | bytes 1024 | tf_op jit(solution)/shard_map/backward/pallas_call | solution.py:139
  21.9 1.8 %collective-permute-start.5 = (bf16[112,1280]{1,0:T(8,128)(2,1)S(1)}, bf16[112,1280]{1,0:T(8,128)(2,1)S(1)}, u32[]{:S(2)}, u32[]{:S(2)}) collective-permute-start(bf16[112,1280]{1,0:T(8,128)(2,1)S(1)} %get-tuple-element.21), channel_id=1, source_target_pairs={{0,24},{8,0},{16,8},{24,16},{1,25},{9,1},{17,9},{25,17},{2,26},{10... | collective-permute-start | bytes 860168 | tf_op jit(solution)/shard_map/ppermute | solution.py:205
  23.7 0.9 %backward.2 = (bf16[112,1280]{1,0:T(8,128)(2,1)S(1)}, f32[2,128]{1,0:T(2,128)S(1)}) custom-call(bf16[112,2560]{1,0:T(8,128)(2,1)S(1)} %collective-permute-done.3.packed_ref, bf16[112,2048]{1,0:T(8,128)(2,1)S(1)} %bitcast.16, f32[4,128]{1,0:T(4,128)S(1)} %collective-permute-done.1.side_ref, s32[4,112]{1,0:T(4,128)S(1)} %bitcast.18), custom_call_target="tpu_custom_call" | custom-call | flops 1024 | bytes 1024 | tf_op jit(solution)/shard_map/backward/pallas_call | solution.py:139
  24.6 3.4 %collective-permute-start.4 = (bf16[112,1280]{1,0:T(8,128)(2,1)S(1)}, bf16[112,1280]{1,0:T(8,128)(2,1)S(1)}, u32[]{:S(2)}, u32[]{:S(2)}) collective-permute-start(bf16[112,1280]{1,0:T(8,128)(2,1)S(1)} %get-tuple-element.20), channel_id=1, source_target_pairs={{0,16},{16,0},{1,17},{17,1},{2,18},{18,2},{3,19},{19,3},{4,20},{20... | collective-permute-start | bytes 860168 | tf_op jit(solution)/shard_map/ppermute | solution.py:205
  28.0 0.1 collective-permute-start.6
  28.1 1.1 %collective-permute-done.6 = f32[2,128]{1,0:T(2,128)S(1)} collective-permute-done((f32[2,128]{1,0:T(2,128)S(1)}, f32[2,128]{1,0:T(2,128)S(1)}, u32[]{:S(2)}, u32[]{:S(2)}) %collective-permute-start.6) | collective-permute-done | bytes 1056 | tf_op jit(solution)/shard_map/ppermute | solution.py:230
  29.3 1.6 %collective-permute-start.7 = (f32[2,128]{1,0:T(2,128)S(1)}, f32[2,128]{1,0:T(2,128)S(1)}, u32[]{:S(2)}, u32[]{:S(2)}) collective-permute-start(f32[2,128]{1,0:T(2,128)S(1)} %add.10), channel_id=1, source_target_pairs={{0,2},{1,3},{2,0},{3,1},{4,6},{5,7},{6,4},{7,5},{8,10},{9,11},{10,... | collective-permute-start | bytes 3080 | tf_op jit(solution)/shard_map/ppermute | solution.py:230
  30.8 0.0 collective-permute-done.packed_ref
  30.8 0.7 %collective-permute-start.2 = (bf16[112,2560]{1,0:T(8,128)(2,1)S(1)}, bf16[112,2560]{1,0:T(8,128)(2,1)S(1)}, u32[]{:S(2)}, u32[]{:S(2)}) collective-permute-start(bf16[112,2560]{1,0:T(8,128)(2,1)S(1)} %collective-permute-done.packed_ref), channel_id=1, source_target_pairs={{0,0},{8,24},{16,16},{24,8},{1,1},{9,25},{17,17},{25,9},{2,2},{10,... | collective-permute-start | bytes 1720328 | tf_op jit(solution)/shard_map/ppermute | solution.py:205
  31.5 1.3 %collective-permute-done.7 = f32[2,128]{1,0:T(2,128)S(1)} collective-permute-done((f32[2,128]{1,0:T(2,128)S(1)}, f32[2,128]{1,0:T(2,128)S(1)}, u32[]{:S(2)}, u32[]{:S(2)}) %collective-permute-start.7) | collective-permute-done | bytes 1056 | tf_op jit(solution)/shard_map/ppermute | solution.py:230
  32.8 0.0 collective-permute-done.5.refs_1_
  32.8 0.8 %collective-permute-done.4 = bf16[112,1280]{1,0:T(8,128)(2,1)S(1)} collective-permute-done((bf16[112,1280]{1,0:T(8,128)(2,1)S(1)}, bf16[112,1280]{1,0:T(8,128)(2,1)S(1)}, u32[]{:S(2)}, u32[]{:S(2)}) %collective-permute-start.4) | collective-permute-done | bytes 286752 | tf_op jit(solution)/shard_map/ppermute | solution.py:205
  33.6 0.1 collective-permute-start.8
  33.7 5.0 %collective-permute-start.10 = (f32[2,128]{1,0:T(2,128)S(1)}, f32[2,128]{1,0:T(2,128)S(1)}, u32[]{:S(2)}, u32[]{:S(2)}) collective-permute-start(f32[2,128]{1,0:T(2,128)S(1)} %add.11), channel_id=1, source_target_pairs={{0,28},{1,29},{2,30},{3,31},{4,24},{5,25},{6,26},{7,27},{8,4},{9,5... | collective-permute-start | bytes 3080 | tf_op jit(solution)/shard_map/ppermute | solution.py:238
  38.7 0.1 collective-permute-start.9
  38.8 1.8 %forward.1 = bf16[112,2048]{1,0:T(8,128)(2,1)} custom-call(bf16[112,2560]{1,0:T(8,128)(2,1)S(1)} %collective-permute-done.packed_ref, f32[4,128]{1,0:T(4,128)S(1)} %collective-permute-done.1.side_ref, s32[4,112]{1,0:T(4,128)S(1)} %bitcast.19), custom_call_target="tpu_custom_call" | custom-call | flops 1024 | bytes 1024 | tf_op jit(solution)/shard_map/forward/pallas_call | solution.py:126
  40.6 0.4 %collective-permute-done.8.refs_0_ = bf16[112,1280]{1,0:T(8,128)(2,1)S(1)} collective-permute-done((bf16[112,1280]{1,0:T(8,128)(2,1)S(1)}, bf16[112,1280]{1,0:T(8,128)(2,1)S(1)}, u32[]{:S(2)}, u32[]{:S(2)}) %collective-permute-start.8) | collective-permute-done | bytes 286752 | tf_op jit(solution)/shard_map/ppermute | solution.py:205
  41.0 0.8 %merge.1 = (bf16[112,2048]{1,0:T(8,128)(2,1)}, bf16[112,512]{1,0:T(8,128)(2,1)}) custom-call(bf16[112,1280]{1,0:T(8,128)(2,1)S(1)} %collective-permute-done.8.refs_0_, bf16[112,1280]{1,0:T(8,128)(2,1)S(1)} %collective-permute-done.5.refs_1_), custom_call_target="tpu_custom_call" | custom-call | flops 1024 | bytes 1024 | tf_op jit(solution)/shard_map/merge/pallas_call | solution.py:183
  41.9 0.0 collective-permute-done.2.packed_ref
  41.9 0.0 collective-permute-done.10.there_ref
  41.9 0.4 collective-permute-done.9.here_ref
  42.3 0.8 %unpack.1 = (bf16[112,2048]{1,0:T(8,128)(2,1)}, bf16[112,512]{1,0:T(8,128)(2,1)}, f32[2,128]{1,0:T(2,128)}) custom-call(bf16[112,2560]{1,0:T(8,128)(2,1)S(1)} %collective-permute-done.2.packed_ref, f32[2,128]{1,0:T(2,128)S(1)} %collective-permute-done.9.here_ref, f32[2,128]{1,0:T(2,128)S(1)} %collective-permute-done.10.there_ref), custom_call_target="tpu_custom_call" | custom-call | flops 1024 | bytes 1024 | tf_op jit(solution)/shard_map/unpack/pallas_call | solution.py:162
  (6 shorter events, 0.1 us)
Async XLA Ops:
  0.6 1.9 %copy-start.2 = (bf16[1,112,2048]{2,1,0:T(8,128)(2,1)S(1)}, bf16[1,112,2048]{2,1,0:T(8,128)(2,1)}, u32[]{:S(2)}) copy-start(bf16[1,112,2048]{2,1,0:T(8,128)(2,1)} %param.8) | copy-start | bytes 1376260
  0.6 1.9 %copy-start.3 = (bf16[1,112,512]{2,1,0:T(8,128)(2,1)S(1)}, bf16[1,112,512]{2,1,0:T(8,128)(2,1)}, u32[]{:S(2)}) copy-start(bf16[1,112,512]{2,1,0:T(8,128)(2,1)} %param.9) | copy-start | bytes 344068
  1.8 19.2 %collective-permute-start.3 = (bf16[112,2560]{1,0:T(8,128)(2,1)S(1)}, bf16[112,2560]{1,0:T(8,128)(2,1)S(1)}, u32[]{:S(2)}, u32[]{:S(2)}) collective-permute-start(bf16[112,2560]{1,0:T(8,128)(2,1)S(1)} %pad_maximum_fusion.1), channel_id=1, source_target_pairs={{0,0},{8,24},{16,16},{24,8},{1,1},{9,25},{17,17},{25,9},{2,2},{10,... | collective-permute-start | bytes 1720328 | tf_op jit(solution)/shard_map/ppermute | solution.py:205
  2.6 5.8 %copy-start.5 = (s32[1,2]{1,0:T(1,128)S(1)}, s32[1,2]{1,0:T(1,128)}, u32[]{:S(2)}) copy-start(s32[1,2]{1,0:T(1,128)} %param.14) | copy-start | bytes 28
  2.6 5.9 %copy-start.4 = (f32[1,2,128]{2,1,0:T(2,128)S(1)}, f32[1,2,128]{2,1,0:T(2,128)}, u32[]{:S(2)}) copy-start(f32[1,2,128]{2,1,0:T(2,128)} %param.13) | copy-start | bytes 3076
  2.6 18.5 %copy-start = (bf16[1,112,2048]{2,1,0:T(8,128)(2,1)S(1)}, bf16[1,112,2048]{2,1,0:T(8,128)(2,1)}, u32[]{:S(2)}) copy-start(bf16[1,112,2048]{2,1,0:T(8,128)(2,1)} %param.12) | copy-start | bytes 1376260
  2.6 18.5 %copy-start.1 = (s32[1,4,112]{2,1,0:T(4,128)S(1)}, s32[1,4,112]{2,1,0:T(4,128)}, u32[]{:S(2)}) copy-start(s32[1,4,112]{2,1,0:T(4,128)} %param.15) | copy-start | bytes 5380
  2.6 28.2 %collective-permute-start = (bf16[112,2560]{1,0:T(8,128)(2,1)S(1)}, bf16[112,2560]{1,0:T(8,128)(2,1)S(1)}, u32[]{:S(2)}, u32[]{:S(2)}) collective-permute-start(bf16[112,2560]{1,0:T(8,128)(2,1)S(1)} %pad_maximum_fusion), channel_id=1, source_target_pairs={{0,8},{8,16},{16,24},{24,0},{1,9},{9,17},{17,25},{25,1},{2,10},{10... | collective-permute-start | bytes 1720328 | tf_op jit(solution)/shard_map/ppermute | solution.py:205
  8.5 12.5 %collective-permute-start.1 = (f32[4,128]{1,0:T(4,128)S(1)}, f32[4,128]{1,0:T(4,128)S(1)}, u32[]{:S(2)}, u32[]{:S(2)}) collective-permute-start(f32[4,128]{1,0:T(4,128)S(1)} %pad_maximum_fusion.2), channel_id=1, source_target_pairs={{0,8},{8,16},{16,24},{24,0},{1,9},{9,17},{17,25},{25,1},{2,10},{10... | collective-permute-start | bytes 6152 | tf_op jit(solution)/shard_map/ppermute | solution.py:205
  21.9 10.9 %collective-permute-start.5 = (bf16[112,1280]{1,0:T(8,128)(2,1)S(1)}, bf16[112,1280]{1,0:T(8,128)(2,1)S(1)}, u32[]{:S(2)}, u32[]{:S(2)}) collective-permute-start(bf16[112,1280]{1,0:T(8,128)(2,1)S(1)} %get-tuple-element.21), channel_id=1, source_target_pairs={{0,24},{8,0},{16,8},{24,16},{1,25},{9,1},{17,9},{25,17},{2,26},{10... | collective-permute-start | bytes 860168 | tf_op jit(solution)/shard_map/ppermute | solution.py:205
  24.6 9.0 %collective-permute-start.4 = (bf16[112,1280]{1,0:T(8,128)(2,1)S(1)}, bf16[112,1280]{1,0:T(8,128)(2,1)S(1)}, u32[]{:S(2)}, u32[]{:S(2)}) collective-permute-start(bf16[112,1280]{1,0:T(8,128)(2,1)S(1)} %get-tuple-element.20), channel_id=1, source_target_pairs={{0,16},{16,0},{1,17},{17,1},{2,18},{18,2},{3,19},{19,3},{4,20},{20... | collective-permute-start | bytes 860168 | tf_op jit(solution)/shard_map/ppermute | solution.py:205
  28.0 1.2 %collective-permute-start.6 = (f32[2,128]{1,0:T(2,128)S(1)}, f32[2,128]{1,0:T(2,128)S(1)}, u32[]{:S(2)}, u32[]{:S(2)}) collective-permute-start(f32[2,128]{1,0:T(2,128)S(1)} %add.9), channel_id=1, source_target_pairs={{0,1},{1,0},{2,3},{3,2},{4,5},{5,4},{6,7},{7,6},{8,9},{9,8},{10,11... | collective-permute-start | bytes 3080 | tf_op jit(solution)/shard_map/ppermute | solution.py:230
  29.3 3.6 %collective-permute-start.7 = (f32[2,128]{1,0:T(2,128)S(1)}, f32[2,128]{1,0:T(2,128)S(1)}, u32[]{:S(2)}, u32[]{:S(2)}) collective-permute-start(f32[2,128]{1,0:T(2,128)S(1)} %add.10), channel_id=1, source_target_pairs={{0,2},{1,3},{2,0},{3,1},{4,6},{5,7},{6,4},{7,5},{8,10},{9,11},{10,... | collective-permute-start | bytes 3080 | tf_op jit(solution)/shard_map/ppermute | solution.py:230
  30.8 11.1 %collective-permute-start.2 = (bf16[112,2560]{1,0:T(8,128)(2,1)S(1)}, bf16[112,2560]{1,0:T(8,128)(2,1)S(1)}, u32[]{:S(2)}, u32[]{:S(2)}) collective-permute-start(bf16[112,2560]{1,0:T(8,128)(2,1)S(1)} %collective-permute-done.packed_ref), channel_id=1, source_target_pairs={{0,0},{8,24},{16,16},{24,8},{1,1},{9,25},{17,17},{25,9},{2,2},{10,... | collective-permute-start | bytes 1720328 | tf_op jit(solution)/shard_map/ppermute | solution.py:205
  33.6 7.4 %collective-permute-start.8 = (bf16[112,1280]{1,0:T(8,128)(2,1)S(1)}, bf16[112,1280]{1,0:T(8,128)(2,1)S(1)}, u32[]{:S(2)}, u32[]{:S(2)}) collective-permute-start(bf16[112,1280]{1,0:T(8,128)(2,1)S(1)} %broadcast_select_fusion), channel_id=1, source_target_pairs={{16,24},{0,8},{8,0},{24,16},{17,25},{1,9},{9,1},{25,17},{18,26},{2... | collective-permute-start | bytes 860168 | tf_op jit(solution)/shard_map/ppermute | solution.py:205
  33.7 8.2 %collective-permute-start.10 = (f32[2,128]{1,0:T(2,128)S(1)}, f32[2,128]{1,0:T(2,128)S(1)}, u32[]{:S(2)}, u32[]{:S(2)}) collective-permute-start(f32[2,128]{1,0:T(2,128)S(1)} %add.11), channel_id=1, source_target_pairs={{0,28},{1,29},{2,30},{3,31},{4,24},{5,25},{6,26},{7,27},{8,4},{9,5... | collective-permute-start | bytes 3080 | tf_op jit(solution)/shard_map/ppermute | solution.py:238
  38.7 3.6 %collective-permute-start.9 = (f32[2,128]{1,0:T(2,128)S(1)}, f32[2,128]{1,0:T(2,128)S(1)}, u32[]{:S(2)}, u32[]{:S(2)}) collective-permute-start(f32[2,128]{1,0:T(2,128)S(1)} %add.11), channel_id=1, source_target_pairs={{0,24},{1,25},{2,26},{3,27},{4,28},{5,29},{6,30},{7,31},{8,0},{9,1... | collective-permute-start | bytes 3080 | tf_op jit(solution)/shard_map/ppermute | solution.py:238

commit v8 on v6

--- a/solution.py
+++ b/solution.py
@@ -56,13 +56,14 @@
     return weights * (1.0 / jnp.sum(weights, axis=0, keepdims=True))
 
 
-def forward_kernel(packed_ref, side_ref, segment_ref, out_ref):
+def forward_kernel(packed_ref, side_ref, segment_ref, out_ref, held_ref, sems):
     side = side_ref[...]
     tokens = packed_ref.shape[0]
     heads = out_ref.shape[1] // HEAD_SIZE
     kv_heads = (packed_ref.shape[1] // HEAD_SIZE - heads) // 2
     per_kv = heads // kv_heads
     allowed = allowed_pairs(segment_ref, side[2:3], per_kv)
+    copies = []
     for g in range(kv_heads):
         key_hat, _ = normalized(head(packed_ref, heads + g))
         key = (key_hat * side[1:2]).astype(jnp.bfloat16)
@@ -73,7 +74,14 @@
         out = dot(probs, value, TN).astype(jnp.bfloat16)
         for i in range(per_kv):
             h = g * per_kv + i
-            out_ref[:, h * HEAD_SIZE : (h + 1) * HEAD_SIZE] = out[i * tokens : (i + 1) * tokens]
+            held_ref[:, h * HEAD_SIZE : (h + 1) * HEAD_SIZE] = out[i * tokens : (i + 1) * tokens]
+        columns = pl.ds(g * per_kv * HEAD_SIZE, per_kv * HEAD_SIZE)
+        copies.append(
+            pltpu.make_async_copy(held_ref.at[:, columns], out_ref.at[:, columns], sems.at[g])
+        )
+        copies[-1].start()
+    for copy in copies:
+        copy.wait()
 
 
 def norm_back(hat, factor, scaled_gain, d_normed):
@@ -137,11 +145,17 @@
 
 
 def forward(fresh, q_width, side, segments):
+    tokens, width = fresh.shape
+    kv_heads = (width - q_width) // HEAD_SIZE // 2
     return pl.pallas_call(
         forward_kernel,
-        out_shape=jax.ShapeDtypeStruct((fresh.shape[0], q_width), fresh.dtype),
+        out_shape=jax.ShapeDtypeStruct((tokens, q_width), fresh.dtype),
         in_specs=[VMEM] * 3,
-        out_specs=VMEM,
+        out_specs=pl.BlockSpec(memory_space=pl.ANY),
+        scratch_shapes=[
+            pltpu.VMEM((tokens, q_width), fresh.dtype),
+            pltpu.SemaphoreType.DMA((kv_heads,)),
+        ],
         cost_estimate=cost(1024),
         compiler_params=pltpu.CompilerParams(vmem_limit_bytes=VMEM_LIMIT),
         name="forward",

time: 43.3 us -> 43.3 us (level)
  transfers between devices with their start and end apart: 11 -> 11, of which waited for: 6 -> 6; matrix products, arithmetic and copies ran while one was open for 1% -> 1% of each run, Pallas kernels for 10% -> 9%
where the time goes in v8:
time: 43.3 us; the launch traced here: 42.8 us
  starting transfers between devices  19.6 us (45%)
  waiting for transfers between devices  16.1 us (37%)
  Pallas kernels  4.9 us (11%)
  other arithmetic  1.32 us (3%)
  between operations  0.78 us (2%)
    ppermute x7, waiting for transfers between devices, hop(): return lax.ppermute(value, 'section', pairs)  13.3 us
    ppermute x7, starting transfers between devices, hop(): return lax.ppermute(value, 'section', pairs)  12.9 us
    ppermute x2, starting transfers between devices, local(): lax.ppermute(gain, ('section', 'dp'), [(i * replicas + j, (i - 1) % secti...  5.06 us
    ppermute x2, waiting for transfers between devices, local(): lax.ppermute(gain, 'dp', [(i, i ^ step) for i in range(replicas)])  2.42 us
    pallas_call x1, Pallas kernels, forward(): pl.pallas_call(forward_kernel, out_shape=jax.ShapeDtypeStruct((tokens, q_...  1.78 us
    ppermute x2, starting transfers between devices, local(): lax.ppermute(gain, 'dp', [(i, i ^ step) for i in range(replicas)])  1.65 us
    pallas_call x1, Pallas kernels, backward(): pl.pallas_call(backward_kernel, out_shape=[jax.ShapeDtypeStruct((tokens,...  1.44 us
    concatenate x1, other arithmetic, local(): jnp.concatenate([held_q[0], retained_key_value[0]], axis=1)  1.17 us
  transfers between devices with their start and end apart: 11, of which 6 were waited for; matrix products, arithmetic and copies ran while one was open for 1% of the time, Pallas kernels for 9%

profile of v8, /device:TPU:0, one launch (start us, length us, event | category | flops | bytes accessed | tf_op | source)
XLA Modules:
  0.0 42.8 jit_solution(6969467039685790886)
XLA Ops:
  0.6 0.0 copy-start.2
  0.6 0.0 copy-start.3
  0.7 1.2 %pad_maximum_fusion.1 = bf16[112,2560]{1,0:T(8,128)(2,1)S(1)} fusion(bf16[112,512]{1,0:T(8,128)(2,1)} %bitcast.21, bf16[112,2048]{1,0:T(8,128)(2,1)} %bitcast.18), kind=kLoop, calls=%fused_computation.1 | loop fusion | flops 1146880 | bytes 1146880 | tf_op jit(solution)/shard_map/concatenate | solution.py:232
  1.8 0.7 %collective-permute-start.3 = (bf16[112,2560]{1,0:T(8,128)(2,1)S(1)}, bf16[112,2560]{1,0:T(8,128)(2,1)S(1)}, u32[]{:S(2)}, u32[]{:S(2)}) collective-permute-start(bf16[112,2560]{1,0:T(8,128)(2,1)S(1)} %pad_maximum_fusion.1), channel_id=1, source_target_pairs={{0,0},{8,24},{16,16},{24,8},{1,1},{9,25},{17,17},{25,9},{2,2},{10,... | collective-permute-start | bytes 1720328 | tf_op jit(solution)/shard_map/ppermute | solution.py:228
  2.5 0.0 copy-done.2
  2.5 0.0 copy-done.3
  2.6 0.0 copy-start.5
  2.6 0.0 copy-start.4
  2.6 0.0 copy-start
  2.6 0.0 copy-start.1
  2.6 5.7 %collective-permute-start = (bf16[112,2560]{1,0:T(8,128)(2,1)S(1)}, bf16[112,2560]{1,0:T(8,128)(2,1)S(1)}, u32[]{:S(2)}, u32[]{:S(2)}) collective-permute-start(bf16[112,2560]{1,0:T(8,128)(2,1)S(1)} %pad_maximum_fusion), channel_id=1, source_target_pairs={{0,8},{8,16},{16,24},{24,0},{1,9},{9,17},{17,25},{25,1},{2,10},{10... | collective-permute-start | bytes 1720328 | tf_op jit(solution)/shard_map/ppermute | solution.py:228
  8.4 0.0 copy-done.5
  8.4 0.1 pad.3.clone
  8.5 0.0 copy-done.4
  8.5 0.1 pad_maximum_fusion.2
  8.5 0.5 %collective-permute-start.1 = (f32[4,128]{1,0:T(4,128)S(1)}, f32[4,128]{1,0:T(4,128)S(1)}, u32[]{:S(2)}, u32[]{:S(2)}) collective-permute-start(f32[4,128]{1,0:T(4,128)S(1)} %pad_maximum_fusion.2), channel_id=1, source_target_pairs={{0,8},{8,16},{16,24},{24,0},{1,9},{9,17},{17,25},{25,1},{2,10},{10... | collective-permute-start | bytes 6152 | tf_op jit(solution)/shard_map/ppermute | solution.py:228
  9.0 12.0 %collective-permute-done.1.side_ref = f32[4,128]{1,0:T(4,128)S(1)} collective-permute-done((f32[4,128]{1,0:T(4,128)S(1)}, f32[4,128]{1,0:T(4,128)S(1)}, u32[]{:S(2)}, u32[]{:S(2)}) %collective-permute-start.1) | collective-permute-done | bytes 2080 | tf_op jit(solution)/shard_map/ppermute | solution.py:228
  21.1 0.0 collective-permute-done.3.packed_ref
  21.1 0.0 copy-done
  21.1 0.0 copy-done.1
  21.1 1.4 %backward.1 = (bf16[112,1280]{1,0:T(8,128)(2,1)S(1)}, bf16[112,1280]{1,0:T(8,128)(2,1)S(1)}, f32[2,128]{1,0:T(2,128)S(1)}) custom-call(bf16[112,2560]{1,0:T(8,128)(2,1)S(1)} %collective-permute-done.3.packed_ref, bf16[112,2048]{1,0:T(8,128)(2,1)S(1)} %bitcast.15, f32[4,128]{1,0:T(4,128)S(1)} %collective-permute-done.1.side_ref, s32[4,112]{1,0:T(4,128)S(1)} %bitcast.16), custom_call_target="tpu_custom_call" | custom-call | flops 1024 | bytes 1024 | tf_op jit(solution)/shard_map/backward/pallas_call | solution.py:168
  22.5 1.8 %collective-permute-start.5 = (bf16[112,1280]{1,0:T(8,128)(2,1)S(1)}, bf16[112,1280]{1,0:T(8,128)(2,1)S(1)}, u32[]{:S(2)}, u32[]{:S(2)}) collective-permute-start(bf16[112,1280]{1,0:T(8,128)(2,1)S(1)} %get-tuple-element.20), channel_id=1, source_target_pairs={{0,24},{8,0},{16,8},{24,16},{1,25},{9,1},{17,9},{25,17},{2,26},{10... | collective-permute-start | bytes 860168 | tf_op jit(solution)/shard_map/ppermute | solution.py:228
  24.3 3.4 %collective-permute-start.4 = (bf16[112,1280]{1,0:T(8,128)(2,1)S(1)}, bf16[112,1280]{1,0:T(8,128)(2,1)S(1)}, u32[]{:S(2)}, u32[]{:S(2)}) collective-permute-start(bf16[112,1280]{1,0:T(8,128)(2,1)S(1)} %get-tuple-element.19), channel_id=1, source_target_pairs={{0,16},{16,0},{1,17},{17,1},{2,18},{18,2},{3,19},{19,3},{4,20},{20... | collective-permute-start | bytes 860168 | tf_op jit(solution)/shard_map/ppermute | solution.py:228
  27.7 0.1 collective-permute-start.6
  27.8 1.1 %collective-permute-done.6 = f32[2,128]{1,0:T(2,128)S(1)} collective-permute-done((f32[2,128]{1,0:T(2,128)S(1)}, f32[2,128]{1,0:T(2,128)S(1)}, u32[]{:S(2)}, u32[]{:S(2)}) %collective-permute-start.6) | collective-permute-done | bytes 1056 | tf_op jit(solution)/shard_map/ppermute | solution.py:246
  28.9 1.6 %collective-permute-start.7 = (f32[2,128]{1,0:T(2,128)S(1)}, f32[2,128]{1,0:T(2,128)S(1)}, u32[]{:S(2)}, u32[]{:S(2)}) collective-permute-start(f32[2,128]{1,0:T(2,128)S(1)} %add.6), channel_id=1, source_target_pairs={{0,2},{1,3},{2,0},{3,1},{4,6},{5,7},{6,4},{7,5},{8,10},{9,11},{10,... | collective-permute-start | bytes 3080 | tf_op jit(solution)/shard_map/ppermute | solution.py:246
  30.5 0.0 collective-permute-done.packed_ref
  30.5 0.7 %collective-permute-start.2 = (bf16[112,2560]{1,0:T(8,128)(2,1)S(1)}, bf16[112,2560]{1,0:T(8,128)(2,1)S(1)}, u32[]{:S(2)}, u32[]{:S(2)}) collective-permute-start(bf16[112,2560]{1,0:T(8,128)(2,1)S(1)} %collective-permute-done.packed_ref), channel_id=1, source_target_pairs={{0,0},{8,24},{16,16},{24,8},{1,1},{9,25},{17,17},{25,9},{2,2},{10,... | collective-permute-start | bytes 1720328 | tf_op jit(solution)/shard_map/ppermute | solution.py:228
  31.2 1.3 %collective-permute-done.7 = f32[2,128]{1,0:T(2,128)S(1)} collective-permute-done((f32[2,128]{1,0:T(2,128)S(1)}, f32[2,128]{1,0:T(2,128)S(1)}, u32[]{:S(2)}, u32[]{:S(2)}) %collective-permute-start.7) | collective-permute-done | bytes 1056 | tf_op jit(solution)/shard_map/ppermute | solution.py:246
  32.5 0.0 collective-permute-done.5.second_ref
  32.5 0.8 %collective-permute-done.4 = bf16[112,1280]{1,0:T(8,128)(2,1)S(1)} collective-permute-done((bf16[112,1280]{1,0:T(8,128)(2,1)S(1)}, bf16[112,1280]{1,0:T(8,128)(2,1)S(1)}, u32[]{:S(2)}, u32[]{:S(2)}) %collective-permute-start.4) | collective-permute-done | bytes 286752 | tf_op jit(solution)/shard_map/ppermute | solution.py:228
  33.3 0.1 collective-permute-start.8
  33.4 5.0 %collective-permute-start.10 = (f32[2,128]{1,0:T(2,128)S(1)}, f32[2,128]{1,0:T(2,128)S(1)}, u32[]{:S(2)}, u32[]{:S(2)}) collective-permute-start(f32[2,128]{1,0:T(2,128)S(1)} %add.7), channel_id=1, source_target_pairs={{0,28},{1,29},{2,30},{3,31},{4,24},{5,25},{6,26},{7,27},{8,4},{9,5... | collective-permute-start | bytes 3080 | tf_op jit(solution)/shard_map/ppermute | solution.py:254
  38.4 0.1 collective-permute-start.9
  38.5 1.8 %forward.1 = bf16[112,2048]{1,0:T(8,128)(2,1)} custom-call(bf16[112,2560]{1,0:T(8,128)(2,1)S(1)} %collective-permute-done.packed_ref, f32[4,128]{1,0:T(4,128)S(1)} %collective-permute-done.1.side_ref, s32[4,112]{1,0:T(4,128)S(1)} %bitcast.17), custom_call_target="tpu_custom_call" | custom-call | flops 1024 | bytes 1024 | tf_op jit(solution)/shard_map/forward/pallas_call | solution.py:150
  40.3 0.5 %collective-permute-done.8.first_ref = bf16[112,1280]{1,0:T(8,128)(2,1)S(1)} collective-permute-done((bf16[112,1280]{1,0:T(8,128)(2,1)S(1)}, bf16[112,1280]{1,0:T(8,128)(2,1)S(1)}, u32[]{:S(2)}, u32[]{:S(2)}) %collective-permute-start.8) | collective-permute-done | bytes 286752 | tf_op jit(solution)/shard_map/ppermute | solution.py:228
  40.7 0.8 %merge.1 = (bf16[112,2048]{1,0:T(8,128)(2,1)}, bf16[112,512]{1,0:T(8,128)(2,1)}) custom-call(bf16[112,1280]{1,0:T(8,128)(2,1)S(1)} %collective-permute-done.8.first_ref, bf16[112,1280]{1,0:T(8,128)(2,1)S(1)} %collective-permute-done.5.second_ref), custom_call_target="tpu_custom_call" | custom-call | flops 1024 | bytes 1024 | tf_op jit(solution)/shard_map/merge/pallas_call | solution.py:206
  41.6 0.0 collective-permute-done.2.packed_ref
  41.6 0.0 collective-permute-done.10.there_ref
  41.6 0.4 collective-permute-done.9.here_ref
  42.0 0.8 %unpack.1 = (bf16[112,2048]{1,0:T(8,128)(2,1)}, bf16[112,512]{1,0:T(8,128)(2,1)}, f32[2,128]{1,0:T(2,128)}) custom-call(bf16[112,2560]{1,0:T(8,128)(2,1)S(1)} %collective-permute-done.2.packed_ref, f32[2,128]{1,0:T(2,128)S(1)} %collective-permute-done.9.here_ref, f32[2,128]{1,0:T(2,128)S(1)} %collective-permute-done.10.there_ref), custom_call_target="tpu_custom_call" | custom-call | flops 1024 | bytes 1024 | tf_op jit(solution)/shard_map/unpack/pallas_call | solution.py:189
  (5 shorter events, 0.1 us)
Async XLA Ops:
  0.6 1.9 %copy-start.2 = (bf16[1,112,2048]{2,1,0:T(8,128)(2,1)S(1)}, bf16[1,112,2048]{2,1,0:T(8,128)(2,1)}, u32[]{:S(2)}) copy-start(bf16[1,112,2048]{2,1,0:T(8,128)(2,1)} %param.8) | copy-start | bytes 1376260
  0.6 1.9 %copy-start.3 = (bf16[1,112,512]{2,1,0:T(8,128)(2,1)S(1)}, bf16[1,112,512]{2,1,0:T(8,128)(2,1)}, u32[]{:S(2)}) copy-start(bf16[1,112,512]{2,1,0:T(8,128)(2,1)} %param.9) | copy-start | bytes 344068
  1.8 19.2 %collective-permute-start.3 = (bf16[112,2560]{1,0:T(8,128)(2,1)S(1)}, bf16[112,2560]{1,0:T(8,128)(2,1)S(1)}, u32[]{:S(2)}, u32[]{:S(2)}) collective-permute-start(bf16[112,2560]{1,0:T(8,128)(2,1)S(1)} %pad_maximum_fusion.1), channel_id=1, source_target_pairs={{0,0},{8,24},{16,16},{24,8},{1,1},{9,25},{17,17},{25,9},{2,2},{10,... | collective-permute-start | bytes 1720328 | tf_op jit(solution)/shard_map/ppermute | solution.py:228
  2.6 5.8 %copy-start.5 = (s32[1,2]{1,0:T(1,128)S(1)}, s32[1,2]{1,0:T(1,128)}, u32[]{:S(2)}) copy-start(s32[1,2]{1,0:T(1,128)} %param.14) | copy-start | bytes 28
  2.6 5.9 %copy-start.4 = (f32[1,2,128]{2,1,0:T(2,128)S(1)}, f32[1,2,128]{2,1,0:T(2,128)}, u32[]{:S(2)}) copy-start(f32[1,2,128]{2,1,0:T(2,128)} %param.13) | copy-start | bytes 3076
  2.6 18.5 %copy-start = (bf16[1,112,2048]{2,1,0:T(8,128)(2,1)S(1)}, bf16[1,112,2048]{2,1,0:T(8,128)(2,1)}, u32[]{:S(2)}) copy-start(bf16[1,112,2048]{2,1,0:T(8,128)(2,1)} %param.12) | copy-start | bytes 1376260
  2.6 18.5 %copy-start.1 = (s32[1,4,112]{2,1,0:T(4,128)S(1)}, s32[1,4,112]{2,1,0:T(4,128)}, u32[]{:S(2)}) copy-start(s32[1,4,112]{2,1,0:T(4,128)} %param.15) | copy-start | bytes 5380
  2.6 27.9 %collective-permute-start = (bf16[112,2560]{1,0:T(8,128)(2,1)S(1)}, bf16[112,2560]{1,0:T(8,128)(2,1)S(1)}, u32[]{:S(2)}, u32[]{:S(2)}) collective-permute-start(bf16[112,2560]{1,0:T(8,128)(2,1)S(1)} %pad_maximum_fusion), channel_id=1, source_target_pairs={{0,8},{8,16},{16,24},{24,0},{1,9},{9,17},{17,25},{25,1},{2,10},{10... | collective-permute-start | bytes 1720328 | tf_op jit(solution)/shard_map/ppermute | solution.py:228
  8.5 12.5 %collective-permute-start.1 = (f32[4,128]{1,0:T(4,128)S(1)}, f32[4,128]{1,0:T(4,128)S(1)}, u32[]{:S(2)}, u32[]{:S(2)}) collective-permute-start(f32[4,128]{1,0:T(4,128)S(1)} %pad_maximum_fusion.2), channel_id=1, source_target_pairs={{0,8},{8,16},{16,24},{24,0},{1,9},{9,17},{17,25},{25,1},{2,10},{10... | collective-permute-start | bytes 6152 | tf_op jit(solution)/shard_map/ppermute | solution.py:228
  22.5 10.0 %collective-permute-start.5 = (bf16[112,1280]{1,0:T(8,128)(2,1)S(1)}, bf16[112,1280]{1,0:T(8,128)(2,1)S(1)}, u32[]{:S(2)}, u32[]{:S(2)}) collective-permute-start(bf16[112,1280]{1,0:T(8,128)(2,1)S(1)} %get-tuple-element.20), channel_id=1, source_target_pairs={{0,24},{8,0},{16,8},{24,16},{1,25},{9,1},{17,9},{25,17},{2,26},{10... | collective-permute-start | bytes 860168 | tf_op jit(solution)/shard_map/ppermute | solution.py:228
  24.3 9.0 %collective-permute-start.4 = (bf16[112,1280]{1,0:T(8,128)(2,1)S(1)}, bf16[112,1280]{1,0:T(8,128)(2,1)S(1)}, u32[]{:S(2)}, u32[]{:S(2)}) collective-permute-start(bf16[112,1280]{1,0:T(8,128)(2,1)S(1)} %get-tuple-element.19), channel_id=1, source_target_pairs={{0,16},{16,0},{1,17},{17,1},{2,18},{18,2},{3,19},{19,3},{4,20},{20... | collective-permute-start | bytes 860168 | tf_op jit(solution)/shard_map/ppermute | solution.py:228
  27.7 1.2 %collective-permute-start.6 = (f32[2,128]{1,0:T(2,128)S(1)}, f32[2,128]{1,0:T(2,128)S(1)}, u32[]{:S(2)}, u32[]{:S(2)}) collective-permute-start(f32[2,128]{1,0:T(2,128)S(1)} %get-tuple-element.21), channel_id=1, source_target_pairs={{0,1},{1,0},{2,3},{3,2},{4,5},{5,4},{6,7},{7,6},{8,9},{9,8},{10,11... | collective-permute-start | bytes 3080 | tf_op jit(solution)/shard_map/ppermute | solution.py:246
  28.9 3.6 %collective-permute-start.7 = (f32[2,128]{1,0:T(2,128)S(1)}, f32[2,128]{1,0:T(2,128)S(1)}, u32[]{:S(2)}, u32[]{:S(2)}) collective-permute-start(f32[2,128]{1,0:T(2,128)S(1)} %add.6), channel_id=1, source_target_pairs={{0,2},{1,3},{2,0},{3,1},{4,6},{5,7},{6,4},{7,5},{8,10},{9,11},{10,... | collective-permute-start | bytes 3080 | tf_op jit(solution)/shard_map/ppermute | solution.py:246
  30.5 11.1 %collective-permute-start.2 = (bf16[112,2560]{1,0:T(8,128)(2,1)S(1)}, bf16[112,2560]{1,0:T(8,128)(2,1)S(1)}, u32[]{:S(2)}, u32[]{:S(2)}) collective-permute-start(bf16[112,2560]{1,0:T(8,128)(2,1)S(1)} %collective-permute-done.packed_ref), channel_id=1, source_target_pairs={{0,0},{8,24},{16,16},{24,8},{1,1},{9,25},{17,17},{25,9},{2,2},{10,... | collective-permute-start | bytes 1720328 | tf_op jit(solution)/shard_map/ppermute | solution.py:228
  33.3 7.4 %collective-permute-start.8 = (bf16[112,1280]{1,0:T(8,128)(2,1)S(1)}, bf16[112,1280]{1,0:T(8,128)(2,1)S(1)}, u32[]{:S(2)}, u32[]{:S(2)}) collective-permute-start(bf16[112,1280]{1,0:T(8,128)(2,1)S(1)} %broadcast_select_fusion), channel_id=1, source_target_pairs={{16,24},{0,8},{8,0},{24,16},{17,25},{1,9},{9,1},{25,17},{18,26},{2... | collective-permute-start | bytes 860168 | tf_op jit(solution)/shard_map/ppermute | solution.py:228
  33.4 8.2 %collective-permute-start.10 = (f32[2,128]{1,0:T(2,128)S(1)}, f32[2,128]{1,0:T(2,128)S(1)}, u32[]{:S(2)}, u32[]{:S(2)}) collective-permute-start(f32[2,128]{1,0:T(2,128)S(1)} %add.7), channel_id=1, source_target_pairs={{0,28},{1,29},{2,30},{3,31},{4,24},{5,25},{6,26},{7,27},{8,4},{9,5... | collective-permute-start | bytes 3080 | tf_op jit(solution)/shard_map/ppermute | solution.py:254
  38.4 3.6 %collective-permute-start.9 = (f32[2,128]{1,0:T(2,128)S(1)}, f32[2,128]{1,0:T(2,128)S(1)}, u32[]{:S(2)}, u32[]{:S(2)}) collective-permute-start(f32[2,128]{1,0:T(2,128)S(1)} %add.7), channel_id=1, source_target_pairs={{0,24},{1,25},{2,26},{3,27},{4,28},{5,29},{6,30},{7,31},{8,0},{9,1... | collective-permute-start | bytes 3080 | tf_op jit(solution)/shard_map/ppermute | solution.py:254
